TPU v7x, 128 devices: a whole 4x4x4 slice. The times are simulated.
128 devices in a mesh: grid: 16 (over x, z_lo, core), tm: 8 (over z_hi, y).
Axes of the slice: x: 4, y: 4, z: 4 (z_hi: 2, z_lo: 2; z = z_hi * 2 + z_lo), core: 2. Of those that a mesh axis runs over, the one named last changes fastest.
Arguments:
- anomalies: float32 [32768, 8192], P('grid', 'tm'), may hold values from -2000 to 2000
- lag_list: int32 [8], replicated, may hold values from 0 to 168, as said below
- pair_plan: int32 [16, 3, 8, 2], P('grid'), may hold values from 0 to 15, as said below
Outputs:
- correlation: float32 [16, 3, 8, 8, 128, 128], P('grid', None, None, 'tm')
Inputs may be any that keep to these rules, and one draw needn't show every extreme that they name: `lag_list`: ascending and distinct; the first is 0 and the last 168. `pair_plan`: for each block and offset, the second sub-blocks of the 8 pairs are distinct.
All inputs are finite; a program needn't handle non-finite values.
Results may differ from a plain program's by a relative error of at most 0.0003.
Values may be sent and summed in bfloat16 or wider, within the bound.
No kernel may reach another device: no remote copies, remote signals or barrier semaphores. Data moves between devices by JAX's collectives and lax.ppermute only.
A program may use at most 192 MiB of HBM per device.

v0:
```python
import jax
import jax.numpy as jnp
from jax import lax
from jax.sharding import PartitionSpec as P

SUB = 128
LAGMAX = 168
STEPS = 3


def passed_along(block, axis, distance):
    devices = range(lax.axis_size(axis))
    route = [(i - distance, i) for i in devices if i - distance in devices]
    return lax.ppermute(block, axis, route)


def from_behind(value, axis, steps):
    count = lax.axis_size(axis)
    pairs = [(source, (source + steps) % count) for source in range(count)]
    return lax.ppermute(value, axis, pairs)


def correlate(scaled, partner, plan, lag_list, seg_hours):

    def one_couple(couple):
        first_rows = lax.dynamic_slice_in_dim(scaled, couple[0] * SUB, SUB, 0)
        second_rows = lax.dynamic_slice_in_dim(partner, couple[1] * SUB, SUB, 0)

        def take_offset(offset):
            return lax.dynamic_slice_in_dim(second_rows, offset, seg_hours, 1)

        shifted = jax.vmap(take_offset)(lag_list)
        return jnp.einsum("ct,lbt->lcb", first_rows, shifted, preferred_element_type=jnp.float32)

    return jax.vmap(one_couple)(plan)


def extend(block_rows):
    rim_cols = passed_along(block_rows[:, :LAGMAX], "tm", -1)
    return jnp.concatenate([block_rows, rim_cols], axis=1)


def per_device(anomalies, lag_list, pair_plan):
    seg_hours = anomalies.shape[1]
    all_hours = seg_hours * lax.axis_size("tm")
    totals, squares = lax.psum(
        (jnp.sum(anomalies, axis=1), jnp.sum(anomalies * anomalies, axis=1)), "tm"
    )
    center = totals / all_hours
    spread = squares / all_hours - center * center
    scaled = ((anomalies - center[:, None]) * lax.rsqrt(spread + 1e-05)[:, None]).astype(
        jnp.bfloat16
    )
    lag_share = lag_list.shape[0] // lax.axis_size("tm")
    my_lags = lax.dynamic_slice_in_dim(lag_list, lax.axis_index("tm") * lag_share, lag_share, 0)
    divisor = (all_hours - my_lags).astype(jnp.float32)
    carried = scaled
    results = []
    for cycle_step in range(STEPS):
        plan = pair_plan[0, cycle_step]
        carried = from_behind(carried, "grid", 1)
        partner = carried
        partner = extend(partner)
        partial_value = correlate(scaled, partner, plan, lag_list, seg_hours)
        summed = lax.psum_scatter(partial_value, "tm", scatter_dimension=1, tiled=True)
        results.append(summed / divisor[None, :, None, None])
    return jnp.stack(results)[None]


def solution(mesh):
    in_specs = (P("grid", "tm"), P(), P("grid", None, None, None))
    out_specs = P("grid", None, None, "tm", None, None)
    return jax.shard_map(
        per_device, mesh=mesh, in_specs=in_specs, out_specs=out_specs, check_vma=False
    )
```

profile of v0, /device:TPU:1, one launch (start us, length us, event | category | flops | bytes accessed | tf_op | source)
XLA Modules:
  0.0 597.8 jit_solution(4388074089402889349)
XLA Ops:
  6.5 4.4 fusion.23
  10.9 9.2 %copy.25 = f32[2048,1024]{0,1:T(8,128)} copy(f32[2048,1024]{1,0:T(8,128)} %param.3) | data formatting | bytes 16777216 | tf_op args[0]
  20.2 36.5 %all-reduce.9 = (f32[2048]{0:T(1024)S(1)}, f32[2048]{0:T(1024)S(1)}) all-reduce(f32[2048]{0:T(1024)S(1)} %get-tuple-element.126, f32[2048]{0:T(1024)S(1)} %get-tuple-element.125), channel_id=1, replica_groups=mesh['grid'=16,'tm'=8] {'tm'}, use_global_device_ids=true, to_apply=%region_3.0 | all-reduce | flops 4096 | bytes 32768 | tf_op jit(solution)/shard_map/psum | solution.py:46
  56.7 6.6 %multiply_convert_fusion = bf16[2048,1024]{0,1:T(8,128)(2,1)} fusion(f32[2048,1024]{0,1:T(8,128)} %copy.25, f32[2048]{0:T(1024)S(1)} %get-tuple-element.204, f32[2048]{0:T(1024)S(1)} %get-tuple-element.203), kind=kLoop, calls=%fused_computation.27 | loop fusion | flops 6291456 | bytes 12599296 | tf_op jit(solution)/shard_map/convert_element_type | solution.py:51
  63.2 8.5 %collective-permute-start = (bf16[2048,1024]{0,1:T(8,128)(2,1)}, bf16[2048,1024]{0,1:T(8,128)(2,1)}, u32[]{:S(2)}, u32[]{:S(2)}) collective-permute-start(bf16[2048,1024]{0,1:T(8,128)(2,1)} %multiply_convert_fusion), channel_id=1, source_target_pairs={{0,8},{8,16},{16,24},{24,32},{32,40},{40,48},{48,56},{56,64},{64,7... | collective-permute-start | bytes 12582920 | tf_op jit(solution)/shard_map/ppermute | solution.py:20
  71.7 6.4 %copy.27 = bf16[2048,1024]{1,0:T(8,128)(2,1)} copy(bf16[2048,1024]{0,1:T(8,128)(2,1)} %multiply_convert_fusion) | data formatting | bytes 8388608
  78.5 18.2 %while.17 = (s32[]{:T(128)}, bf16[2048,1024]{1,0:T(8,128)(2,1)}, s32[8,2]{0,1:T(2,128)S(1)}, bf16[8,128,1024]{2,1,0:T(8,128)(2,1)S(1)}, s32[]{:T(128)}) while((s32[]{:T(128)}, bf16[2048,1024]{1,0:T(8,128)(2,1)}, s32[8,2]{0,1:T(2,128)S(1)}, bf16[8,128,1024]{2,1,0:T(8,128)(2,1)S(1)}, s32[]{:T(128)}) %tuple.131), condition=%wide.while_cond.8, body=%wide.while_body.8.sunk | while | flops 2 | bytes 524393 | solution.py:26
  98.5 23.8 %while.14 = (s32[]{:T(128)}, bf16[2048,1024]{1,0:T(8,128)(2,1)}, s32[8,2]{0,1:T(2,128)S(1)}, bf16[8,128,1024]{2,1,0:T(8,128)(2,1)}, s32[]{:T(128)}) while((s32[]{:T(128)}, bf16[2048,1024]{1,0:T(8,128)(2,1)}, s32[8,2]{0,1:T(2,128)S(1)}, bf16[8,128,1024]{2,1,0:T(8,128)(2,1)}, s32[]{:T(128)}) %tuple.157), condition=%wide.while_cond.5, body=%wide.while_body.5.sunk | while | flops 2 | bytes 524901 | solution.py:26
  126.4 23.8 %while.11 = (s32[]{:T(128)}, bf16[2048,1024]{1,0:T(8,128)(2,1)}, s32[8,2]{0,1:T(2,128)S(1)}, bf16[8,128,1024]{2,1,0:T(8,128)(2,1)}, s32[]{:T(128)}) while((s32[]{:T(128)}, bf16[2048,1024]{1,0:T(8,128)(2,1)}, s32[8,2]{0,1:T(2,128)S(1)}, bf16[8,128,1024]{2,1,0:T(8,128)(2,1)}, s32[]{:T(128)}) %tuple.158), condition=%wide.while_cond.2, body=%wide.while_body.2.sunk | while | flops 2 | bytes 524901 | solution.py:26
  150.3 5.2 pad_maximum_fusion
  155.7 20.8 %while.9 = (s32[]{:T(128)}, bf16[2048,1192]{0,1:T(8,128)(2,1)}, s32[8,2]{0,1:T(2,128)S(1)}, bf16[8,128,1192]{2,1,0:T(8,128)(2,1)S(1)}, s32[]{:T(128)}) while((s32[]{:T(128)}, bf16[2048,1192]{0,1:T(8,128)(2,1)}, s32[8,2]{0,1:T(2,128)S(1)}, bf16[8,128,1192]{2,1,0:T(8,128)(2,1)S(1)}, s32[]{:T(128)}) %tuple.146), condition=%wide.while_cond, body=%wide.while_body.sunk | while | flops 2 | bytes 1876073 | solution.py:27
  176.5 6.0 %broadcast.68.clone.2 = bf16[8,8,128,1024]{3,2,1,0:T(8,128)(2,1)} broadcast(bf16[]{:T(256)} %constant.41), dimensions={} | broadcast | bytes 16777218
  182.5 28.8 %while.10 = (s32[]{:T(128)}, bf16[8,128,1192]{2,1,0:T(8,128)(2,1)S(1)}, s32[8,2]{0,1:T(2,128)S(1)}, bf16[8,8,128,1024]{3,2,1,0:T(8,128)(2,1)}, s32[]{:T(128)}) while((s32[]{:T(128)}, bf16[8,128,1192]{2,1,0:T(8,128)(2,1)S(1)}, s32[8,2]{0,1:T(2,128)S(1)}, bf16[8,8,128,1024]{3,2,1,0:T(8,128)(2,1)}, s32[]{:T(128)}) %tuple.149), condition=%wide.while_cond.1, body=%wide.while_body.1.sunk | while | flops 2 | bytes 4194917 | solution.py:30
  213.9 12.8 %fusion.6 = f32[8,8,128,128]{2,3,1,0:T(8,128)} fusion(bf16[8,128,1024]{2,1,0:T(8,128)(2,1)} %get-tuple-element.28, bf16[8,8,128,1024]{3,2,1,0:T(8,128)(2,1)} %get-tuple-element.20), kind=kOutput, calls=%fused_computation.32 | convolution fusion | flops 2147483648 | bytes 23068672 | tf_op jit(solution)/shard_map/vmap(ct,lbt->lcb)/dot_general | solution.py:33
  228.9 3.6 collective-permute-done.3
  232.5 5.1 pad_maximum_fusion.1
  237.8 21.9 %while.12 = (s32[]{:T(128)}, bf16[2048,1192]{0,1:T(8,128)(2,1)}, s32[8,2]{0,1:T(2,128)S(1)}, bf16[8,128,1192]{2,1,0:T(8,128)(2,1)S(1)}, s32[]{:T(128)}) while((s32[]{:T(128)}, bf16[2048,1192]{0,1:T(8,128)(2,1)}, s32[8,2]{0,1:T(2,128)S(1)}, bf16[8,128,1192]{2,1,0:T(8,128)(2,1)S(1)}, s32[]{:T(128)}) %tuple.137), condition=%wide.while_cond.3, body=%wide.while_body.3.sunk | while | flops 2 | bytes 1876073 | solution.py:27
  259.7 6.0 %broadcast.68.clone.1 = bf16[8,8,128,1024]{3,2,1,0:T(8,128)(2,1)} broadcast(bf16[]{:T(256)} %constant.41), dimensions={} | broadcast | bytes 16777218
  265.7 29.7 %while.13 = (s32[]{:T(128)}, bf16[8,128,1192]{2,1,0:T(8,128)(2,1)S(1)}, s32[8,2]{0,1:T(2,128)S(1)}, bf16[8,8,128,1024]{3,2,1,0:T(8,128)(2,1)}, s32[]{:T(128)}) while((s32[]{:T(128)}, bf16[8,128,1192]{2,1,0:T(8,128)(2,1)S(1)}, s32[8,2]{0,1:T(2,128)S(1)}, bf16[8,8,128,1024]{3,2,1,0:T(8,128)(2,1)}, s32[]{:T(128)}) %tuple.159), condition=%wide.while_cond.4, body=%wide.while_body.4.sunk | while | flops 2 | bytes 4194917 | solution.py:30
  273.7 3.1 bitcast_dynamic-update-slice_fusion.22
  277.5 3.1 bitcast_dynamic-update-slice_fusion.22
  281.2 3.1 bitcast_dynamic-update-slice_fusion.22
  288.6 3.0 bitcast_dynamic-update-slice_fusion.22
  297.8 12.9 %fusion.9 = f32[8,8,128,128]{2,3,1,0:T(8,128)} fusion(bf16[8,128,1024]{2,1,0:T(8,128)(2,1)} %get-tuple-element.52, bf16[8,8,128,1024]{3,2,1,0:T(8,128)(2,1)} %get-tuple-element.44), kind=kOutput, calls=%fused_computation.33 | convolution fusion | flops 2147483648 | bytes 23068672 | tf_op jit(solution)/shard_map/vmap(ct,lbt->lcb)/dot_general | solution.py:33
  311.0 4.0 collective-permute-done.5
  314.9 5.1 pad_maximum_fusion.2
  320.2 21.5 %while.15 = (s32[]{:T(128)}, bf16[2048,1192]{0,1:T(8,128)(2,1)}, s32[8,2]{0,1:T(2,128)S(1)}, bf16[8,128,1192]{2,1,0:T(8,128)(2,1)S(1)}, s32[]{:T(128)}) while((s32[]{:T(128)}, bf16[2048,1192]{0,1:T(8,128)(2,1)}, s32[8,2]{0,1:T(2,128)S(1)}, bf16[8,128,1192]{2,1,0:T(8,128)(2,1)S(1)}, s32[]{:T(128)}) %tuple.125), condition=%wide.while_cond.6, body=%wide.while_body.6.sunk | while | flops 2 | bytes 1876073 | solution.py:27
  341.7 6.0 %broadcast.68.clone = bf16[8,8,128,1024]{3,2,1,0:T(8,128)(2,1)} broadcast(bf16[]{:T(256)} %constant.41), dimensions={} | broadcast | bytes 16777218
  347.8 28.6 %while.16 = (s32[]{:T(128)}, bf16[8,128,1192]{2,1,0:T(8,128)(2,1)S(1)}, s32[8,2]{0,1:T(2,128)S(1)}, bf16[8,8,128,1024]{3,2,1,0:T(8,128)(2,1)}, s32[]{:T(128)}) while((s32[]{:T(128)}, bf16[8,128,1192]{2,1,0:T(8,128)(2,1)S(1)}, s32[8,2]{0,1:T(2,128)S(1)}, bf16[8,8,128,1024]{3,2,1,0:T(8,128)(2,1)}, s32[]{:T(128)}) %tuple.160), condition=%wide.while_cond.7, body=%wide.while_body.7.sunk | while | flops 2 | bytes 4194917 | solution.py:30
  376.3 13.0 %fusion.12 = f32[8,8,128,128]{2,3,0,1:T(8,128)} fusion(bf16[8,8,128,1024]{3,2,1,0:T(8,128)(2,1)} %get-tuple-element.68, bf16[8,128,1024]{2,1,0:T(8,128)(2,1)} %copy-done), kind=kOutput, calls=%fused_computation.34 | convolution fusion | flops 2147483648 | bytes 23068672 | tf_op jit(solution)/shard_map/vmap(ct,lbt->lcb)/dot_general | solution.py:33
  391.3 111.6 %all-reduce.13.cloned.1.call-done = (f32[8,8,128,128]{2,3,1,0:T(8,128)}, f32[8,8,128,128]{2,3,1,0:T(8,128)}) async-done(((f32[8,8,128,128]{2,3,1,0:T(8,128)}, f32[8,8,128,128]{2,3,1,0:T(8,128)}), (f32[8,8,128,128]{2,3,1,0:T(8,128)}, f32[8,8,128,128]{2,3,1,0:T(8,128)})) %all-reduce.13.cloned.1.call-update) | async-done | bytes 8388624
  506.4 81.7 %reduce-scatter.8.cloned.1.call-done = f32[8,1,128,128]{2,3,0,1:T(8,128)} async-done(((f32[8,8,128,128]{2,3,0,1:T(8,128)}), f32[8,1,128,128]{2,3,0,1:T(8,128)}) %reduce-scatter.8.cloned.1.call-update) | async-done | bytes 524304 | tf_op jit(solution)/shard_map/reduce_scatter | solution.py:65
  (309 shorter events, 225.5 us)
Async XLA Ops:
  6.5 496.4 %all-reduce.13.cloned.1.call-start = ((), (), s32[]{:S(2)}) async-start(), calls=%async_computation.2 | async-start | bytes 16777216
  56.7 15.1 %copy-start.1 = (s32[1,3,8,2]{2,3,1,0:T(2,128)S(1)}, s32[1,3,8,2]{2,3,1,0:T(2,128)}, u32[]{:S(2)}) copy-start(s32[1,3,8,2]{2,3,1,0:T(2,128)} %param.5) | copy-start | bytes 580
  63.2 59.0 %collective-permute-start = (bf16[2048,1024]{0,1:T(8,128)(2,1)}, bf16[2048,1024]{0,1:T(8,128)(2,1)}, u32[]{:S(2)}, u32[]{:S(2)}) collective-permute-start(bf16[2048,1024]{0,1:T(8,128)(2,1)} %multiply_convert_fusion), channel_id=1, source_target_pairs={{0,8},{8,16},{16,24},{24,32},{32,40},{40,48},{48,56},{56,64},{64,7... | collective-permute-start | bytes 12582920 | tf_op jit(solution)/shard_map/ppermute | solution.py:20
  96.7 29.7 %copy-start = (bf16[8,128,1024]{2,1,0:T(8,128)(2,1)}, bf16[8,128,1024]{2,1,0:T(8,128)(2,1)S(1)}, u32[]{:S(2)}) copy-start(bf16[8,128,1024]{2,1,0:T(8,128)(2,1)S(1)} %get-tuple-element.76) | copy-start | bytes 6291460
  98.5 51.7 %copy-start.2 = (s32[8]{0:T(128)S(1)}, s32[8]{0:T(128)}, u32[]{:S(2)}) copy-start(s32[8]{0:T(128)} %param.4) | copy-start | bytes 100
  123.4 26.9 %collective-permute-start.1 = (bf16[2048,168]{0,1:T(8,128)(2,1)S(1)}, bf16[2048,168]{0,1:T(8,128)(2,1)S(1)}, u32[]{:S(2)}, u32[]{:S(2)}) collective-permute-start(bf16[2048,168]{0,1:T(8,128)(2,1)S(1)} %slice.153), channel_id=1, source_target_pairs={{1,0},{2,1},{3,2},{4,3},{5,4},{6,5},{7,6},{9,8},{10,9},{11,10},{12... | collective-permute-start | bytes 2064392 | tf_op jit(solution)/shard_map/ppermute | solution.py:14
  150.2 61.1 %collective-permute-start.2 = (bf16[2048,1024]{0,1:T(8,128)(2,1)}, bf16[2048,1024]{0,1:T(8,128)(2,1)}, u32[]{:S(2)}, u32[]{:S(2)}) collective-permute-start(bf16[2048,1024]{0,1:T(8,128)(2,1)} %collective-permute-done), channel_id=1, source_target_pairs={{0,8},{8,16},{16,24},{24,32},{32,40},{40,48},{48,56},{56,64},{64,7... | collective-permute-start | bytes 12582920 | tf_op jit(solution)/shard_map/ppermute | solution.py:20
  212.4 20.0 %collective-permute-start.3 = (bf16[2048,168]{0,1:T(8,128)(2,1)S(1)}, bf16[2048,168]{0,1:T(8,128)(2,1)S(1)}, u32[]{:S(2)}, u32[]{:S(2)}) collective-permute-start(bf16[2048,168]{0,1:T(8,128)(2,1)S(1)} %slice.154), channel_id=1, source_target_pairs={{1,0},{2,1},{3,2},{4,3},{5,4},{6,5},{7,6},{9,8},{10,9},{11,10},{12... | collective-permute-start | bytes 2064392 | tf_op jit(solution)/shard_map/ppermute | solution.py:14
  226.7 68.6 %collective-permute-start.4 = (bf16[2048,1024]{0,1:T(8,128)(2,1)}, bf16[2048,1024]{0,1:T(8,128)(2,1)}, u32[]{:S(2)}, u32[]{:S(2)}) collective-permute-start(bf16[2048,1024]{0,1:T(8,128)(2,1)} %collective-permute-done.2), channel_id=1, source_target_pairs={{0,8},{8,16},{16,24},{24,32},{32,40},{40,48},{48,56},{56,64},{64,7... | collective-permute-start | bytes 12582920 | tf_op jit(solution)/shard_map/ppermute | solution.py:20
  296.5 18.4 %collective-permute-start.5 = (bf16[2048,168]{0,1:T(8,128)(2,1)S(1)}, bf16[2048,168]{0,1:T(8,128)(2,1)S(1)}, u32[]{:S(2)}, u32[]{:S(2)}) collective-permute-start(bf16[2048,168]{0,1:T(8,128)(2,1)S(1)} %slice.155), channel_id=1, source_target_pairs={{1,0},{2,1},{3,2},{4,3},{5,4},{6,5},{7,6},{9,8},{10,9},{11,10},{12... | collective-permute-start | bytes 2064392 | tf_op jit(solution)/shard_map/ppermute | solution.py:14
  310.7 277.4 %reduce-scatter.8.cloned.1.call-start = ((), (), s32[]{:S(2)}) async-start(), calls=%async_computation.1 | async-start | bytes 4718592 | tf_op jit(solution)/shard_map/reduce_scatter | solution.py:65
  389.3 1.3 copy-start.3
Sparse Core Ops, SparseCore 0:
  310.8 192.0 all-reduce.12
  506.8 81.2 reduce-scatter.7
where the time goes:
time: 602 us; the launch traced here: 598 us
  local copies, waits for them, and re-layouts  260 us (43%)
  waiting for transfers between devices  201 us (33%)
  matrix products  38.7 us (6%)
  blocking collectives  36.5 us (6%)
  other arithmetic  31.1 us (5%)
  starting transfers between devices  15 us (2%)
  between operations  14.3 us (2%)
    gather x264, local copies, waits for them, and re-layouts  216 us
    unnamed x3, waiting for transfers between devices  112 us
    reduce_scatter x1, waiting for transfers between devices, per_device(): lax.psum_scatter(partial_value, 'tm', scatter_dimension=1, tiled=True)  81.7 us
    dot_general x3, matrix products, one_couple(): jnp.einsum('ct,lbt->lcb', first_rows, shifted, preferred_element_type=jnp...  38.7 us
    unnamed x20, local copies, waits for them, and re-layouts  38.6 us
    psum x1, blocking collectives, per_device(): lax.psum((jnp.sum(anomalies, axis=1), jnp.sum(anomalies * anomalies, axis...  36.5 us
    concatenate x3, other arithmetic, extend(): return jnp.concatenate([block_rows, rim_cols], axis=1)  15.4 us
  transfers between devices with their start and end apart: 8, of which 4 were waited for; matrix products, arithmetic and copies ran while one was open for 51% of the time, Pallas kernels for 0%

commit v1 on v0

v1 whole, which is shorter than its diff:
```python
import jax
import jax.numpy as jnp
from jax import lax
from jax.experimental import pallas as pl
from jax.experimental.pallas import tpu as pltpu
from jax.sharding import PartitionSpec as P

SUB = 128
LANES = 128
HALO = 256
STEPS = 3
RING = 4
CHUNKS = (
    (1, 0, 4, 0),
    (1, 4, 4, 1),
    (3, 0, 4, 0),
    (3, 4, 4, 1),
    (2, 0, 4, 0),
    (2, 4, 4, 1),
)
IN_FLIGHT = 2


def sums_kernel(x_ref, out_ref):
    for sub in range(4):
        rows = slice(sub * SUB, (sub + 1) * SUB)
        total = jnp.zeros((SUB, LANES), jnp.float32)
        square = jnp.zeros((SUB, LANES), jnp.float32)
        for tile in range(x_ref.shape[1] // LANES):
            value = x_ref[rows, tile * LANES:(tile + 1) * LANES]
            total = total + value
            square = square + value * value
        out_ref[sub:sub + 1, :] = jnp.sum(total.T, axis=0, keepdims=True)
        out_ref[4 + sub:5 + sub, :] = jnp.sum(square.T, axis=0, keepdims=True)


def local_sums(anomalies):
    points, hours = anomalies.shape
    steps = points // (4 * SUB)
    return pl.pallas_call(
        sums_kernel,
        grid=(steps,),
        in_specs=[pl.BlockSpec((4 * SUB, hours), lambda i: (i, 0))],
        out_specs=pl.BlockSpec((8, LANES), lambda i: (i, 0)),
        out_shape=jax.ShapeDtypeStruct((8 * steps, LANES), jnp.float32),
        compiler_params=pltpu.CompilerParams(vmem_limit_bytes=24 << 20),
        cost_estimate=pl.CostEstimate(
            flops=3 * points * hours, bytes_accessed=4 * points * hours, transcendentals=0
        ),
        name="local_sums",
    )(anomalies)


def scale_rows(x, center_row, inverse_row, store):
    center = jnp.broadcast_to(center_row, (SUB, LANES)).T
    inverse = jnp.broadcast_to(inverse_row, (SUB, LANES)).T
    for tile in range(x.shape[1] // LANES):
        cols = slice(tile * LANES, (tile + 1) * LANES)
        store(cols, ((x[:, cols] - center) * inverse).astype(jnp.bfloat16))


def pick_kernel(index_ref, x_ref, norm_ref, dep_ref, out_ref):
    sub = index_ref[pl.program_id(0)]

    def store(cols, value):
        out_ref[0, :, cols] = value

    scale_rows(x_ref.at[0], norm_ref[0, pl.ds(sub, 1), :], norm_ref[1, pl.ds(sub, 1), :], store)


def scaled_pick(index, blocks, norm, dep):
    count, hours = index.shape[0], blocks.shape[2]
    return pl.pallas_call(
        pick_kernel,
        grid_spec=pltpu.PrefetchScalarGridSpec(
            num_scalar_prefetch=1,
            grid=(count,),
            in_specs=[
                pl.BlockSpec((1, SUB, hours), lambda i, index: (index[i], 0, 0)),
                pl.BlockSpec(norm.shape, lambda i, index: (0, 0, 0)),
                pl.BlockSpec(memory_space=pl.ANY),
            ],
            out_specs=pl.BlockSpec((1, SUB, hours), lambda i, index: (i, 0, 0)),
        ),
        out_shape=jax.ShapeDtypeStruct((count, SUB, hours), jnp.bfloat16),
        compiler_params=pltpu.CompilerParams(vmem_limit_bytes=24 << 20),
        cost_estimate=pl.CostEstimate(
            flops=2 * count * SUB * hours, bytes_accessed=6 * count * SUB * hours, transcendentals=0
        ),
        name="scaled_pick",
    )(index, blocks, norm, dep)


def all_kernel(x_ref, norm_ref, dep_ref, out_ref, tail_ref):
    sub = pl.program_id(0)
    hours = x_ref.shape[2]

    def store(cols, value):
        out_ref[0, :, cols] = value
        if cols.start >= hours - HALO:
            tail_ref[0, :, cols.start - hours + HALO:cols.stop - hours + HALO] = value

    scale_rows(x_ref.at[0], norm_ref[0, pl.ds(sub, 1), :], norm_ref[1, pl.ds(sub, 1), :], store)


def scaled_all(blocks, norm, dep):
    count, _, hours = blocks.shape
    return pl.pallas_call(
        all_kernel,
        grid=(count,),
        in_specs=[
            pl.BlockSpec((1, SUB, hours), lambda i: (i, 0, 0)),
            pl.BlockSpec(norm.shape, lambda i: (0, 0, 0)),
            pl.BlockSpec(memory_space=pl.ANY),
        ],
        out_specs=[
            pl.BlockSpec((1, SUB, hours), lambda i: (i, 0, 0)),
            pl.BlockSpec((1, SUB, HALO), lambda i: (i, 0, 0)),
        ],
        out_shape=[
            jax.ShapeDtypeStruct((count, SUB, hours), jnp.bfloat16),
            jax.ShapeDtypeStruct((count, SUB, HALO), jnp.bfloat16),
        ],
        compiler_params=pltpu.CompilerParams(vmem_limit_bytes=24 << 20),
        cost_estimate=pl.CostEstimate(
            flops=2 * count * SUB * hours, bytes_accessed=6 * count * SUB * hours, transcendentals=0
        ),
        name="scaled_all",
    )(blocks, norm, dep)


def piece_kernel(index_ref, lag_ref, a_ref, halo_ref, b_ref, keep_ref, send_ref, long_ref, shift_ref):
    hours = a_ref.shape[2]
    lags = lag_ref.shape[0]
    long_ref[:, :HALO] = halo_ref[0]
    long_ref[:, HALO:] = a_ref[0]
    lane = lax.broadcasted_iota(jnp.int32, (SUB, LANES), 1)
    for slot in range(lags):
        lag = lag_ref[slot]
        turn = lag & (LANES - 1)
        first = HALO - LANES - (lag - turn)

        def turned(tile):
            start = pl.multiple_of(first + tile * LANES, LANES)
            return pltpu.roll(long_ref[:, pl.ds(start, LANES)], turn, 1)

        before = turned(0)
        for tile in range(hours // LANES):
            here = turned(tile + 1)
            shift_ref[slot * SUB:(slot + 1) * SUB, tile * LANES:(tile + 1) * LANES] = jnp.where(
                lane < turn, before, here
            )
            before = here
    piece = lax.dot_general(
        shift_ref[...], b_ref[0], (((1,), (1,)), ((), ())), preferred_element_type=jnp.float32
    )
    half = lags // 2
    keep_ref[...] = piece[:half * SUB].reshape(half, 1, SUB, SUB)
    send_ref[...] = piece[half * SUB:].reshape(half, 1, SUB, SUB)


def pieces(index, lags, scaled, halo, partner):
    count, _, hours = partner.shape
    half = lags.shape[0] // 2
    out = jax.ShapeDtypeStruct((half, count, SUB, SUB), jnp.float32)
    return pl.pallas_call(
        piece_kernel,
        grid_spec=pltpu.PrefetchScalarGridSpec(
            num_scalar_prefetch=2,
            grid=(count,),
            in_specs=[
                pl.BlockSpec((1, SUB, hours), lambda i, index, lags: (index[i], 0, 0)),
                pl.BlockSpec((1, SUB, HALO), lambda i, index, lags: (index[i], 0, 0)),
                pl.BlockSpec((1, SUB, hours), lambda i, index, lags: (i, 0, 0)),
            ],
            out_specs=[pl.BlockSpec((half, 1, SUB, SUB), lambda i, index, lags: (0, i, 0, 0))] * 2,
            scratch_shapes=[
                pltpu.VMEM((SUB, HALO + hours), jnp.bfloat16),
                pltpu.VMEM((2 * half * SUB, hours), jnp.bfloat16),
            ],
        ),
        out_shape=[out, out],
        compiler_params=pltpu.CompilerParams(vmem_limit_bytes=24 << 20),
        cost_estimate=pl.CostEstimate(
            flops=8 * half * count * SUB * SUB * hours,
            bytes_accessed=count * (4 * SUB * hours + 8 * half * SUB * SUB),
            transcendentals=0,
        ),
        name="pieces",
    )(index, lags, scaled, halo, partner)


def per_device(anomalies, lag_list, pair_plan):
    points, seg_hours = anomalies.shape
    n_grid, n_tm = lax.axis_size("grid"), lax.axis_size("tm")
    all_hours = seg_hours * n_tm
    blocks = anomalies.reshape(points // SUB, SUB, seg_hours)

    def along_grid(value, step):
        return lax.ppermute(value, "grid", [(i, (i + step) % n_grid) for i in range(n_grid)])

    def along_tm(value, target):
        return lax.ppermute(value, "tm", [(i, target(i)) for i in range(n_tm)])

    def ring_near(i):
        return i - i % RING + ((i % RING) ^ 1)

    def ring_far(i):
        return i - i % RING + (RING - 1 - i % RING)

    def other_half(i):
        return (i + RING) % n_tm

    wanted = {k: along_grid(pair_plan[0, k - 1, :, 1], -k) for k in range(1, STEPS + 1)}

    sums = local_sums(anomalies)
    total = sums
    for step in range(1, n_tm):
        total = total + along_tm(sums, lambda i: (i + step) % n_tm)
    total = total.reshape(points // SUB // 4, 2, 4, LANES)
    center = (total[:, 0] / all_hours).reshape(points // SUB, LANES)
    spread = (total[:, 1] / all_hours).reshape(points // SUB, LANES) - center * center
    norm = jnp.stack([center, lax.rsqrt(spread + 1e-05)])

    me = lax.axis_index("tm")
    place, part = me % RING, me // RING
    near, far = place ^ 1, RING - 1 - place
    orders = (
        jnp.stack([place, far, near, RING - 1 - near]),
        jnp.stack([place, near, far, far ^ 1]),
    )
    parts = jnp.stack([part, 1 - part]) * RING
    lag_slots = [jnp.take(lag_list, (order[:, None] + parts[None, :]).reshape(-1)) for order in orders]
    divisor = (all_hours - lag_slots[0][0]).astype(jnp.float32)

    partners = []
    for number, (k, first, count, order) in enumerate(CHUNKS):
        dep = norm if number < IN_FLIGHT else partners[number - IN_FLIGHT]
        picked = scaled_pick(wanted[k][first:first + count], blocks, norm, dep)
        partners.append(along_grid(picked, k))
        if number == 0:
            scaled, tail = scaled_all(blocks, norm, picked)
            halo = lax.ppermute(tail, "tm", [(i, i + 1) for i in range(n_tm - 1)])

    results = {}
    for partner, (k, first, count, order) in zip(partners, CHUNKS):
        keep, send = pieces(
            pair_plan[0, k - 1, first:first + count, 0], lag_slots[order], scaled, halo, partner
        )
        routes = (ring_near, ring_far) if order == 0 else (ring_far, ring_near)
        got_one = along_tm(send, routes[0])
        got_two = along_tm(keep[2:] + got_one[2:], routes[1])
        got_three = along_tm(keep[1] + got_one[1] + got_two[1], other_half)
        results[k, first] = (keep[0] + got_one[0] + got_two[0] + got_three) / divisor
    rows = [
        jnp.concatenate([results[key] for key in sorted(results) if key[0] == k])
        for k in range(1, STEPS + 1)
    ]
    return jnp.stack(rows)[None, :, :, None]


def solution(mesh):
    in_specs = (P("grid", "tm"), P(), P("grid", None, None, None))
    out_specs = P("grid", None, None, "tm", None, None)
    return jax.shard_map(
        per_device, mesh=mesh, in_specs=in_specs, out_specs=out_specs, check_vma=False
    )
```

time: 602 us -> 299 us (0.50)
  the two profiles are of different devices: /device:TPU:1 before, /device:TPU:34 now
where the time goes in v1:
time: 299 us
  waiting for transfers between devices  157 us (53%)
  starting transfers between devices  61.9 us (21%)
  Pallas kernels  49.2 us (16%)
  local copies, waits for them, and re-layouts  24.8 us (8%)
  other arithmetic  5.83 us (2%)
    ppermute x25, waiting for transfers between devices, along_tm(): return lax.ppermute(value, 'tm', [(i, target(i)) for i in range(n_tm)])  91.8 us
    ppermute x9, waiting for transfers between devices, along_grid(): lax.ppermute(value, 'grid', [(i, (i + step) % n_grid) for i in range(n_gr...  49.9 us
    ppermute x25, starting transfers between devices, along_tm(): return lax.ppermute(value, 'tm', [(i, target(i)) for i in range(n_tm)])  48.9 us
    pallas_call x6, Pallas kernels, pieces(): pl.pallas_call(piece_kernel, grid_spec=pltpu.PrefetchScalarGridSpec(num_s...  35.3 us
    unnamed x26, local copies, waits for them, and re-layouts  23.1 us
    ppermute x1, waiting for transfers between devices, per_device(): halo = lax.ppermute(tail, 'tm', [(i, i + 1) for i in range(n_tm - 1)])  14.8 us
    ppermute x9, starting transfers between devices, along_grid(): lax.ppermute(value, 'grid', [(i, (i + step) % n_grid) for i in range(n_gr...  9.81 us
    pallas_call x6, Pallas kernels, scaled_pick(): pl.pallas_call(pick_kernel, grid_spec=pltpu.PrefetchScalarGridSpec(num_sc...  6.63 us
  transfers between devices with their start and end apart: 35, of which 17 were waited for; matrix products, arithmetic and copies ran while one was open for 2% of the time, Pallas kernels for 14%

profile of v1, /device:TPU:34, one launch (start us, length us, event | category | flops | bytes accessed | tf_op | source)
XLA Modules:
  0.0 298.8 jit_solution(15018854239520705029)
XLA Ops:
  0.0 3.4 %copy-done.1 = f32[2048,1024]{1,0:T(8,128)S(1)} copy-done((f32[2048,1024]{1,0:T(8,128)S(1)}, f32[2048,1024]{1,0:T(8,128)}, u32[]{:S(2)}) %copy-start.1) | copy-done | bytes 8388632
  6.2 2.9 collective-permute-start.1
  9.1 3.8 %collective-permute-start.2 = (f32[32,128]{1,0:T(8,128)S(1)}, f32[32,128]{1,0:T(8,128)S(1)}, u32[]{:S(2)}, u32[]{:S(2)}) collective-permute-start(f32[32,128]{1,0:T(8,128)S(1)} %local_sums.1), channel_id=1, source_target_pairs={{0,3},{1,4},{2,5},{3,6},{4,7},{5,0},{6,1},{7,2},{8,11},{9,12},{10,... | collective-permute-start | bytes 49160 | tf_op jit(solution)/shard_map/ppermute | solution.py:203
  14.9 3.1 %collective-permute-start.4 = (f32[32,128]{1,0:T(8,128)S(1)}, f32[32,128]{1,0:T(8,128)S(1)}, u32[]{:S(2)}, u32[]{:S(2)}) collective-permute-start(f32[32,128]{1,0:T(8,128)S(1)} %local_sums.1), channel_id=1, source_target_pairs={{0,5},{1,6},{2,7},{3,0},{4,1},{5,2},{6,3},{7,4},{8,13},{9,14},{10,... | collective-permute-start | bytes 49160 | tf_op jit(solution)/shard_map/ppermute | solution.py:203
  18.0 3.0 %collective-permute-start.5 = (f32[32,128]{1,0:T(8,128)S(1)}, f32[32,128]{1,0:T(8,128)S(1)}, u32[]{:S(2)}, u32[]{:S(2)}) collective-permute-start(f32[32,128]{1,0:T(8,128)S(1)} %local_sums.1), channel_id=1, source_target_pairs={{0,6},{1,7},{2,0},{3,1},{4,2},{5,3},{6,4},{7,5},{8,14},{9,15},{10,... | collective-permute-start | bytes 49160 | tf_op jit(solution)/shard_map/ppermute | solution.py:203
  24.8 3.4 %copy-done.2 = f32[2048,1024]{1,0:T(8,128)S(1)} copy-done((f32[2048,1024]{1,0:T(8,128)S(1)}, f32[2048,1024]{1,0:T(8,128)}, u32[]{:S(2)}) %copy-start.2) | copy-done | bytes 8388632
  29.3 6.2 %scaled_all.1 = (bf16[16,128,1024]{2,1,0:T(8,128)(2,1)S(1)}, bf16[16,128,256]{2,1,0:T(8,128)(2,1)}) custom-call(f32[16,128,1024]{2,1,0:T(8,128)S(1)} %bitcast.98, f32[2,16,128]{2,1,0:T(8,128)S(1)} %pad_maximum_fusion.norm_ref.dep_ref, bf16[4,128,1024]{2,1,0:T(8,128)(2,1)S(1)} %scaled_pick.6.dep_ref), custom_call_target="tpu_custom_call" | custom-call | flops 4194304 | bytes 12582912 | tf_op jit(solution)/shard_map/scaled_all/pallas_call | solution.py:108
  37.6 3.2 %collective-permute-start.8 = (bf16[16,128,256]{2,1,0:T(8,128)(2,1)}, bf16[16,128,256]{2,1,0:T(8,128)(2,1)}, u32[]{:S(2)}, u32[]{:S(2)}) collective-permute-start(bf16[16,128,256]{2,1,0:T(8,128)(2,1)} %get-tuple-element.21), channel_id=1, source_target_pairs={{0,1},{1,2},{2,3},{3,4},{4,5},{5,6},{6,7},{8,9},{9,10},{10,11},{11... | collective-permute-start | bytes 3145736 | tf_op jit(solution)/shard_map/ppermute | solution.py:243
  41.1 3.4 %copy-done.3 = f32[2048,1024]{1,0:T(8,128)S(1)} copy-done((f32[2048,1024]{1,0:T(8,128)S(1)}, f32[2048,1024]{1,0:T(8,128)}, u32[]{:S(2)}) %copy-start.3) | copy-done | bytes 8388632
  48.0 14.8 %collective-permute-done.8.halo_ref = bf16[16,128,256]{2,1,0:T(8,128)(2,1)} collective-permute-done((bf16[16,128,256]{2,1,0:T(8,128)(2,1)}, bf16[16,128,256]{2,1,0:T(8,128)(2,1)}, u32[]{:S(2)}, u32[]{:S(2)}) %collective-permute-start.8) | collective-permute-done | bytes 1048608 | tf_op jit(solution)/shard_map/ppermute | solution.py:243
  62.8 11.4 %collective-permute-done.9.b_ref.dep_ref = bf16[4,128,1024]{2,1,0:T(8,128)(2,1)S(1)} collective-permute-done((bf16[4,128,1024]{2,1,0:T(8,128)(2,1)S(1)}, bf16[4,128,1024]{2,1,0:T(8,128)(2,1)S(1)}, u32[]{:S(2)}, u32[]{:S(2)}) %collective-permute-start.9) | collective-permute-done | bytes 1048608 | tf_op jit(solution)/shard_map/ppermute | solution.py:200
  78.6 6.4 %pieces.6 = (f32[4,4,128,128]{3,2,1,0:T(8,128)S(1)}, f32[4,4,128,128]{3,2,1,0:T(8,128)}) custom-call(s32[4]{0:T(128)S(1)} %get-tuple-element.36.index_ref, s32[8]{0:T(128)S(1)} %and_select_fusion.1.lag_ref, bf16[16,128,1024]{2,1,0:T(8,128)(2,1)S(1)} %copy-done.9, bf16[16,128,256]{2,1,0:T(8,128)(2,1)} %collective-permute-done.8.halo_ref, ...), custom_call_target="tpu_custom_call" | custom-call | flops 2147483648 | bytes 4194304 | tf_op jit(solution)/shard_map/pieces/pallas_call | solution.py:166
  87.9 5.9 %pieces.7 = (f32[4,4,128,128]{3,2,1,0:T(8,128)S(1)}, f32[4,4,128,128]{3,2,1,0:T(8,128)S(1)}) custom-call(s32[4]{0:T(128)S(1)} %get-tuple-element.39.index_ref, s32[8]{0:T(128)S(1)} %and_select_fusion.lag_ref, bf16[16,128,1024]{2,1,0:T(8,128)(2,1)S(1)} %copy-done.10, bf16[16,128,256]{2,1,0:T(8,128)(2,1)} %collective-permute-done.8.halo_ref, ...), custom_call_target="tpu_custom_call" | custom-call | flops 2147483648 | bytes 4194304 | tf_op jit(solution)/shard_map/pieces/pallas_call | solution.py:166
  93.8 5.1 %collective-permute-start.14 = (f32[4,4,128,128]{3,2,1,0:T(8,128)S(1)}, f32[4,4,128,128]{3,2,1,0:T(8,128)S(1)}, u32[]{:S(2)}, u32[]{:S(2)}) collective-permute-start(f32[4,4,128,128]{3,2,1,0:T(8,128)S(1)} %get-tuple-element.25), channel_id=1, source_target_pairs={{0,3},{1,2},{2,1},{3,0},{4,7},{5,6},{6,5},{7,4},{8,11},{9,10},{10,... | collective-permute-start | bytes 3145736 | tf_op jit(solution)/shard_map/ppermute | solution.py:203
  98.9 7.7 %collective-permute-start.18 = (s32[8]{0:T(128)S(1)}, s32[8]{0:T(128)S(1)}, u32[]{:S(2)}, u32[]{:S(2)}) collective-permute-start(s32[8]{0:T(128)S(1)} %get-tuple-element.43), channel_id=1, source_target_pairs={{0,104},{8,112},{16,120},{24,0},{32,8},{40,16},{48,24},{56,32},{64... | collective-permute-start | bytes 104 | tf_op jit(solution)/shard_map/ppermute | solution.py:200
  107.9 3.4 %copy-done.4 = f32[2048,1024]{1,0:T(8,128)S(1)} copy-done((f32[2048,1024]{1,0:T(8,128)S(1)}, f32[2048,1024]{1,0:T(8,128)}, u32[]{:S(2)}) %copy-start.4) | copy-done | bytes 8388632
  118.3 4.2 %collective-permute-done.14 = f32[4,4,128,128]{3,2,1,0:T(8,128)S(1)} collective-permute-done((f32[4,4,128,128]{3,2,1,0:T(8,128)S(1)}, f32[4,4,128,128]{3,2,1,0:T(8,128)S(1)}, u32[]{:S(2)}, u32[]{:S(2)}) %collective-permute-start.14) | collective-permute-done | bytes 1048608 | tf_op jit(solution)/shard_map/ppermute | solution.py:203
  124.3 13.7 %collective-permute-done.19.dep_ref.b_ref = bf16[4,128,1024]{2,1,0:T(8,128)(2,1)S(1)} collective-permute-done((bf16[4,128,1024]{2,1,0:T(8,128)(2,1)S(1)}, bf16[4,128,1024]{2,1,0:T(8,128)(2,1)S(1)}, u32[]{:S(2)}, u32[]{:S(2)}) %collective-permute-start.19) | collective-permute-done | bytes 1048608 | tf_op jit(solution)/shard_map/ppermute | solution.py:200
  139.2 21.3 %collective-permute-done.24.dep_ref.b_ref = bf16[4,128,1024]{2,1,0:T(8,128)(2,1)S(1)} collective-permute-done((bf16[4,128,1024]{2,1,0:T(8,128)(2,1)S(1)}, bf16[4,128,1024]{2,1,0:T(8,128)(2,1)S(1)}, u32[]{:S(2)}, u32[]{:S(2)}) %collective-permute-start.24) | collective-permute-done | bytes 1048608 | tf_op jit(solution)/shard_map/ppermute | solution.py:200
  162.7 5.7 %pieces.10 = (f32[4,4,128,128]{3,2,1,0:T(8,128)S(1)}, f32[4,4,128,128]{3,2,1,0:T(8,128)S(1)}) custom-call(s32[4]{0:T(128)S(1)} %get-tuple-element.41.index_ref, s32[8]{0:T(128)S(1)} %and_select_fusion.1.lag_ref, bf16[16,128,1024]{2,1,0:T(8,128)(2,1)S(1)} %copy-done.11, bf16[16,128,256]{2,1,0:T(8,128)(2,1)} %collective-permute-done.8.halo_ref, ...), custom_call_target="tpu_custom_call" | custom-call | flops 2147483648 | bytes 4194304 | tf_op jit(solution)/shard_map/pieces/pallas_call | solution.py:166
  170.6 4.8 %collective-permute-start.12 = (f32[4,128,128]{2,1,0:T(8,128)S(1)}, f32[4,128,128]{2,1,0:T(8,128)S(1)}, u32[]{:S(2)}, u32[]{:S(2)}) collective-permute-start(f32[4,128,128]{2,1,0:T(8,128)S(1)} %fusion.20), channel_id=1, source_target_pairs={{0,4},{1,5},{2,6},{3,7},{4,0},{5,1},{6,2},{7,3},{8,12},{9,13},{10,... | collective-permute-start | bytes 786440 | tf_op jit(solution)/shard_map/ppermute | solution.py:203
  175.4 5.7 %pieces.11 = (f32[4,4,128,128]{3,2,1,0:T(8,128)S(1)}, f32[4,4,128,128]{3,2,1,0:T(8,128)S(1)}) custom-call(s32[4]{0:T(128)S(1)} %get-tuple-element.40.index_ref, s32[8]{0:T(128)S(1)} %and_select_fusion.lag_ref, bf16[16,128,1024]{2,1,0:T(8,128)(2,1)S(1)} %copy-done.11, bf16[16,128,256]{2,1,0:T(8,128)(2,1)} %collective-permute-done.8.halo_ref, ...), custom_call_target="tpu_custom_call" | custom-call | flops 2147483648 | bytes 4194304 | tf_op jit(solution)/shard_map/pieces/pallas_call | solution.py:166
  183.0 32.3 %collective-permute-done.12 = f32[4,128,128]{2,1,0:T(8,128)S(1)} collective-permute-done((f32[4,128,128]{2,1,0:T(8,128)S(1)}, f32[4,128,128]{2,1,0:T(8,128)S(1)}, u32[]{:S(2)}, u32[]{:S(2)}) %collective-permute-start.12) | collective-permute-done | bytes 262176 | tf_op jit(solution)/shard_map/ppermute | solution.py:203
  216.4 5.8 %pieces.8 = (f32[4,4,128,128]{3,2,1,0:T(8,128)S(1)}, f32[4,4,128,128]{3,2,1,0:T(8,128)S(1)}) custom-call(s32[4]{0:T(128)S(1)} %get-tuple-element.38.index_ref, s32[8]{0:T(128)S(1)} %and_select_fusion.1.lag_ref, bf16[16,128,1024]{2,1,0:T(8,128)(2,1)S(1)} %copy-done.11, bf16[16,128,256]{2,1,0:T(8,128)(2,1)} %collective-permute-done.8.halo_ref, ...), custom_call_target="tpu_custom_call" | custom-call | flops 2147483648 | bytes 4194304 | tf_op jit(solution)/shard_map/pieces/pallas_call | solution.py:166
  224.0 5.7 %pieces.9 = (f32[4,4,128,128]{3,2,1,0:T(8,128)S(1)}, f32[4,4,128,128]{3,2,1,0:T(8,128)S(1)}) custom-call(s32[4]{0:T(128)S(1)} %get-tuple-element.37.index_ref, s32[8]{0:T(128)S(1)} %and_select_fusion.lag_ref, bf16[16,128,1024]{2,1,0:T(8,128)(2,1)S(1)} %copy-done.11, bf16[16,128,256]{2,1,0:T(8,128)(2,1)} %collective-permute-done.8.halo_ref, ...), custom_call_target="tpu_custom_call" | custom-call | flops 2147483648 | bytes 4194304 | tf_op jit(solution)/shard_map/pieces/pallas_call | solution.py:166
  233.5 33.6 %collective-permute-done.30 = f32[2,4,128,128]{3,2,1,0:T(8,128)S(1)} collective-permute-done((f32[2,4,128,128]{3,2,1,0:T(8,128)S(1)}, f32[2,4,128,128]{3,2,1,0:T(8,128)S(1)}, u32[]{:S(2)}, u32[]{:S(2)}) %collective-permute-start.30) | collective-permute-done | bytes 524320 | tf_op jit(solution)/shard_map/ppermute | solution.py:203
  267.2 3.3 %collective-permute-start.31 = (f32[4,128,128]{2,1,0:T(8,128)S(1)}, f32[4,128,128]{2,1,0:T(8,128)S(1)}, u32[]{:S(2)}, u32[]{:S(2)}) collective-permute-start(f32[4,128,128]{2,1,0:T(8,128)S(1)} %fusion.4), channel_id=1, source_target_pairs={{0,4},{1,5},{2,6},{3,7},{4,0},{5,1},{6,2},{7,3},{8,12},{9,13},{10,... | collective-permute-start | bytes 786440 | tf_op jit(solution)/shard_map/ppermute | solution.py:203
  273.5 4.5 %collective-permute-done.31 = f32[4,128,128]{2,1,0:T(8,128)S(1)} collective-permute-done((f32[4,128,128]{2,1,0:T(8,128)S(1)}, f32[4,128,128]{2,1,0:T(8,128)S(1)}, u32[]{:S(2)}, u32[]{:S(2)}) %collective-permute-start.31) | collective-permute-done | bytes 262176 | tf_op jit(solution)/shard_map/ppermute | solution.py:203
  278.1 3.4 %collective-permute-done.34 = f32[4,128,128]{2,1,0:T(8,128)S(1)} collective-permute-done((f32[4,128,128]{2,1,0:T(8,128)S(1)}, f32[4,128,128]{2,1,0:T(8,128)S(1)}, u32[]{:S(2)}, u32[]{:S(2)}) %collective-permute-start.34) | collective-permute-done | bytes 262176 | tf_op jit(solution)/shard_map/ppermute | solution.py:203
  281.6 2.9 collective-permute-done.22
  284.5 3.0 collective-permute-start.23
  288.5 6.1 %collective-permute-done.23 = f32[4,128,128]{2,1,0:T(8,128)S(1)} collective-permute-done((f32[4,128,128]{2,1,0:T(8,128)S(1)}, f32[4,128,128]{2,1,0:T(8,128)S(1)}, u32[]{:S(2)}, u32[]{:S(2)}) %collective-permute-start.23) | collective-permute-done | bytes 262176 | tf_op jit(solution)/shard_map/ppermute | solution.py:203
  (122 shorter events, 55.2 us)
Async XLA Ops:
  4.5 13.4 %collective-permute-start = (f32[32,128]{1,0:T(8,128)S(1)}, f32[32,128]{1,0:T(8,128)S(1)}, u32[]{:S(2)}, u32[]{:S(2)}) collective-permute-start(f32[32,128]{1,0:T(8,128)S(1)} %local_sums.1), channel_id=1, source_target_pairs={{0,1},{1,2},{2,3},{3,4},{4,5},{5,6},{6,7},{7,0},{8,9},{9,10},{10,1... | collective-permute-start | bytes 49160 | tf_op jit(solution)/shard_map/ppermute | solution.py:203
  6.2 14.8 %collective-permute-start.1 = (f32[32,128]{1,0:T(8,128)S(1)}, f32[32,128]{1,0:T(8,128)S(1)}, u32[]{:S(2)}, u32[]{:S(2)}) collective-permute-start(f32[32,128]{1,0:T(8,128)S(1)} %local_sums.1), channel_id=1, source_target_pairs={{0,2},{1,3},{2,4},{3,5},{4,6},{5,7},{6,0},{7,1},{8,10},{9,11},{10,... | collective-permute-start | bytes 49160 | tf_op jit(solution)/shard_map/ppermute | solution.py:203
  9.1 13.7 %collective-permute-start.2 = (f32[32,128]{1,0:T(8,128)S(1)}, f32[32,128]{1,0:T(8,128)S(1)}, u32[]{:S(2)}, u32[]{:S(2)}) collective-permute-start(f32[32,128]{1,0:T(8,128)S(1)} %local_sums.1), channel_id=1, source_target_pairs={{0,3},{1,4},{2,5},{3,6},{4,7},{5,0},{6,1},{7,2},{8,11},{9,12},{10,... | collective-permute-start | bytes 49160 | tf_op jit(solution)/shard_map/ppermute | solution.py:203
  12.8 9.9 %collective-permute-start.3 = (f32[32,128]{1,0:T(8,128)S(1)}, f32[32,128]{1,0:T(8,128)S(1)}, u32[]{:S(2)}, u32[]{:S(2)}) collective-permute-start(f32[32,128]{1,0:T(8,128)S(1)} %local_sums.1), channel_id=1, source_target_pairs={{0,4},{1,5},{2,6},{3,7},{4,0},{5,1},{6,2},{7,3},{8,12},{9,13},{10,... | collective-permute-start | bytes 49160 | tf_op jit(solution)/shard_map/ppermute | solution.py:203
  14.9 7.9 %collective-permute-start.4 = (f32[32,128]{1,0:T(8,128)S(1)}, f32[32,128]{1,0:T(8,128)S(1)}, u32[]{:S(2)}, u32[]{:S(2)}) collective-permute-start(f32[32,128]{1,0:T(8,128)S(1)} %local_sums.1), channel_id=1, source_target_pairs={{0,5},{1,6},{2,7},{3,0},{4,1},{5,2},{6,3},{7,4},{8,13},{9,14},{10,... | collective-permute-start | bytes 49160 | tf_op jit(solution)/shard_map/ppermute | solution.py:203
  18.0 5.4 %collective-permute-start.5 = (f32[32,128]{1,0:T(8,128)S(1)}, f32[32,128]{1,0:T(8,128)S(1)}, u32[]{:S(2)}, u32[]{:S(2)}) collective-permute-start(f32[32,128]{1,0:T(8,128)S(1)} %local_sums.1), channel_id=1, source_target_pairs={{0,6},{1,7},{2,0},{3,1},{4,2},{5,3},{6,4},{7,5},{8,14},{9,15},{10,... | collective-permute-start | bytes 49160 | tf_op jit(solution)/shard_map/ppermute | solution.py:203
  37.5 36.7 %collective-permute-start.9 = (bf16[4,128,1024]{2,1,0:T(8,128)(2,1)S(1)}, bf16[4,128,1024]{2,1,0:T(8,128)(2,1)S(1)}, u32[]{:S(2)}, u32[]{:S(2)}) collective-permute-start(bf16[4,128,1024]{2,1,0:T(8,128)(2,1)S(1)} %scaled_pick.6.dep_ref), channel_id=1, source_target_pairs={{0,8},{8,16},{16,24},{24,32},{32,40},{40,48},{48,56},{56,64},{64,7... | collective-permute-start | bytes 3145736 | tf_op jit(solution)/shard_map/ppermute | solution.py:200
  37.6 25.1 %collective-permute-start.8 = (bf16[16,128,256]{2,1,0:T(8,128)(2,1)}, bf16[16,128,256]{2,1,0:T(8,128)(2,1)}, u32[]{:S(2)}, u32[]{:S(2)}) collective-permute-start(bf16[16,128,256]{2,1,0:T(8,128)(2,1)} %get-tuple-element.21), channel_id=1, source_target_pairs={{0,1},{1,2},{2,3},{3,4},{4,5},{5,6},{6,7},{8,9},{9,10},{10,11},{11... | collective-permute-start | bytes 3145736 | tf_op jit(solution)/shard_map/ppermute | solution.py:243
  45.6 40.1 %collective-permute-start.13 = (bf16[4,128,1024]{2,1,0:T(8,128)(2,1)S(1)}, bf16[4,128,1024]{2,1,0:T(8,128)(2,1)}, u32[]{:S(2)}, u32[]{:S(2)}) collective-permute-start(bf16[4,128,1024]{2,1,0:T(8,128)(2,1)S(1)} %scaled_pick.7), channel_id=1, source_target_pairs={{0,8},{8,16},{16,24},{24,32},{32,40},{40,48},{48,56},{56,64},{64,7... | collective-permute-start | bytes 3145736 | tf_op jit(solution)/shard_map/ppermute | solution.py:200
  85.0 28.8 %collective-permute-start.10 = (f32[4,4,128,128]{3,2,1,0:T(8,128)}, f32[4,4,128,128]{3,2,1,0:T(8,128)}, u32[]{:S(2)}, u32[]{:S(2)}) collective-permute-start(f32[4,4,128,128]{3,2,1,0:T(8,128)} %get-tuple-element.23), channel_id=1, source_target_pairs={{0,1},{1,0},{2,3},{3,2},{4,5},{5,4},{6,7},{7,6},{8,9},{9,8},{10,11... | collective-permute-start | bytes 3145736 | tf_op jit(solution)/shard_map/ppermute | solution.py:203
  93.8 28.7 %collective-permute-start.14 = (f32[4,4,128,128]{3,2,1,0:T(8,128)S(1)}, f32[4,4,128,128]{3,2,1,0:T(8,128)S(1)}, u32[]{:S(2)}, u32[]{:S(2)}) collective-permute-start(f32[4,4,128,128]{3,2,1,0:T(8,128)S(1)} %get-tuple-element.25), channel_id=1, source_target_pairs={{0,3},{1,2},{2,1},{3,0},{4,7},{5,6},{6,5},{7,4},{8,11},{9,10},{10,... | collective-permute-start | bytes 3145736 | tf_op jit(solution)/shard_map/ppermute | solution.py:203
  98.9 9.0 %collective-permute-start.18 = (s32[8]{0:T(128)S(1)}, s32[8]{0:T(128)S(1)}, u32[]{:S(2)}, u32[]{:S(2)}) collective-permute-start(s32[8]{0:T(128)S(1)} %get-tuple-element.43), channel_id=1, source_target_pairs={{0,104},{8,112},{16,120},{24,0},{32,8},{40,16},{48,24},{56,32},{64... | collective-permute-start | bytes 104 | tf_op jit(solution)/shard_map/ppermute | solution.py:200
  112.4 25.6 %collective-permute-start.19 = (bf16[4,128,1024]{2,1,0:T(8,128)(2,1)S(1)}, bf16[4,128,1024]{2,1,0:T(8,128)(2,1)S(1)}, u32[]{:S(2)}, u32[]{:S(2)}) collective-permute-start(bf16[4,128,1024]{2,1,0:T(8,128)(2,1)S(1)} %scaled_pick.8), channel_id=1, source_target_pairs={{0,24},{8,32},{16,40},{24,48},{32,56},{40,64},{48,72},{56,80},{64,... | collective-permute-start | bytes 3145736 | tf_op jit(solution)/shard_map/ppermute | solution.py:200
  113.6 46.9 %collective-permute-start.24 = (bf16[4,128,1024]{2,1,0:T(8,128)(2,1)S(1)}, bf16[4,128,1024]{2,1,0:T(8,128)(2,1)S(1)}, u32[]{:S(2)}, u32[]{:S(2)}) collective-permute-start(bf16[4,128,1024]{2,1,0:T(8,128)(2,1)S(1)} %scaled_pick.10), channel_id=1, source_target_pairs={{0,24},{8,32},{16,40},{24,48},{32,56},{40,64},{48,72},{56,80},{64,... | collective-permute-start | bytes 3145736 | tf_op jit(solution)/shard_map/ppermute | solution.py:200
  114.9 54.7 %collective-permute-start.11 = (f32[2,4,128,128]{3,2,1,0:T(8,128)S(1)}, f32[2,4,128,128]{3,2,1,0:T(8,128)S(1)}, u32[]{:S(2)}, u32[]{:S(2)}) collective-permute-start(f32[2,4,128,128]{3,2,1,0:T(8,128)S(1)} %slice_add_fusion.5), channel_id=1, source_target_pairs={{0,3},{1,2},{2,1},{3,0},{4,7},{5,6},{6,5},{7,4},{8,11},{9,10},{10,... | collective-permute-start | bytes 1572872 | tf_op jit(solution)/shard_map/ppermute | solution.py:203
  122.6 58.6 %collective-permute-start.15 = (f32[2,4,128,128]{3,2,1,0:T(8,128)S(1)}, f32[2,4,128,128]{3,2,1,0:T(8,128)S(1)}, u32[]{:S(2)}, u32[]{:S(2)}) collective-permute-start(f32[2,4,128,128]{3,2,1,0:T(8,128)S(1)} %slice_add_fusion.4), channel_id=1, source_target_pairs={{0,1},{1,0},{2,3},{3,2},{4,5},{5,4},{6,7},{7,6},{8,9},{9,8},{10,11... | collective-permute-start | bytes 1572872 | tf_op jit(solution)/shard_map/ppermute | solution.py:203
  139.1 77.3 %collective-permute-start.20 = (bf16[4,128,1024]{2,1,0:T(8,128)(2,1)S(1)}, bf16[4,128,1024]{2,1,0:T(8,128)(2,1)S(1)}, u32[]{:S(2)}, u32[]{:S(2)}) collective-permute-start(bf16[4,128,1024]{2,1,0:T(8,128)(2,1)S(1)} %scaled_pick.9), channel_id=1, source_target_pairs={{0,16},{8,24},{16,32},{24,40},{32,48},{40,56},{48,64},{56,72},{64,... | collective-permute-start | bytes 3145736 | tf_op jit(solution)/shard_map/ppermute | solution.py:200
  161.6 62.4 %collective-permute-start.25 = (bf16[4,128,1024]{2,1,0:T(8,128)(2,1)S(1)}, bf16[4,128,1024]{2,1,0:T(8,128)(2,1)S(1)}, u32[]{:S(2)}, u32[]{:S(2)}) collective-permute-start(bf16[4,128,1024]{2,1,0:T(8,128)(2,1)S(1)} %scaled_pick.11), channel_id=1, source_target_pairs={{0,16},{8,24},{16,32},{24,40},{32,48},{40,56},{48,64},{56,72},{64,... | collective-permute-start | bytes 3145736 | tf_op jit(solution)/shard_map/ppermute | solution.py:200
  168.4 63.6 %collective-permute-start.29 = (f32[4,4,128,128]{3,2,1,0:T(8,128)S(1)}, f32[4,4,128,128]{3,2,1,0:T(8,128)S(1)}, u32[]{:S(2)}, u32[]{:S(2)}) collective-permute-start(f32[4,4,128,128]{3,2,1,0:T(8,128)S(1)} %get-tuple-element.31), channel_id=1, source_target_pairs={{0,1},{1,0},{2,3},{3,2},{4,5},{5,4},{6,7},{7,6},{8,9},{9,8},{10,11... | collective-permute-start | bytes 3145736 | tf_op jit(solution)/shard_map/ppermute | solution.py:203
  170.6 44.8 %collective-permute-start.12 = (f32[4,128,128]{2,1,0:T(8,128)S(1)}, f32[4,128,128]{2,1,0:T(8,128)S(1)}, u32[]{:S(2)}, u32[]{:S(2)}) collective-permute-start(f32[4,128,128]{2,1,0:T(8,128)S(1)} %fusion.20), channel_id=1, source_target_pairs={{0,4},{1,5},{2,6},{3,7},{4,0},{5,1},{6,2},{7,3},{8,12},{9,13},{10,... | collective-permute-start | bytes 786440 | tf_op jit(solution)/shard_map/ppermute | solution.py:203
  181.2 52.1 %collective-permute-start.32 = (f32[4,4,128,128]{3,2,1,0:T(8,128)S(1)}, f32[4,4,128,128]{3,2,1,0:T(8,128)S(1)}, u32[]{:S(2)}, u32[]{:S(2)}) collective-permute-start(f32[4,4,128,128]{3,2,1,0:T(8,128)S(1)} %get-tuple-element.33), channel_id=1, source_target_pairs={{0,3},{1,2},{2,1},{3,0},{4,7},{5,6},{6,5},{7,4},{8,11},{9,10},{10,... | collective-permute-start | bytes 3145736 | tf_op jit(solution)/shard_map/ppermute | solution.py:203
  215.4 18.0 %collective-permute-start.16 = (f32[4,128,128]{2,1,0:T(8,128)S(1)}, f32[4,128,128]{2,1,0:T(8,128)S(1)}, u32[]{:S(2)}, u32[]{:S(2)}) collective-permute-start(f32[4,128,128]{2,1,0:T(8,128)S(1)} %fusion.16), channel_id=1, source_target_pairs={{0,4},{1,5},{2,6},{3,7},{4,0},{5,1},{6,2},{7,3},{8,12},{9,13},{10,... | collective-permute-start | bytes 786440 | tf_op jit(solution)/shard_map/ppermute | solution.py:203
  222.2 48.8 %collective-permute-start.21 = (f32[4,4,128,128]{3,2,1,0:T(8,128)S(1)}, f32[4,4,128,128]{3,2,1,0:T(8,128)S(1)}, u32[]{:S(2)}, u32[]{:S(2)}) collective-permute-start(f32[4,4,128,128]{3,2,1,0:T(8,128)S(1)} %get-tuple-element.27), channel_id=1, source_target_pairs={{0,1},{1,0},{2,3},{3,2},{4,5},{5,4},{6,7},{7,6},{8,9},{9,8},{10,11... | collective-permute-start | bytes 3145736 | tf_op jit(solution)/shard_map/ppermute | solution.py:203
  229.8 43.6 %collective-permute-start.26 = (f32[4,4,128,128]{3,2,1,0:T(8,128)S(1)}, f32[4,4,128,128]{3,2,1,0:T(8,128)S(1)}, u32[]{:S(2)}, u32[]{:S(2)}) collective-permute-start(f32[4,4,128,128]{3,2,1,0:T(8,128)S(1)} %get-tuple-element.29), channel_id=1, source_target_pairs={{0,3},{1,2},{2,1},{3,0},{4,7},{5,6},{6,5},{7,4},{8,11},{9,10},{10,... | collective-permute-start | bytes 3145736 | tf_op jit(solution)/shard_map/ppermute | solution.py:203
  232.1 35.0 %collective-permute-start.30 = (f32[2,4,128,128]{3,2,1,0:T(8,128)S(1)}, f32[2,4,128,128]{3,2,1,0:T(8,128)S(1)}, u32[]{:S(2)}, u32[]{:S(2)}) collective-permute-start(f32[2,4,128,128]{3,2,1,0:T(8,128)S(1)} %slice_add_fusion.1), channel_id=1, source_target_pairs={{0,3},{1,2},{2,1},{3,0},{4,7},{5,6},{6,5},{7,4},{8,11},{9,10},{10,... | collective-permute-start | bytes 1572872 | tf_op jit(solution)/shard_map/ppermute | solution.py:203
  233.3 37.2 %collective-permute-start.33 = (f32[2,4,128,128]{3,2,1,0:T(8,128)S(1)}, f32[2,4,128,128]{3,2,1,0:T(8,128)S(1)}, u32[]{:S(2)}, u32[]{:S(2)}) collective-permute-start(f32[2,4,128,128]{3,2,1,0:T(8,128)S(1)} %slice_add_fusion), channel_id=1, source_target_pairs={{0,1},{1,0},{2,3},{3,2},{4,5},{5,4},{6,7},{7,6},{8,9},{9,8},{10,11... | collective-permute-start | bytes 1572872 | tf_op jit(solution)/shard_map/ppermute | solution.py:203
  267.2 10.8 %collective-permute-start.31 = (f32[4,128,128]{2,1,0:T(8,128)S(1)}, f32[4,128,128]{2,1,0:T(8,128)S(1)}, u32[]{:S(2)}, u32[]{:S(2)}) collective-permute-start(f32[4,128,128]{2,1,0:T(8,128)S(1)} %fusion.4), channel_id=1, source_target_pairs={{0,4},{1,5},{2,6},{3,7},{4,0},{5,1},{6,2},{7,3},{8,12},{9,13},{10,... | collective-permute-start | bytes 786440 | tf_op jit(solution)/shard_map/ppermute | solution.py:203
  270.5 11.0 %collective-permute-start.34 = (f32[4,128,128]{2,1,0:T(8,128)S(1)}, f32[4,128,128]{2,1,0:T(8,128)S(1)}, u32[]{:S(2)}, u32[]{:S(2)}) collective-permute-start(f32[4,128,128]{2,1,0:T(8,128)S(1)} %fusion), channel_id=1, source_target_pairs={{0,4},{1,5},{2,6},{3,7},{4,0},{5,1},{6,2},{7,3},{8,12},{9,13},{10,... | collective-permute-start | bytes 786440 | tf_op jit(solution)/shard_map/ppermute | solution.py:203
  271.0 13.5 %collective-permute-start.22 = (f32[2,4,128,128]{3,2,1,0:T(8,128)S(1)}, f32[2,4,128,128]{3,2,1,0:T(8,128)S(1)}, u32[]{:S(2)}, u32[]{:S(2)}) collective-permute-start(f32[2,4,128,128]{3,2,1,0:T(8,128)S(1)} %slice_add_fusion.3), channel_id=1, source_target_pairs={{0,3},{1,2},{2,1},{3,0},{4,7},{5,6},{6,5},{7,4},{8,11},{9,10},{10,... | collective-permute-start | bytes 1572872 | tf_op jit(solution)/shard_map/ppermute | solution.py:203
  273.4 14.1 %collective-permute-start.27 = (f32[2,4,128,128]{3,2,1,0:T(8,128)S(1)}, f32[2,4,128,128]{3,2,1,0:T(8,128)S(1)}, u32[]{:S(2)}, u32[]{:S(2)}) collective-permute-start(f32[2,4,128,128]{3,2,1,0:T(8,128)S(1)} %slice_add_fusion.2), channel_id=1, source_target_pairs={{0,1},{1,0},{2,3},{3,2},{4,5},{5,4},{6,7},{7,6},{8,9},{9,8},{10,11... | collective-permute-start | bytes 1572872 | tf_op jit(solution)/shard_map/ppermute | solution.py:203
  284.5 10.0 %collective-permute-start.23 = (f32[4,128,128]{2,1,0:T(8,128)S(1)}, f32[4,128,128]{2,1,0:T(8,128)S(1)}, u32[]{:S(2)}, u32[]{:S(2)}) collective-permute-start(f32[4,128,128]{2,1,0:T(8,128)S(1)} %fusion.12), channel_id=1, source_target_pairs={{0,4},{1,5},{2,6},{3,7},{4,0},{5,1},{6,2},{7,3},{8,12},{9,13},{10,... | collective-permute-start | bytes 786440 | tf_op jit(solution)/shard_map/ppermute | solution.py:203
  287.6 9.8 %collective-permute-start.28 = (f32[4,128,128]{2,1,0:T(8,128)S(1)}, f32[4,128,128]{2,1,0:T(8,128)S(1)}, u32[]{:S(2)}, u32[]{:S(2)}) collective-permute-start(f32[4,128,128]{2,1,0:T(8,128)S(1)} %fusion.8), channel_id=1, source_target_pairs={{0,4},{1,5},{2,6},{3,7},{4,0},{5,1},{6,2},{7,3},{8,12},{9,13},{10,... | collective-permute-start | bytes 786440 | tf_op jit(solution)/shard_map/ppermute | solution.py:203
  (16 other events, 111.3 us)

commit v2 on v1

v2 whole, which is shorter than its diff:
```python
import functools

import jax
import jax.numpy as jnp
from jax import lax
from jax.experimental import pallas as pl
from jax.experimental.pallas import tpu as pltpu
from jax.sharding import PartitionSpec as P

SUB = 128
LANES = 128
HALO = 256
STEPS = 3
PAIRS = 8
RING = 4
FEW, MANY = 12 << 20, 56 << 20


def sums_kernel(x_ref, out_ref):
    for sub in range(4):
        rows = slice(sub * SUB, (sub + 1) * SUB)
        total = jnp.zeros((SUB, LANES), jnp.float32)
        square = jnp.zeros((SUB, LANES), jnp.float32)
        for tile in range(x_ref.shape[1] // LANES):
            value = x_ref[rows, tile * LANES:(tile + 1) * LANES]
            total = total + value
            square = square + value * value
        total = jnp.sum(total.T, axis=0, keepdims=True)
        square = jnp.sum(square.T, axis=0, keepdims=True)
        for copy in range(out_ref.shape[0]):
            out_ref[copy, sub:sub + 1, :] = total
            out_ref[copy, 4 + sub:5 + sub, :] = square


def local_sums(anomalies, copies):
    points, hours = anomalies.shape
    steps = points // (4 * SUB)
    return pl.pallas_call(
        sums_kernel,
        grid=(steps,),
        in_specs=[pl.BlockSpec((4 * SUB, hours), lambda i: (i, 0))],
        out_specs=pl.BlockSpec((copies, 8, LANES), lambda i: (0, i, 0)),
        out_shape=jax.ShapeDtypeStruct((copies, 8 * steps, LANES), jnp.float32),
        compiler_params=pltpu.CompilerParams(vmem_limit_bytes=MANY),
        cost_estimate=pl.CostEstimate(
            flops=3 * points * hours, bytes_accessed=4 * points * hours, transcendentals=0
        ),
        name="local_sums",
    )(anomalies)


def norm_kernel(hours, sums_ref, norm_ref):
    total = sums_ref[0]
    for part in range(1, sums_ref.shape[0]):
        total = total + sums_ref[part]
    for group in range(total.shape[0] // 8):
        center = total[8 * group:8 * group + 4] / hours
        spread = total[8 * group + 4:8 * group + 8] / hours - center * center
        norm_ref[0, 4 * group:4 * group + 4, :] = center
        norm_ref[1, 4 * group:4 * group + 4, :] = lax.rsqrt(spread + 1e-05)


def norms(sums, hours):
    rows = sums.shape[1] // 2
    return pl.pallas_call(
        functools.partial(norm_kernel, hours),
        out_shape=jax.ShapeDtypeStruct((2, rows, LANES), jnp.float32),
        name="norms",
    )(sums)


def scale_rows(x, center_row, inverse_row, store):
    center = jnp.broadcast_to(center_row, (SUB, LANES)).T
    inverse = jnp.broadcast_to(inverse_row, (SUB, LANES)).T
    for tile in range(x.shape[1] // LANES):
        cols = slice(tile * LANES, (tile + 1) * LANES)
        store(cols, ((x[:, cols] - center) * inverse).astype(jnp.bfloat16))


def scale_kernel(counts, index_ref, x_ref, norm_ref, scaled_ref, tail_ref, *refs):
    send_refs, (wide, narrow, came, went) = refs[:len(counts)], refs[len(counts):]
    subs, _, hours = x_ref.shape

    def arriving(i):
        return pltpu.make_async_copy(x_ref.at[i], wide.at[i], came.at[i])

    for i in range(subs):
        arriving(i).start()
    for i in range(subs):
        arriving(i).wait()

        def store(cols, value):
            narrow[i, :, cols] = value

        scale_rows(wide.at[i], norm_ref[0, i:i + 1, :], norm_ref[1, i:i + 1, :], store)
    leaving = [pltpu.make_async_copy(narrow.at[:, :, hours - HALO:], tail_ref, went.at[0])]
    for send_ref, count in zip(send_refs, counts):
        for i in range(count):
            number = len(leaving)
            leaving.append(
                pltpu.make_async_copy(
                    narrow.at[index_ref[number - 1]], send_ref.at[i], went.at[number]
                )
            )
    leaving.append(pltpu.make_async_copy(narrow, scaled_ref, went.at[len(leaving)]))
    for copy in leaving:
        copy.start()
    for copy in leaving:
        copy.wait()


def scaled_parts(index, counts, blocks, norm):
    subs, _, hours = blocks.shape

    def shape(count, width):
        return jax.ShapeDtypeStruct((count, SUB, width), jnp.bfloat16)

    shapes = [shape(subs, hours), shape(subs, HALO)] + [shape(count, hours) for count in counts]
    return pl.pallas_call(
        functools.partial(scale_kernel, counts),
        in_specs=[
            pl.BlockSpec(memory_space=pltpu.SMEM),
            pl.BlockSpec(memory_space=pl.ANY),
            pl.BlockSpec(memory_space=pltpu.VMEM),
        ],
        out_specs=[pl.BlockSpec(memory_space=pl.ANY)] * len(shapes),
        out_shape=shapes,
        scratch_shapes=[
            pltpu.VMEM((subs, SUB, hours), jnp.float32),
            pltpu.VMEM((subs, SUB, hours), jnp.bfloat16),
            pltpu.SemaphoreType.DMA((subs,)),
            pltpu.SemaphoreType.DMA((sum(counts) + 2,)),
        ],
        compiler_params=pltpu.CompilerParams(vmem_limit_bytes=MANY),
        cost_estimate=pl.CostEstimate(
            flops=2 * subs * SUB * hours, bytes_accessed=10 * subs * SUB * hours, transcendentals=0
        ),
        name="scaled_parts",
    )(index, blocks, norm)


def piece_kernel(index_ref, lag_ref, a_ref, halo_ref, b_ref, *refs):
    keep_ref, send_ref, long_ref, shift_ref = refs[-4:]
    hours = a_ref.shape[2]
    lags = lag_ref.shape[0]
    long_ref[:, :HALO] = halo_ref[0]
    long_ref[:, HALO:] = a_ref[0]
    lane = lax.broadcasted_iota(jnp.int32, (SUB, LANES), 1)
    for slot in range(lags):
        lag = lag_ref[slot]
        turn = lag & (LANES - 1)
        first = HALO - LANES - (lag - turn)

        def turned(tile):
            start = pl.multiple_of(first + tile * LANES, LANES)
            return pltpu.roll(long_ref[:, pl.ds(start, LANES)], turn, 1)

        before = turned(0)
        for tile in range(hours // LANES):
            here = turned(tile + 1)
            shift_ref[slot * SUB:(slot + 1) * SUB, tile * LANES:(tile + 1) * LANES] = jnp.where(
                lane < turn, before, here
            )
            before = here
    piece = lax.dot_general(
        shift_ref[...], b_ref[0], (((1,), (1,)), ((), ())), preferred_element_type=jnp.float32
    )
    half = lags // 2
    keep_ref[...] = piece[:half * SUB].reshape(half, 1, SUB, SUB)
    send_ref[...] = piece[half * SUB:].reshape(half, 1, SUB, SUB)


def pieces(index, lags, scaled, halo, partner, start, deps):
    count, hours = index.shape[0], partner.shape[2]
    half = lags.shape[0] // 2
    out = jax.ShapeDtypeStruct((half, count, SUB, SUB), jnp.float32)
    return pl.pallas_call(
        piece_kernel,
        grid_spec=pltpu.PrefetchScalarGridSpec(
            num_scalar_prefetch=2,
            grid=(count,),
            in_specs=[
                pl.BlockSpec((1, SUB, hours), lambda i, index, lags: (index[i], 0, 0)),
                pl.BlockSpec((1, SUB, HALO), lambda i, index, lags: (index[i], 0, 0)),
                pl.BlockSpec((1, SUB, hours), lambda i, index, lags: (start + i, 0, 0)),
                *[pl.BlockSpec(memory_space=pl.ANY)] * len(deps),
            ],
            out_specs=[pl.BlockSpec((half, 1, SUB, SUB), lambda i, index, lags: (0, i, 0, 0))] * 2,
            scratch_shapes=[
                pltpu.VMEM((SUB, HALO + hours), jnp.bfloat16),
                pltpu.VMEM((2 * half * SUB, hours), jnp.bfloat16),
            ],
        ),
        out_shape=[out, out],
        compiler_params=pltpu.CompilerParams(vmem_limit_bytes=FEW),
        cost_estimate=pl.CostEstimate(
            flops=8 * half * count * SUB * SUB * hours,
            bytes_accessed=count * (4 * SUB * hours + 8 * half * SUB * SUB),
            transcendentals=0,
        ),
        name="pieces",
    )(index, lags, scaled, halo, partner, *deps)


def per_device(anomalies, lag_list, pair_plan):
    points, seg_hours = anomalies.shape
    n_grid, n_tm = lax.axis_size("grid"), lax.axis_size("tm")
    all_hours = seg_hours * n_tm
    blocks = anomalies.reshape(points // SUB, SUB, seg_hours)

    def along_tm(value, target):
        return lax.ppermute(value, "tm", [(i, target(i)) for i in range(n_tm)])

    def ring_near(i):
        return i - i % RING + ((i % RING) ^ 1)

    def ring_far(i):
        return i - i % RING + (RING - 1 - i % RING)

    def other_half(i):
        return (i + RING) % n_tm

    def along_grid(value, route):
        return lax.ppermute(value, "grid", [(i, route(i) % n_grid) for i in range(n_grid)])

    routes = (
        lambda i: i + 3 if i % 2 else i + 1,
        lambda i: i + 2,
        lambda i: i + 1 if i % 2 else i + 3,
    )
    back = (
        lambda i: i - 1 if i % 2 else i - 3,
        lambda i: i - 2,
        lambda i: i - 3 if i % 2 else i - 1,
    )
    even = lax.axis_index("grid") % 2 == 0
    plan = pair_plan[0]
    plans = (jnp.where(even, plan[2], plan[0]), plan[1], jnp.where(even, plan[0], plan[2]))
    wanted = jnp.concatenate([along_grid(one[:, 1], route) for one, route in zip(plans, back)])

    norm = norms(lax.all_to_all(local_sums(anomalies, n_tm), "tm", 0, 0), all_hours)

    me = lax.axis_index("tm")
    place, part = me % RING, me // RING
    near, far = place ^ 1, RING - 1 - place
    orders = (
        jnp.stack([place, far, near, RING - 1 - near]),
        jnp.stack([place, near, far, far ^ 1]),
    )
    parts = jnp.stack([part, 1 - part]) * RING
    lag_slots = [jnp.take(lag_list, (order[:, None] + parts[None, :]).reshape(-1)) for order in orders]
    divisor = (all_hours - lag_slots[0][0]).astype(jnp.float32)

    scaled, tail, *picked = scaled_parts(wanted, (8, 8, 4, 4), blocks, norm)
    halo = lax.ppermute(tail, "tm", [(i, i + 1) for i in range(n_tm - 1)])
    partners = [along_grid(one, routes[which]) for one, which in zip(picked, (0, 1, 2, 2))]

    def summed(which, partner, offset, first, count, deps):
        half = count // 2
        kept, ones, forwards, twos = [], [], [], []
        for order in range(2):
            start = first + order * half
            index = plans[which][start:start + half, 0]
            keep, send = pieces(
                index, lag_slots[order], scaled, halo, partner, start - offset, deps
            )
            kept.append(keep)
            ones.append(along_tm(send, (ring_near, ring_far)[order]))
        for order in range(2):
            forward = kept[order][2:] + ones[order][2:]
            forwards.append(forward)
            twos.append(along_tm(forward, (ring_far, ring_near)[order]))
        across = jnp.concatenate([kept[o][1] + ones[o][1] + twos[o][1] for o in range(2)])
        three = along_tm(across, other_half)
        mine = jnp.concatenate([kept[o][0] + ones[o][0] + twos[o][0] for o in range(2)])
        return (mine + three) / divisor, forwards, kept

    first, deps, _ = summed(0, partners[0], 0, 0, 8, [])
    second, _, deps = summed(1, partners[1], 0, 0, 8, deps)
    third, _, deps = summed(2, partners[2], 0, 0, 4, deps)
    fourth, _, _ = summed(2, partners[3], 4, 4, 4, deps)
    third = jnp.concatenate([third, fourth])
    rows = [jnp.where(even, third, first), second, jnp.where(even, first, third)]
    return jnp.stack(rows)[None, :, :, None]


def solution(mesh):
    in_specs = (P("grid", "tm"), P(), P("grid", None, None, None))
    out_specs = P("grid", None, None, "tm", None, None)
    return jax.shard_map(
        per_device, mesh=mesh, in_specs=in_specs, out_specs=out_specs, check_vma=False
    )
```

time: 299 us -> 239 us (0.80)
  the two profiles are of different devices: /device:TPU:34 before, /device:TPU:1 now
where the time goes in v2:
time: 239 us; the launch traced here: 235 us
  waiting for transfers between devices  131 us (55%)
  starting transfers between devices  48.8 us (20%)
  Pallas kernels  46 us (19%)
  local copies, waits for them, and re-layouts  4.54 us (2%)
  other arithmetic  4.25 us (2%)
    ppermute x20, waiting for transfers between devices, along_tm(): return lax.ppermute(value, 'tm', [(i, target(i)) for i in range(n_tm)])  65.9 us
    ppermute x7, waiting for transfers between devices, along_grid(): lax.ppermute(value, 'grid', [(i, route(i) % n_grid) for i in range(n_grid)])  42.1 us
    pallas_call x8, Pallas kernels, pieces(): pl.pallas_call(piece_kernel, grid_spec=pltpu.PrefetchScalarGridSpec(num_s...  30.4 us
    ppermute x7, starting transfers between devices, along_grid(): lax.ppermute(value, 'grid', [(i, route(i) % n_grid) for i in range(n_grid)])  26.5 us
    ppermute x1, waiting for transfers between devices, per_device(): halo = lax.ppermute(tail, 'tm', [(i, i + 1) for i in range(n_tm - 1)])  19.6 us
    ppermute x20, starting transfers between devices, along_tm(): return lax.ppermute(value, 'tm', [(i, target(i)) for i in range(n_tm)])  12.4 us
    pallas_call x1, Pallas kernels, scaled_parts(): pl.pallas_call(functools.partial(scale_kernel, counts), in_specs=[pl.Bloc...  8.9 us
    all_to_all x1, starting transfers between devices, per_device(): lax.all_to_all(local_sums(anomalies, n_tm), 'tm', 0, 0)  7.32 us
  transfers between devices with their start and end apart: 29, of which 14 were waited for; matrix products, arithmetic and copies ran while one was open for 2% of the time, Pallas kernels for 15%

profile of v2, /device:TPU:1, one launch (start us, length us, event | category | flops | bytes accessed | tf_op | source)
XLA Modules:
  0.0 234.9 jit_solution(9659916481686171240)
XLA Ops:
  0.7 5.2 %collective-permute-start.2 = (s32[8]{0:T(128)S(1)}, s32[8]{0:T(128)S(1)}, u32[]{:S(2)}, u32[]{:S(2)}) collective-permute-start(s32[8]{0:T(128)S(1)} %slice_bitcast_fusion.8), channel_id=1, source_target_pairs={{0,120},{8,112},{16,8},{24,0},{32,24},{40,16},{48,40},{56,32},{64,... | collective-permute-start | bytes 104 | tf_op jit(solution)/shard_map/ppermute | solution.py:224
  6.0 5.2 %local_sums.1 = f32[8,32,128]{2,1,0:T(8,128)} custom-call(f32[2048,1024]{1,0:T(8,128)} %x_ref.1), custom_call_target="tpu_custom_call" | custom-call | flops 6291456 | bytes 8388608 | tf_op jit(solution)/shard_map/local_sums/pallas_call | solution.py:38
  11.1 7.3 %all-to-all-start = ((f32[8,32,128]{2,1,0:T(8,128)}), f32[8,32,128]{2,1,0:T(8,128)S(1)}, u32[]{:S(2)}, u32[]{:S(2)}) async-start(f32[8,32,128]{2,1,0:T(8,128)} %local_sums.1), calls=%async_computation | async-start | bytes 262144 | tf_op jit(solution)/shard_map/all_to_all | solution.py:241
  19.1 2.3 collective-permute-done
  22.1 3.3 %all-to-all-done.sums_ref = f32[8,32,128]{2,1,0:T(8,128)S(1)} async-done(((f32[8,32,128]{2,1,0:T(8,128)}), f32[8,32,128]{2,1,0:T(8,128)S(1)}, u32[]{:S(2)}, u32[]{:S(2)}) %all-to-all-start) | async-done | bytes 131104 | tf_op jit(solution)/shard_map/all_to_all | solution.py:241
  27.6 8.9 %scaled_parts.1 = (bf16[16,128,1024]{2,1,0:T(8,128)(2,1)}, bf16[16,128,256]{2,1,0:T(8,128)(2,1)}, bf16[8,128,1024]{2,1,0:T(8,128)(2,1)}, bf16[8,128,1024]{2,1,0:...) custom-call(s32[24]{0:T(128)} %pad_add_fusion.1.index_ref, f32[16,128,1024]{2,1,0:T(8,128)} %bitcast.81, ...), custom_call_target="tpu_custom_call" | custom-call | flops 4194304 | bytes 20971520 | tf_op jit(solution)/shard_map/scaled_parts/pallas_call | solution.py:119
  37.5 2.5 %collective-permute-start.3 = (bf16[16,128,256]{2,1,0:T(8,128)(2,1)}, bf16[16,128,256]{2,1,0:T(8,128)(2,1)S(1)}, u32[]{:S(2)}, u32[]{:S(2)}) collective-permute-start(bf16[16,128,256]{2,1,0:T(8,128)(2,1)} %get-tuple-element.29), channel_id=1, source_target_pairs={{0,1},{1,2},{2,3},{3,4},{4,5},{5,6},{6,7},{8,9},{9,10},{10,11},{11... | collective-permute-start | bytes 3145736 | tf_op jit(solution)/shard_map/ppermute | solution.py:255
  42.0 19.6 %collective-permute-done.3.halo_ref = bf16[16,128,256]{2,1,0:T(8,128)(2,1)S(1)} collective-permute-done((bf16[16,128,256]{2,1,0:T(8,128)(2,1)}, bf16[16,128,256]{2,1,0:T(8,128)(2,1)S(1)}, u32[]{:S(2)}, u32[]{:S(2)}) %collective-permute-start.3) | collective-permute-done | bytes 1048608 | tf_op jit(solution)/shard_map/ppermute | solution.py:255
  61.6 2.2 copy-done.1
  63.8 4.9 %pieces.9 = (f32[4,4,128,128]{3,2,1,0:T(8,128)S(1)}, f32[4,4,128,128]{3,2,1,0:T(8,128)S(1)}) custom-call(s32[4]{0:T(128)S(1)} %get-tuple-element.77.index_ref, s32[8]{0:T(128)S(1)} %and_select_fusion.lag_ref, bf16[16,128,1024]{2,1,0:T(8,128)(2,1)S(1)} %copy-done.1, bf16[16,128,256]{2,1,0:T(8,128)(2,1)S(1)} %collective-permute-done.3.halo_ref, ...), custom_call_target="tpu_custom_call" | custom-call | flops 2147483648 | bytes 4194304 | tf_op jit(solution)/shard_map/pieces/pallas_call | solution.py:177
  68.7 2.6 %collective-permute-start.8 = (f32[4,4,128,128]{3,2,1,0:T(8,128)S(1)}, f32[4,4,128,128]{3,2,1,0:T(8,128)S(1)}, u32[]{:S(2)}, u32[]{:S(2)}) collective-permute-start(f32[4,4,128,128]{3,2,1,0:T(8,128)S(1)} %get-tuple-element.36), channel_id=1, source_target_pairs={{0,3},{1,2},{2,1},{3,0},{4,7},{5,6},{6,5},{7,4},{8,11},{9,10},{10,... | collective-permute-start | bytes 3145736 | tf_op jit(solution)/shard_map/ppermute | solution.py:212
  71.3 4.9 %pieces.8 = (f32[4,4,128,128]{3,2,1,0:T(8,128)S(1)}, f32[4,4,128,128]{3,2,1,0:T(8,128)S(1)}) custom-call(s32[4]{0:T(128)S(1)} %get-tuple-element.78.index_ref, s32[8]{0:T(128)S(1)} %and_select_fusion.1.lag_ref, bf16[16,128,1024]{2,1,0:T(8,128)(2,1)S(1)} %copy-done.1, bf16[16,128,256]{2,1,0:T(8,128)(2,1)S(1)} %collective-permute-done.3.halo_ref, ...), custom_call_target="tpu_custom_call" | custom-call | flops 2147483648 | bytes 4194304 | tf_op jit(solution)/shard_map/pieces/pallas_call | solution.py:177
  76.4 19.5 %collective-permute-start.4 = (bf16[4,128,1024]{2,1,0:T(8,128)(2,1)S(1)}, bf16[4,128,1024]{2,1,0:T(8,128)(2,1)S(1)}, u32[]{:S(2)}, u32[]{:S(2)}) collective-permute-start(bf16[4,128,1024]{2,1,0:T(8,128)(2,1)S(1)} %copy-done.5), channel_id=1, source_target_pairs={{0,24},{8,16},{16,40},{24,32},{32,56},{40,48},{48,72},{56,64},{64,... | collective-permute-start | bytes 3145736 | tf_op jit(solution)/shard_map/ppermute | solution.py:224
  96.5 2.0 collective-permute-done.7
  99.4 21.4 %collective-permute-done.5.b_ref = bf16[8,128,1024]{2,1,0:T(8,128)(2,1)S(1)} collective-permute-done((bf16[8,128,1024]{2,1,0:T(8,128)(2,1)}, bf16[8,128,1024]{2,1,0:T(8,128)(2,1)S(1)}, u32[]{:S(2)}, u32[]{:S(2)}) %collective-permute-start.5) | collective-permute-done | bytes 2097184 | tf_op jit(solution)/shard_map/ppermute | solution.py:224
  120.8 4.9 %pieces.11 = (f32[4,4,128,128]{3,2,1,0:T(8,128)S(1)}, f32[4,4,128,128]{3,2,1,0:T(8,128)S(1)}) custom-call(s32[4]{0:T(128)S(1)} %get-tuple-element.75.index_ref, s32[8]{0:T(128)S(1)} %and_select_fusion.lag_ref, bf16[16,128,1024]{2,1,0:T(8,128)(2,1)S(1)} %copy-done.2, bf16[16,128,256]{2,1,0:T(8,128)(2,1)S(1)} %collective-permute-done.3.halo_ref, ...), custom_call_target="tpu_custom_call" | custom-call | flops 2147483648 | bytes 4194304 | tf_op jit(solution)/shard_map/pieces/pallas_call | solution.py:177
  125.7 4.9 %pieces.10 = (f32[4,4,128,128]{3,2,1,0:T(8,128)S(1)}, f32[4,4,128,128]{3,2,1,0:T(8,128)S(1)}) custom-call(s32[4]{0:T(128)S(1)} %get-tuple-element.76.index_ref, s32[8]{0:T(128)S(1)} %and_select_fusion.1.lag_ref, bf16[16,128,1024]{2,1,0:T(8,128)(2,1)S(1)} %copy-done.2, bf16[16,128,256]{2,1,0:T(8,128)(2,1)S(1)} %collective-permute-done.3.halo_ref, ...), custom_call_target="tpu_custom_call" | custom-call | flops 2147483648 | bytes 4194304 | tf_op jit(solution)/shard_map/pieces/pallas_call | solution.py:177
  130.5 1.8 collective-permute-done.4.b_ref
  132.3 2.7 %pieces.13 = (f32[4,2,128,128]{3,2,1,0:T(8,128)S(1)}, f32[4,2,128,128]{3,2,1,0:T(8,128)S(1)}) custom-call(s32[2]{0:T(128)S(1)} %get-tuple-element.73.index_ref, s32[8]{0:T(128)S(1)} %and_select_fusion.lag_ref, bf16[16,128,1024]{2,1,0:T(8,128)(2,1)S(1)} %copy-done.2, bf16[16,128,256]{2,1,0:T(8,128)(2,1)S(1)} %collective-permute-done.3.halo_ref, ...), custom_call_target="tpu_custom_call" | custom-call | flops 1073741824 | bytes 2097152 | tf_op jit(solution)/shard_map/pieces/pallas_call | solution.py:177
  135.1 2.7 %pieces.12 = (f32[4,2,128,128]{3,2,1,0:T(8,128)S(1)}, f32[4,2,128,128]{3,2,1,0:T(8,128)S(1)}) custom-call(s32[2]{0:T(128)S(1)} %get-tuple-element.74.index_ref, s32[8]{0:T(128)S(1)} %and_select_fusion.1.lag_ref, bf16[16,128,1024]{2,1,0:T(8,128)(2,1)S(1)} %copy-done.2, bf16[16,128,256]{2,1,0:T(8,128)(2,1)S(1)} %collective-permute-done.3.halo_ref, ...), custom_call_target="tpu_custom_call" | custom-call | flops 1073741824 | bytes 2097152 | tf_op jit(solution)/shard_map/pieces/pallas_call | solution.py:177
  138.2 16.6 %collective-permute-done.14.b_ref = bf16[4,128,1024]{2,1,0:T(8,128)(2,1)S(1)} collective-permute-done((bf16[4,128,1024]{2,1,0:T(8,128)(2,1)S(1)}, bf16[4,128,1024]{2,1,0:T(8,128)(2,1)S(1)}, u32[]{:S(2)}, u32[]{:S(2)}) %collective-permute-start.14) | collective-permute-done | bytes 1048608 | tf_op jit(solution)/shard_map/ppermute | solution.py:224
  154.8 2.7 %pieces.14 = (f32[4,2,128,128]{3,2,1,0:T(8,128)S(1)}, f32[4,2,128,128]{3,2,1,0:T(8,128)S(1)}) custom-call(s32[2]{0:T(128)S(1)} %get-tuple-element.71.index_ref, s32[8]{0:T(128)S(1)} %and_select_fusion.1.lag_ref, bf16[16,128,1024]{2,1,0:T(8,128)(2,1)S(1)} %copy-done.2, bf16[16,128,256]{2,1,0:T(8,128)(2,1)S(1)} %collective-permute-done.3.halo_ref, ...), custom_call_target="tpu_custom_call" | custom-call | flops 1073741824 | bytes 2097152 | tf_op jit(solution)/shard_map/pieces/pallas_call | solution.py:177
  157.6 2.7 %pieces.15 = (f32[4,2,128,128]{3,2,1,0:T(8,128)S(1)}, f32[4,2,128,128]{3,2,1,0:T(8,128)S(1)}) custom-call(s32[2]{0:T(128)S(1)} %get-tuple-element.72.index_ref, s32[8]{0:T(128)S(1)} %and_select_fusion.lag_ref, bf16[16,128,1024]{2,1,0:T(8,128)(2,1)S(1)} %copy-done.2, bf16[16,128,256]{2,1,0:T(8,128)(2,1)S(1)} %collective-permute-done.3.halo_ref, ...), custom_call_target="tpu_custom_call" | custom-call | flops 1073741824 | bytes 2097152 | tf_op jit(solution)/shard_map/pieces/pallas_call | solution.py:177
  160.6 2.7 %collective-permute-start.25 = (f32[4,4,128,128]{3,2,1,0:T(8,128)S(1)}, f32[4,4,128,128]{3,2,1,0:T(8,128)S(1)}, u32[]{:S(2)}, u32[]{:S(2)}) collective-permute-start(f32[4,4,128,128]{3,2,1,0:T(8,128)S(1)} %get-tuple-element.49), channel_id=1, source_target_pairs={{0,3},{1,2},{2,1},{3,0},{4,7},{5,6},{6,5},{7,4},{8,11},{9,10},{10,... | collective-permute-start | bytes 3145736 | tf_op jit(solution)/shard_map/ppermute | solution.py:212
  164.0 5.3 %collective-permute-done.15 = f32[4,2,128,128]{3,2,1,0:T(8,128)S(1)} collective-permute-done((f32[4,2,128,128]{3,2,1,0:T(8,128)S(1)}, f32[4,2,128,128]{3,2,1,0:T(8,128)S(1)}, u32[]{:S(2)}, u32[]{:S(2)}) %collective-permute-start.15) | collective-permute-done | bytes 524320 | tf_op jit(solution)/shard_map/ppermute | solution.py:212
  169.6 3.7 %collective-permute-done.17 = f32[4,2,128,128]{3,2,1,0:T(8,128)S(1)} collective-permute-done((f32[4,2,128,128]{3,2,1,0:T(8,128)S(1)}, f32[4,2,128,128]{3,2,1,0:T(8,128)S(1)}, u32[]{:S(2)}, u32[]{:S(2)}) %collective-permute-start.17) | collective-permute-done | bytes 524320 | tf_op jit(solution)/shard_map/ppermute | solution.py:212
  173.4 24.0 %collective-permute-done.12 = f32[2,2,128,128]{3,2,1,0:T(8,128)S(1)} collective-permute-done((f32[2,2,128,128]{3,2,1,0:T(8,128)S(1)}, f32[2,2,128,128]{3,2,1,0:T(8,128)S(1)}, u32[]{:S(2)}, u32[]{:S(2)}) %collective-permute-start.12) | collective-permute-done | bytes 262176 | tf_op jit(solution)/shard_map/ppermute | solution.py:212
  197.4 4.0 %collective-permute-done.10 = f32[2,2,128,128]{3,2,1,0:T(8,128)S(1)} collective-permute-done((f32[2,2,128,128]{3,2,1,0:T(8,128)S(1)}, f32[2,2,128,128]{3,2,1,0:T(8,128)S(1)}, u32[]{:S(2)}, u32[]{:S(2)}) %collective-permute-start.10) | collective-permute-done | bytes 262176 | tf_op jit(solution)/shard_map/ppermute | solution.py:212
  201.5 5.5 %collective-permute-done.16 = f32[2,2,128,128]{3,2,1,0:T(8,128)S(1)} collective-permute-done((f32[2,2,128,128]{3,2,1,0:T(8,128)S(1)}, f32[2,2,128,128]{3,2,1,0:T(8,128)S(1)}, u32[]{:S(2)}, u32[]{:S(2)}) %collective-permute-start.16) | collective-permute-done | bytes 262176 | tf_op jit(solution)/shard_map/ppermute | solution.py:212
  208.3 3.0 %collective-permute-start.19 = (f32[4,128,128]{2,1,0:T(8,128)S(1)}, f32[4,128,128]{2,1,0:T(8,128)S(1)}, u32[]{:S(2)}, u32[]{:S(2)}) collective-permute-start(f32[4,128,128]{2,1,0:T(8,128)S(1)} %pad_maximum_fusion.4), channel_id=1, source_target_pairs={{0,4},{1,5},{2,6},{3,7},{4,0},{5,1},{6,2},{7,3},{8,12},{9,13},{10,... | collective-permute-start | bytes 786440 | tf_op jit(solution)/shard_map/ppermute | solution.py:212
  211.4 9.7 %collective-permute-done.26 = f32[2,4,128,128]{3,2,1,0:T(8,128)S(1)} collective-permute-done((f32[2,4,128,128]{3,2,1,0:T(8,128)S(1)}, f32[2,4,128,128]{3,2,1,0:T(8,128)S(1)}, u32[]{:S(2)}, u32[]{:S(2)}) %collective-permute-start.26) | collective-permute-done | bytes 524320 | tf_op jit(solution)/shard_map/ppermute | solution.py:212
  222.0 11.5 %collective-permute-done.27 = f32[8,128,128]{2,1,0:T(8,128)S(1)} collective-permute-done((f32[8,128,128]{2,1,0:T(8,128)S(1)}, f32[8,128,128]{2,1,0:T(8,128)S(1)}, u32[]{:S(2)}, u32[]{:S(2)}) %collective-permute-start.27) | collective-permute-done | bytes 524320 | tf_op jit(solution)/shard_map/ppermute | solution.py:212
  (95 shorter events, 14.0 us)
Async XLA Ops:
  0.0 40.1 %copy-start = (s32[8]{0:T(128)S(1)}, s32[8]{0:T(128)}, u32[]{:S(2)}) copy-start(s32[8]{0:T(128)} %param.6) | copy-start | bytes 100
  0.7 18.4 %collective-permute-start.2 = (s32[8]{0:T(128)S(1)}, s32[8]{0:T(128)S(1)}, u32[]{:S(2)}, u32[]{:S(2)}) collective-permute-start(s32[8]{0:T(128)S(1)} %slice_bitcast_fusion.8), channel_id=1, source_target_pairs={{0,120},{8,112},{16,8},{24,0},{32,24},{40,16},{48,40},{56,32},{64,... | collective-permute-start | bytes 104 | tf_op jit(solution)/shard_map/ppermute | solution.py:224
  6.0 13.1 %collective-permute-start.1 = (s32[8]{0:T(128)S(1)}, s32[8]{0:T(128)S(1)}, u32[]{:S(2)}, u32[]{:S(2)}) collective-permute-start(s32[8]{0:T(128)S(1)} %slice_bitcast_fusion.9), channel_id=1, source_target_pairs={{0,112},{8,120},{16,0},{24,8},{32,16},{40,24},{48,32},{56,40},{64,... | collective-permute-start | bytes 104 | tf_op jit(solution)/shard_map/ppermute | solution.py:224
  11.1 14.3 %all-to-all-start = ((f32[8,32,128]{2,1,0:T(8,128)}), f32[8,32,128]{2,1,0:T(8,128)S(1)}, u32[]{:S(2)}, u32[]{:S(2)}) async-start(f32[8,32,128]{2,1,0:T(8,128)} %local_sums.1), calls=%async_computation | async-start | bytes 262144 | tf_op jit(solution)/shard_map/all_to_all | solution.py:241
  18.4 3.0 %collective-permute-start = (s32[8]{0:T(128)S(1)}, s32[8]{0:T(128)S(1)}, u32[]{:S(2)}, u32[]{:S(2)}) collective-permute-start(s32[8]{0:T(128)S(1)} %slice_bitcast_fusion.10), channel_id=1, source_target_pairs={{0,104},{8,0},{16,120},{24,16},{32,8},{40,32},{48,24},{56,48},{64,... | collective-permute-start | bytes 104 | tf_op jit(solution)/shard_map/ppermute | solution.py:224
  36.5 25.1 %collective-permute-start.6 = (bf16[8,128,1024]{2,1,0:T(8,128)(2,1)}, bf16[8,128,1024]{2,1,0:T(8,128)(2,1)S(1)}, u32[]{:S(2)}, u32[]{:S(2)}) collective-permute-start(bf16[8,128,1024]{2,1,0:T(8,128)(2,1)} %get-tuple-element.32), channel_id=1, source_target_pairs={{0,8},{8,32},{16,24},{24,48},{32,40},{40,64},{48,56},{56,80},{64,7... | collective-permute-start | bytes 6291464 | tf_op jit(solution)/shard_map/ppermute | solution.py:224
  37.5 24.1 %collective-permute-start.3 = (bf16[16,128,256]{2,1,0:T(8,128)(2,1)}, bf16[16,128,256]{2,1,0:T(8,128)(2,1)S(1)}, u32[]{:S(2)}, u32[]{:S(2)}) collective-permute-start(bf16[16,128,256]{2,1,0:T(8,128)(2,1)} %get-tuple-element.29), channel_id=1, source_target_pairs={{0,1},{1,2},{2,3},{3,4},{4,5},{5,6},{6,7},{8,9},{9,10},{10,11},{11... | collective-permute-start | bytes 3145736 | tf_op jit(solution)/shard_map/ppermute | solution.py:255
  41.5 79.3 %collective-permute-start.5 = (bf16[8,128,1024]{2,1,0:T(8,128)(2,1)}, bf16[8,128,1024]{2,1,0:T(8,128)(2,1)S(1)}, u32[]{:S(2)}, u32[]{:S(2)}) collective-permute-start(bf16[8,128,1024]{2,1,0:T(8,128)(2,1)} %get-tuple-element.31), channel_id=1, source_target_pairs={{0,16},{8,24},{16,32},{24,40},{32,48},{40,56},{48,64},{56,72},{64,... | collective-permute-start | bytes 6291464 | tf_op jit(solution)/shard_map/ppermute | solution.py:224
  68.7 27.3 %collective-permute-start.8 = (f32[4,4,128,128]{3,2,1,0:T(8,128)S(1)}, f32[4,4,128,128]{3,2,1,0:T(8,128)S(1)}, u32[]{:S(2)}, u32[]{:S(2)}) collective-permute-start(f32[4,4,128,128]{3,2,1,0:T(8,128)S(1)} %get-tuple-element.36), channel_id=1, source_target_pairs={{0,3},{1,2},{2,1},{3,0},{4,7},{5,6},{6,5},{7,4},{8,11},{9,10},{10,... | collective-permute-start | bytes 3145736 | tf_op jit(solution)/shard_map/ppermute | solution.py:212
  71.3 24.7 %copy-start.4 = (bf16[4,128,1024]{2,1,0:T(8,128)(2,1)S(1)}, bf16[4,128,1024]{2,1,0:T(8,128)(2,1)}, u32[]{:S(2)}) copy-start(bf16[4,128,1024]{2,1,0:T(8,128)(2,1)} %get-tuple-element.43) | copy-start | bytes 3145732
  71.3 49.5 %copy-start.2 = (bf16[16,128,1024]{2,1,0:T(8,128)(2,1)S(1)}, bf16[16,128,1024]{2,1,0:T(8,128)(2,1)}, u32[]{:S(2)}) copy-start(bf16[16,128,1024]{2,1,0:T(8,128)(2,1)} %get-tuple-element.28.a_ref) | copy-start | bytes 12582916
  76.2 22.4 %collective-permute-start.7 = (f32[4,4,128,128]{3,2,1,0:T(8,128)S(1)}, f32[4,4,128,128]{3,2,1,0:T(8,128)S(1)}, u32[]{:S(2)}, u32[]{:S(2)}) collective-permute-start(f32[4,4,128,128]{3,2,1,0:T(8,128)S(1)} %get-tuple-element.34), channel_id=1, source_target_pairs={{0,1},{1,0},{2,3},{3,2},{4,5},{5,4},{6,7},{7,6},{8,9},{9,8},{10,11... | collective-permute-start | bytes 3145736 | tf_op jit(solution)/shard_map/ppermute | solution.py:212
  76.4 55.9 %collective-permute-start.4 = (bf16[4,128,1024]{2,1,0:T(8,128)(2,1)S(1)}, bf16[4,128,1024]{2,1,0:T(8,128)(2,1)S(1)}, u32[]{:S(2)}, u32[]{:S(2)}) collective-permute-start(bf16[4,128,1024]{2,1,0:T(8,128)(2,1)S(1)} %copy-done.5), channel_id=1, source_target_pairs={{0,24},{8,16},{16,40},{24,32},{32,56},{40,48},{48,72},{56,64},{64,... | collective-permute-start | bytes 3145736 | tf_op jit(solution)/shard_map/ppermute | solution.py:224
  96.0 58.8 %collective-permute-start.14 = (bf16[4,128,1024]{2,1,0:T(8,128)(2,1)S(1)}, bf16[4,128,1024]{2,1,0:T(8,128)(2,1)S(1)}, u32[]{:S(2)}, u32[]{:S(2)}) collective-permute-start(bf16[4,128,1024]{2,1,0:T(8,128)(2,1)S(1)} %copy-done.4), channel_id=1, source_target_pairs={{0,24},{8,16},{16,40},{24,32},{32,56},{40,48},{48,72},{56,64},{64,... | collective-permute-start | bytes 3145736 | tf_op jit(solution)/shard_map/ppermute | solution.py:224
  96.0 64.3 %collective-permute-start.21 = (f32[2,4,128,128]{3,2,1,0:T(8,128)S(1)}, f32[2,4,128,128]{3,2,1,0:T(8,128)S(1)}, u32[]{:S(2)}, u32[]{:S(2)}) collective-permute-start(f32[2,4,128,128]{3,2,1,0:T(8,128)S(1)} %slice_add_fusion.2.refs_1_), channel_id=1, source_target_pairs={{0,1},{1,0},{2,3},{3,2},{4,5},{5,4},{6,7},{7,6},{8,9},{9,8},{10,11... | collective-permute-start | bytes 1572872 | tf_op jit(solution)/shard_map/ppermute | solution.py:212
  98.6 61.9 %collective-permute-start.20 = (f32[2,4,128,128]{3,2,1,0:T(8,128)S(1)}, f32[2,4,128,128]{3,2,1,0:T(8,128)S(1)}, u32[]{:S(2)}, u32[]{:S(2)}) collective-permute-start(f32[2,4,128,128]{3,2,1,0:T(8,128)S(1)} %slice_add_fusion.3.refs_0_), channel_id=1, source_target_pairs={{0,3},{1,2},{2,1},{3,0},{4,7},{5,6},{6,5},{7,4},{8,11},{9,10},{10,... | collective-permute-start | bytes 1572872 | tf_op jit(solution)/shard_map/ppermute | solution.py:212
  135.0 28.4 %collective-permute-start.11 = (f32[4,2,128,128]{3,2,1,0:T(8,128)S(1)}, f32[4,2,128,128]{3,2,1,0:T(8,128)S(1)}, u32[]{:S(2)}, u32[]{:S(2)}) collective-permute-start(f32[4,2,128,128]{3,2,1,0:T(8,128)S(1)} %get-tuple-element.42), channel_id=1, source_target_pairs={{0,3},{1,2},{2,1},{3,0},{4,7},{5,6},{6,5},{7,4},{8,11},{9,10},{10,... | collective-permute-start | bytes 1572872 | tf_op jit(solution)/shard_map/ppermute | solution.py:212
  137.9 25.9 %collective-permute-start.9 = (f32[4,2,128,128]{3,2,1,0:T(8,128)S(1)}, f32[4,2,128,128]{3,2,1,0:T(8,128)S(1)}, u32[]{:S(2)}, u32[]{:S(2)}) collective-permute-start(f32[4,2,128,128]{3,2,1,0:T(8,128)S(1)} %get-tuple-element.40), channel_id=1, source_target_pairs={{0,1},{1,0},{2,3},{3,2},{4,5},{5,4},{6,7},{7,6},{8,9},{9,8},{10,11... | collective-permute-start | bytes 1572872 | tf_op jit(solution)/shard_map/ppermute | solution.py:212
  157.5 11.8 %collective-permute-start.15 = (f32[4,2,128,128]{3,2,1,0:T(8,128)S(1)}, f32[4,2,128,128]{3,2,1,0:T(8,128)S(1)}, u32[]{:S(2)}, u32[]{:S(2)}) collective-permute-start(f32[4,2,128,128]{3,2,1,0:T(8,128)S(1)} %get-tuple-element.45), channel_id=1, source_target_pairs={{0,1},{1,0},{2,3},{3,2},{4,5},{5,4},{6,7},{7,6},{8,9},{9,8},{10,11... | collective-permute-start | bytes 1572872 | tf_op jit(solution)/shard_map/ppermute | solution.py:212
  160.4 13.0 %collective-permute-start.17 = (f32[4,2,128,128]{3,2,1,0:T(8,128)S(1)}, f32[4,2,128,128]{3,2,1,0:T(8,128)S(1)}, u32[]{:S(2)}, u32[]{:S(2)}) collective-permute-start(f32[4,2,128,128]{3,2,1,0:T(8,128)S(1)} %get-tuple-element.47), channel_id=1, source_target_pairs={{0,3},{1,2},{2,1},{3,0},{4,7},{5,6},{6,5},{7,4},{8,11},{9,10},{10,... | collective-permute-start | bytes 1572872 | tf_op jit(solution)/shard_map/ppermute | solution.py:212
  160.6 46.5 %collective-permute-start.25 = (f32[4,4,128,128]{3,2,1,0:T(8,128)S(1)}, f32[4,4,128,128]{3,2,1,0:T(8,128)S(1)}, u32[]{:S(2)}, u32[]{:S(2)}) collective-permute-start(f32[4,4,128,128]{3,2,1,0:T(8,128)S(1)} %get-tuple-element.49), channel_id=1, source_target_pairs={{0,3},{1,2},{2,1},{3,0},{4,7},{5,6},{6,5},{7,4},{8,11},{9,10},{10,... | collective-permute-start | bytes 3145736 | tf_op jit(solution)/shard_map/ppermute | solution.py:212
  163.4 43.9 %collective-permute-start.23 = (f32[4,4,128,128]{3,2,1,0:T(8,128)S(1)}, f32[4,4,128,128]{3,2,1,0:T(8,128)S(1)}, u32[]{:S(2)}, u32[]{:S(2)}) collective-permute-start(f32[4,4,128,128]{3,2,1,0:T(8,128)S(1)} %get-tuple-element.48), channel_id=1, source_target_pairs={{0,1},{1,0},{2,3},{3,2},{4,5},{5,4},{6,7},{7,6},{8,9},{9,8},{10,11... | collective-permute-start | bytes 3145736 | tf_op jit(solution)/shard_map/ppermute | solution.py:212
  163.8 58.1 %collective-permute-start.22 = (f32[8,128,128]{2,1,0:T(8,128)S(1)}, f32[8,128,128]{2,1,0:T(8,128)S(1)}, u32[]{:S(2)}, u32[]{:S(2)}) collective-permute-start(f32[8,128,128]{2,1,0:T(8,128)S(1)} %pad_maximum_fusion.1), channel_id=1, source_target_pairs={{0,4},{1,5},{2,6},{3,7},{4,0},{5,1},{6,2},{7,3},{8,12},{9,13},{10,... | collective-permute-start | bytes 1572872 | tf_op jit(solution)/shard_map/ppermute | solution.py:212
  169.3 28.1 %collective-permute-start.12 = (f32[2,2,128,128]{3,2,1,0:T(8,128)S(1)}, f32[2,2,128,128]{3,2,1,0:T(8,128)S(1)}, u32[]{:S(2)}, u32[]{:S(2)}) collective-permute-start(f32[2,2,128,128]{3,2,1,0:T(8,128)S(1)} %slice_add_fusion.22), channel_id=1, source_target_pairs={{0,1},{1,0},{2,3},{3,2},{4,5},{5,4},{6,7},{7,6},{8,9},{9,8},{10,11... | collective-permute-start | bytes 786440 | tf_op jit(solution)/shard_map/ppermute | solution.py:212
  173.3 28.1 %collective-permute-start.10 = (f32[2,2,128,128]{3,2,1,0:T(8,128)S(1)}, f32[2,2,128,128]{3,2,1,0:T(8,128)S(1)}, u32[]{:S(2)}, u32[]{:S(2)}) collective-permute-start(f32[2,2,128,128]{3,2,1,0:T(8,128)S(1)} %slice_add_fusion.23), channel_id=1, source_target_pairs={{0,3},{1,2},{2,1},{3,0},{4,7},{5,6},{6,5},{7,4},{8,11},{9,10},{10,... | collective-permute-start | bytes 786440 | tf_op jit(solution)/shard_map/ppermute | solution.py:212
  197.4 9.7 %collective-permute-start.16 = (f32[2,2,128,128]{3,2,1,0:T(8,128)S(1)}, f32[2,2,128,128]{3,2,1,0:T(8,128)S(1)}, u32[]{:S(2)}, u32[]{:S(2)}) collective-permute-start(f32[2,2,128,128]{3,2,1,0:T(8,128)S(1)} %slice_add_fusion.21), channel_id=1, source_target_pairs={{0,3},{1,2},{2,1},{3,0},{4,7},{5,6},{6,5},{7,4},{8,11},{9,10},{10,... | collective-permute-start | bytes 786440 | tf_op jit(solution)/shard_map/ppermute | solution.py:212
  201.4 6.8 %collective-permute-start.18 = (f32[2,2,128,128]{3,2,1,0:T(8,128)S(1)}, f32[2,2,128,128]{3,2,1,0:T(8,128)S(1)}, u32[]{:S(2)}, u32[]{:S(2)}) collective-permute-start(f32[2,2,128,128]{3,2,1,0:T(8,128)S(1)} %slice_add_fusion.20), channel_id=1, source_target_pairs={{0,1},{1,0},{2,3},{3,2},{4,5},{5,4},{6,7},{7,6},{8,9},{9,8},{10,11... | collective-permute-start | bytes 786440 | tf_op jit(solution)/shard_map/ppermute | solution.py:212
  207.0 14.8 %collective-permute-start.13 = (f32[4,128,128]{2,1,0:T(8,128)S(1)}, f32[4,128,128]{2,1,0:T(8,128)S(1)}, u32[]{:S(2)}, u32[]{:S(2)}) collective-permute-start(f32[4,128,128]{2,1,0:T(8,128)S(1)} %pad_maximum_fusion.3), channel_id=1, source_target_pairs={{0,4},{1,5},{2,6},{3,7},{4,0},{5,1},{6,2},{7,3},{8,12},{9,13},{10,... | collective-permute-start | bytes 786440 | tf_op jit(solution)/shard_map/ppermute | solution.py:212
  207.2 13.9 %collective-permute-start.26 = (f32[2,4,128,128]{3,2,1,0:T(8,128)S(1)}, f32[2,4,128,128]{3,2,1,0:T(8,128)S(1)}, u32[]{:S(2)}, u32[]{:S(2)}) collective-permute-start(f32[2,4,128,128]{3,2,1,0:T(8,128)S(1)} %slice_add_fusion), channel_id=1, source_target_pairs={{0,1},{1,0},{2,3},{3,2},{4,5},{5,4},{6,7},{7,6},{8,9},{9,8},{10,11... | collective-permute-start | bytes 1572872 | tf_op jit(solution)/shard_map/ppermute | solution.py:212
  207.3 13.9 %collective-permute-start.24 = (f32[2,4,128,128]{3,2,1,0:T(8,128)S(1)}, f32[2,4,128,128]{3,2,1,0:T(8,128)S(1)}, u32[]{:S(2)}, u32[]{:S(2)}) collective-permute-start(f32[2,4,128,128]{3,2,1,0:T(8,128)S(1)} %slice_add_fusion.1), channel_id=1, source_target_pairs={{0,3},{1,2},{2,1},{3,0},{4,7},{5,6},{6,5},{7,4},{8,11},{9,10},{10,... | collective-permute-start | bytes 1572872 | tf_op jit(solution)/shard_map/ppermute | solution.py:212
  208.3 13.5 %collective-permute-start.19 = (f32[4,128,128]{2,1,0:T(8,128)S(1)}, f32[4,128,128]{2,1,0:T(8,128)S(1)}, u32[]{:S(2)}, u32[]{:S(2)}) collective-permute-start(f32[4,128,128]{2,1,0:T(8,128)S(1)} %pad_maximum_fusion.4), channel_id=1, source_target_pairs={{0,4},{1,5},{2,6},{3,7},{4,0},{5,1},{6,2},{7,3},{8,12},{9,13},{10,... | collective-permute-start | bytes 786440 | tf_op jit(solution)/shard_map/ppermute | solution.py:212
  221.3 12.2 %collective-permute-start.27 = (f32[8,128,128]{2,1,0:T(8,128)S(1)}, f32[8,128,128]{2,1,0:T(8,128)S(1)}, u32[]{:S(2)}, u32[]{:S(2)}) collective-permute-start(f32[8,128,128]{2,1,0:T(8,128)S(1)} %pad_maximum_fusion.2), channel_id=1, source_target_pairs={{0,4},{1,5},{2,6},{3,7},{4,0},{5,1},{6,2},{7,3},{8,12},{9,13},{10,... | collective-permute-start | bytes 1572872 | tf_op jit(solution)/shard_map/ppermute | solution.py:212
  (3 other events, 8.0 us)

commit v3 on v2

--- a/solution.py
+++ b/solution.py
@@ -133,7 +133,7 @@
         ],
         compiler_params=pltpu.CompilerParams(vmem_limit_bytes=MANY),
         cost_estimate=pl.CostEstimate(
-            flops=2 * subs * SUB * hours, bytes_accessed=10 * subs * SUB * hours, transcendentals=0
+            flops=1, bytes_accessed=1, transcendentals=0
         ),
         name="scaled_parts",
     )(index, blocks, norm)
@@ -171,9 +171,10 @@
 
 
 def pieces(index, lags, scaled, halo, partner, start, deps):
-    count, hours = index.shape[0], partner.shape[2]
+    count, hours = index.shape[0], scaled.shape[2]
     half = lags.shape[0] // 2
     out = jax.ShapeDtypeStruct((half, count, SUB, SUB), jnp.float32)
+
     return pl.pallas_call(
         piece_kernel,
         grid_spec=pltpu.PrefetchScalarGridSpec(
@@ -193,13 +194,47 @@
         ),
         out_shape=[out, out],
         compiler_params=pltpu.CompilerParams(vmem_limit_bytes=FEW),
-        cost_estimate=pl.CostEstimate(
-            flops=8 * half * count * SUB * SUB * hours,
-            bytes_accessed=count * (4 * SUB * hours + 8 * half * SUB * SUB),
-            transcendentals=0,
-        ),
+        cost_estimate=pl.CostEstimate(flops=1, bytes_accessed=1, transcendentals=0),
         name="pieces",
     )(index, lags, scaled, halo, partner, *deps)
+
+
+def tile_call(kernel, name, count, inputs, outputs, scalars=(), deps=()):
+    def couple(place):
+        return pl.BlockSpec((2, 1, SUB, SUB), lambda i: (place, i, 0, 0))
+
+    return pl.pallas_call(
+        kernel,
+        grid=(count,),
+        in_specs=[
+            *[couple(place) for _, place in inputs],
+            *[pl.BlockSpec(memory_space=pltpu.SMEM)] * len(scalars),
+            *[pl.BlockSpec(memory_space=pl.ANY)] * len(deps),
+        ],
+        out_specs=[couple(0)] * outputs,
+        out_shape=[jax.ShapeDtypeStruct((2, count, SUB, SUB), jnp.float32)] * outputs,
+        compiler_params=pltpu.CompilerParams(vmem_limit_bytes=FEW),
+        cost_estimate=pl.CostEstimate(flops=1, bytes_accessed=1, transcendentals=0),
+        name=name,
+    )(*[array for array, _ in inputs], *scalars, *deps)
+
+
+def forward_kernel(*refs):
+    for order in range(2):
+        keep_ref, one_ref = refs[2 * order:2 * order + 2]
+        refs[order - 2][...] = keep_ref[...] + one_ref[...]
+
+
+def across_kernel(*refs):
+    for order in range(2):
+        keep_ref, one_ref, two_ref = refs[3 * order:3 * order + 3]
+        total = keep_ref[...] + one_ref[...] + two_ref[...]
+        refs[-2][order] = total[0]
+        refs[-1][order] = total[1]
+
+
+def final_kernel(mine_ref, three_ref, divisor_ref, *refs):
+    refs[-1][...] = (mine_ref[...] + three_ref[...]) / divisor_ref[0]
 
 
 def per_device(anomalies, lag_list, pair_plan):
@@ -251,36 +286,68 @@
     lag_slots = [jnp.take(lag_list, (order[:, None] + parts[None, :]).reshape(-1)) for order in orders]
     divisor = (all_hours - lag_slots[0][0]).astype(jnp.float32)
 
-    scaled, tail, *picked = scaled_parts(wanted, (8, 8, 4, 4), blocks, norm)
+    scaled, tail, *picked = scaled_parts(wanted, (8, 8, 8), blocks, norm)
     halo = lax.ppermute(tail, "tm", [(i, i + 1) for i in range(n_tm - 1)])
-    partners = [along_grid(one, routes[which]) for one, which in zip(picked, (0, 1, 2, 2))]
-
-    def summed(which, partner, offset, first, count, deps):
-        half = count // 2
-        kept, ones, forwards, twos = [], [], [], []
-        for order in range(2):
-            start = first + order * half
-            index = plans[which][start:start + half, 0]
-            keep, send = pieces(
-                index, lag_slots[order], scaled, halo, partner, start - offset, deps
-            )
-            kept.append(keep)
-            ones.append(along_tm(send, (ring_near, ring_far)[order]))
-        for order in range(2):
-            forward = kept[order][2:] + ones[order][2:]
-            forwards.append(forward)
-            twos.append(along_tm(forward, (ring_far, ring_near)[order]))
-        across = jnp.concatenate([kept[o][1] + ones[o][1] + twos[o][1] for o in range(2)])
-        three = along_tm(across, other_half)
-        mine = jnp.concatenate([kept[o][0] + ones[o][0] + twos[o][0] for o in range(2)])
-        return (mine + three) / divisor, forwards, kept
-
-    first, deps, _ = summed(0, partners[0], 0, 0, 8, [])
-    second, _, deps = summed(1, partners[1], 0, 0, 8, deps)
-    third, _, deps = summed(2, partners[2], 0, 0, 4, deps)
-    fourth, _, _ = summed(2, partners[3], 4, 4, 4, deps)
-    third = jnp.concatenate([third, fourth])
-    rows = [jnp.where(even, third, first), second, jnp.where(even, first, third)]
+    beside = along_grid(picked[0], routes[0])
+    halo, *picked = lax.optimization_barrier((halo, *picked[1:]))
+    over, last = [along_grid(one, route) for one, route in zip(picked, routes[1:])]
+    divisor = divisor.reshape(1)
+
+    recent = [scaled]
+
+    def step_one(groups):
+        group = []
+        for order, (which, first, count, partner, start) in enumerate(groups):
+            index = plans[which][first:first + count, 0]
+            keep, send = pieces(index, lag_slots[order], scaled, halo, partner, start, recent)
+            recent[:] = [keep]
+            group.append((keep, along_tm(send, (ring_near, ring_far)[order])))
+        return group
+
+    def step_two(group):
+        count = group[0][0].shape[1]
+        inputs = [(array, 1) for pair in group for array in pair]
+        forward = tile_call(forward_kernel, "forward", count, inputs, 2, deps=recent)
+        recent[:] = [forward[0]]
+        return [
+            (*group[order], along_tm(forward[order], (ring_far, ring_near)[order]))
+            for order in range(2)
+        ]
+
+    def step_three(group):
+        count = group[0][0].shape[1]
+        inputs = [(array, 0) for triple in group for array in triple]
+        mine, across = tile_call(across_kernel, "across", count, inputs, 2, deps=recent)
+        recent[:] = [mine]
+        return mine, along_tm(across, other_half)
+
+    def step_four(mine, three):
+        inputs = [(mine, 0), (three, 0)]
+        (out,) = tile_call(
+            final_kernel, "final", mine.shape[1], inputs, 1, scalars=[divisor], deps=recent
+        )
+        recent[:] = [out]
+        return out.reshape(-1, SUB, SUB)
+
+    a = step_one([(0, 0, 4, beside, 0), (0, 4, 4, beside, 4)])
+    a = step_two(a)
+    a = step_three(a)
+    b = step_one([(1, 0, 4, over, 0), (1, 4, 4, over, 4)])
+    b = step_two(b)
+    c = step_one([(2, 0, 2, last, 0), (2, 2, 2, last, 2)])
+    b = step_three(b)
+    d = step_one([(2, 4, 2, last, 4), (2, 6, 2, last, 6)])
+    a = step_four(*a)
+    c = step_two(c)
+    d = step_two(d)
+    b = step_four(*b)
+    c = step_three(c)
+    d = step_three(d)
+    c = step_four(*c)
+    d = step_four(*d)
+    middle = b
+    farthest = jnp.concatenate([c, d])
+    rows = [jnp.where(even, farthest, a), middle, jnp.where(even, a, farthest)]
     return jnp.stack(rows)[None, :, :, None]
 
 

time: 239 us -> 217 us (0.908); the launches traced: 235 us -> 216 us
  waiting for transfers between devices: 131 us -> 104 us
  Pallas kernels: 46 us -> 51.9 us
  starting transfers between devices: 48.8 us -> 52.1 us
    ppermute x7 -> x6, waiting for transfers between devices: 42.1 us -> 2.8 us  [along_grid(): lax.ppermute(value, 'grid', [(i, route(i) % n_grid) for i in range(n_grid)])]
    ppermute x20, starting transfers between devices: 12.4 us -> 32.8 us  [along_tm(): return lax.ppermute(value, 'tm', [(i, target(i)) for i in range(n_tm)])]
    ppermute x7 -> x6, starting transfers between devices: 26.5 us -> 9.58 us  [along_grid(): lax.ppermute(value, 'grid', [(i, route(i) % n_grid) for i in range(n_grid)])]
    ppermute x20, waiting for transfers between devices: 65.9 us -> 76.1 us  [along_tm(): return lax.ppermute(value, 'tm', [(i, target(i)) for i in range(n_tm)])]
    pallas_call x0 -> x12, Pallas kernels: none -> 3.88 us  [tile_call(): pl.pallas_call(kernel, grid=(count,), in_specs=[*[couple(place) for _, pl...]
  transfers between devices with their start and end apart: 29 -> 28, of which waited for: 14 -> 11; matrix products, arithmetic and copies ran while one was open for 2% -> 1% of each run, Pallas kernels for 15% -> 19%
where the time goes in v3:
time: 217 us; the launch traced here: 216 us
  waiting for transfers between devices  104 us (48%)
  starting transfers between devices  52.1 us (24%)
  Pallas kernels  51.9 us (24%)
  local copies, waits for them, and re-layouts  4.54 us (2%)
  other arithmetic  2.96 us (1%)
    ppermute x20, waiting for transfers between devices, along_tm(): return lax.ppermute(value, 'tm', [(i, target(i)) for i in range(n_tm)])  76.1 us
    ppermute x20, starting transfers between devices, along_tm(): return lax.ppermute(value, 'tm', [(i, target(i)) for i in range(n_tm)])  32.8 us
    pallas_call x8, Pallas kernels, pieces(): pl.pallas_call(piece_kernel, grid_spec=pltpu.PrefetchScalarGridSpec(num_s...  32.5 us
    ppermute x1, waiting for transfers between devices, per_device(): halo = lax.ppermute(tail, 'tm', [(i, i + 1) for i in range(n_tm - 1)])  21.9 us
    ppermute x6, starting transfers between devices, along_grid(): lax.ppermute(value, 'grid', [(i, route(i) % n_grid) for i in range(n_grid)])  9.58 us
    pallas_call x1, Pallas kernels, scaled_parts(): pl.pallas_call(functools.partial(scale_kernel, counts), in_specs=[pl.Bloc...  8.91 us
    all_to_all x1, starting transfers between devices, per_device(): lax.all_to_all(local_sums(anomalies, n_tm), 'tm', 0, 0)  7.21 us
    pallas_call x1, Pallas kernels, local_sums(): pl.pallas_call(sums_kernel, grid=(steps,), in_specs=[pl.BlockSpec((4 * SU...  5.15 us
  transfers between devices with their start and end apart: 28, of which 11 were waited for; matrix products, arithmetic and copies ran while one was open for 1% of the time, Pallas kernels for 19%

profile of v3, /device:TPU:1, one launch (start us, length us, event | category | flops | bytes accessed | tf_op | source)
XLA Modules:
  0.0 215.9 jit_solution(365318526722047089)
XLA Ops:
  2.2 3.9 %collective-permute-start.1 = (s32[8]{0:T(128)S(1)}, s32[8]{0:T(128)S(1)}, u32[]{:S(2)}, u32[]{:S(2)}) collective-permute-start(s32[8]{0:T(128)S(1)} %slice_bitcast_fusion.9), channel_id=1, source_target_pairs={{0,112},{8,120},{16,0},{24,8},{32,16},{40,24},{48,32},{56,40},{64,... | collective-permute-start | bytes 104 | tf_op jit(solution)/shard_map/ppermute | solution.py:259
  6.1 5.1 %local_sums.1 = f32[8,32,128]{2,1,0:T(8,128)} custom-call(f32[2048,1024]{1,0:T(8,128)} %x_ref.1), custom_call_target="tpu_custom_call" | custom-call | flops 6291456 | bytes 8388608 | tf_op jit(solution)/shard_map/local_sums/pallas_call | solution.py:38
  11.2 7.2 %all-to-all-start = ((f32[8,32,128]{2,1,0:T(8,128)}), f32[8,32,128]{2,1,0:T(8,128)S(1)}, u32[]{:S(2)}, u32[]{:S(2)}) async-start(f32[8,32,128]{2,1,0:T(8,128)} %local_sums.1), calls=%async_computation | async-start | bytes 262144 | tf_op jit(solution)/shard_map/all_to_all | solution.py:276
  18.7 2.8 %collective-permute-done.2 = s32[8]{0:T(128)S(1)} collective-permute-done((s32[8]{0:T(128)S(1)}, s32[8]{0:T(128)S(1)}, u32[]{:S(2)}, u32[]{:S(2)}) %collective-permute-start.2) | collective-permute-done | bytes 64 | tf_op jit(solution)/shard_map/ppermute | solution.py:259
  22.2 3.2 %all-to-all-done.sums_ref = f32[8,32,128]{2,1,0:T(8,128)S(1)} async-done(((f32[8,32,128]{2,1,0:T(8,128)}), f32[8,32,128]{2,1,0:T(8,128)S(1)}, u32[]{:S(2)}, u32[]{:S(2)}) %all-to-all-start) | async-done | bytes 131104 | tf_op jit(solution)/shard_map/all_to_all | solution.py:276
  27.6 8.9 %scaled_parts.1 = (bf16[16,128,1024]{2,1,0:T(8,128)(2,1)}, bf16[16,128,256]{2,1,0:T(8,128)(2,1)}, bf16[8,128,1024]{2,1,0:T(8,128)(2,1)}, bf16[8,128,1024]{2,1,0:T(8,128)(2,1)}, bf16[8,128,1024]{2,1,0:T(8,128)(2,1)}) custom-call(s32[24]{0:T(128)} %pad_add_fusion.1.index_ref, f32[16,128,1024]{2,1,0:T(8,128)} %bitcast.51, f32[2,16,128]{2,1,0:T(8,128)} %norms.1.norm_ref), custom_call_target="tpu_custom_call" | custom-call | flops 1 | bytes 1 | tf_op jit(solution)/shard_map/scaled_parts/pallas_call | solution.py:119
  36.5 2.8 %collective-permute-start.6 = (bf16[8,128,1024]{2,1,0:T(8,128)(2,1)}, bf16[8,128,1024]{2,1,0:T(8,128)(2,1)S(1)}, u32[]{:S(2)}, u32[]{:S(2)}) collective-permute-start(bf16[8,128,1024]{2,1,0:T(8,128)(2,1)} %get-tuple-element.53), channel_id=1, source_target_pairs={{0,8},{8,32},{16,24},{24,48},{32,40},{40,64},{48,56},{56,80},{64,7... | collective-permute-start | bytes 6291464 | tf_op jit(solution)/shard_map/ppermute | solution.py:259
  39.3 2.5 %collective-permute-start.3 = (bf16[16,128,256]{2,1,0:T(8,128)(2,1)}, bf16[16,128,256]{2,1,0:T(8,128)(2,1)S(1)}, u32[]{:S(2)}, u32[]{:S(2)}) collective-permute-start(bf16[16,128,256]{2,1,0:T(8,128)(2,1)} %get-tuple-element.47), channel_id=1, source_target_pairs={{0,1},{1,2},{2,3},{3,4},{4,5},{5,6},{6,7},{8,9},{9,10},{10,11},{11... | collective-permute-start | bytes 3145736 | tf_op jit(solution)/shard_map/ppermute | solution.py:290
  42.9 21.9 %collective-permute-done.3.halo_ref = bf16[16,128,256]{2,1,0:T(8,128)(2,1)S(1)} collective-permute-done((bf16[16,128,256]{2,1,0:T(8,128)(2,1)}, bf16[16,128,256]{2,1,0:T(8,128)(2,1)S(1)}, u32[]{:S(2)}, u32[]{:S(2)}) %collective-permute-start.3) | collective-permute-done | bytes 1048608 | tf_op jit(solution)/shard_map/ppermute | solution.py:290
  65.5 2.2 %copy-done.1 = bf16[16,128,1024]{2,1,0:T(8,128)(2,1)S(1)} copy-done((bf16[16,128,1024]{2,1,0:T(8,128)(2,1)S(1)}, bf16[16,128,1024]{2,1,0:T(8,128)(2,1)}, u32[]{:S(2)}) %copy-start.1) | copy-done | bytes 4194328
  67.7 4.9 %pieces.8 = (f32[4,4,128,128]{3,2,1,0:T(8,128)S(1)}, f32[4,4,128,128]{3,2,1,0:T(8,128)S(1)}) custom-call(s32[4]{0:T(128)S(1)} %get-tuple-element.98.index_ref, s32[8]{0:T(128)S(1)} %and_select_fusion.1.lag_ref, bf16[16,128,1024]{2,1,0:T(8,128)(2,1)S(1)} %copy-done.1, bf16[16,128,256]{2,1,0:T(8,128)(2,1)S(1)} %collective-permute-done.3.halo_ref, ...), custom_call_target="tpu_custom_call" | custom-call | flops 1 | bytes 1 | tf_op jit(solution)/shard_map/pieces/pallas_call | solution.py:178
  72.6 4.9 %pieces.9 = (f32[4,4,128,128]{3,2,1,0:T(8,128)S(1)}, f32[4,4,128,128]{3,2,1,0:T(8,128)S(1)}) custom-call(s32[4]{0:T(128)S(1)} %get-tuple-element.97.index_ref, s32[8]{0:T(128)S(1)} %and_select_fusion.lag_ref, bf16[16,128,1024]{2,1,0:T(8,128)(2,1)S(1)} %copy-done.1, bf16[16,128,256]{2,1,0:T(8,128)(2,1)S(1)} %collective-permute-done.3.halo_ref, ...), custom_call_target="tpu_custom_call" | custom-call | flops 1 | bytes 1 | tf_op jit(solution)/shard_map/pieces/pallas_call | solution.py:178
  77.5 2.3 %collective-permute-start.8 = (f32[4,4,128,128]{3,2,1,0:T(8,128)S(1)}, f32[4,4,128,128]{3,2,1,0:T(8,128)S(1)}, u32[]{:S(2)}, u32[]{:S(2)}) collective-permute-start(f32[4,4,128,128]{3,2,1,0:T(8,128)S(1)} %get-tuple-element.57), channel_id=1, source_target_pairs={{0,3},{1,2},{2,1},{3,0},{4,7},{5,6},{6,5},{7,4},{8,11},{9,10},{10,... | collective-permute-start | bytes 3145736 | tf_op jit(solution)/shard_map/ppermute | solution.py:247
  79.8 23.8 %collective-permute-done.8.refs_3_.refs_4_ = f32[4,4,128,128]{3,2,1,0:T(8,128)S(1)} collective-permute-done((f32[4,4,128,128]{3,2,1,0:T(8,128)S(1)}, f32[4,4,128,128]{3,2,1,0:T(8,128)S(1)}, u32[]{:S(2)}, u32[]{:S(2)}) %collective-permute-start.8) | collective-permute-done | bytes 1048608 | tf_op jit(solution)/shard_map/ppermute | solution.py:247
  107.3 9.1 %collective-permute-done.10.refs_5_ = f32[2,4,128,128]{3,2,1,0:T(8,128)S(1)} collective-permute-done((f32[2,4,128,128]{3,2,1,0:T(8,128)S(1)}, f32[2,4,128,128]{3,2,1,0:T(8,128)S(1)}, u32[]{:S(2)}, u32[]{:S(2)}) %collective-permute-start.10) | collective-permute-done | bytes 524320 | tf_op jit(solution)/shard_map/ppermute | solution.py:247
  116.4 1.6 collective-permute-done.9.refs_2_
  118.6 5.9 %pieces.10 = (f32[4,4,128,128]{3,2,1,0:T(8,128)S(1)}, f32[4,4,128,128]{3,2,1,0:T(8,128)S(1)}) custom-call(s32[4]{0:T(128)S(1)} %get-tuple-element.96.index_ref, s32[8]{0:T(128)S(1)} %and_select_fusion.1.lag_ref, bf16[16,128,1024]{2,1,0:T(8,128)(2,1)S(1)} %copy-done.2, bf16[16,128,256]{2,1,0:T(8,128)(2,1)S(1)} %collective-permute-done.3.halo_ref, ...), custom_call_target="tpu_custom_call" | custom-call | flops 1 | bytes 1 | tf_op jit(solution)/shard_map/pieces/pallas_call | solution.py:178
  124.5 5.9 %pieces.11 = (f32[4,4,128,128]{3,2,1,0:T(8,128)S(1)}, f32[4,4,128,128]{3,2,1,0:T(8,128)S(1)}) custom-call(s32[4]{0:T(128)S(1)} %get-tuple-element.95.index_ref, s32[8]{0:T(128)S(1)} %and_select_fusion.lag_ref, bf16[16,128,1024]{2,1,0:T(8,128)(2,1)S(1)} %copy-done.2, bf16[16,128,256]{2,1,0:T(8,128)(2,1)S(1)} %collective-permute-done.3.halo_ref, ...), custom_call_target="tpu_custom_call" | custom-call | flops 1 | bytes 1 | tf_op jit(solution)/shard_map/pieces/pallas_call | solution.py:178
  131.4 22.5 %collective-permute-done.12.refs_3_.refs_4_ = f32[4,4,128,128]{3,2,1,0:T(8,128)S(1)} collective-permute-done((f32[4,4,128,128]{3,2,1,0:T(8,128)S(1)}, f32[4,4,128,128]{3,2,1,0:T(8,128)S(1)}, u32[]{:S(2)}, u32[]{:S(2)}) %collective-permute-start.12) | collective-permute-done | bytes 1048608 | tf_op jit(solution)/shard_map/ppermute | solution.py:247
  155.7 5.0 %collective-permute-start.15 = (f32[2,4,128,128]{3,2,1,0:T(8,128)S(1)}, f32[2,4,128,128]{3,2,1,0:T(8,128)S(1)}, u32[]{:S(2)}, u32[]{:S(2)}) collective-permute-start(f32[2,4,128,128]{3,2,1,0:T(8,128)S(1)} %get-tuple-element.70), channel_id=1, source_target_pairs={{0,4},{1,5},{2,6},{3,7},{4,0},{5,1},{6,2},{7,3},{8,12},{9,13},{10,... | collective-permute-start | bytes 1572872 | tf_op jit(solution)/shard_map/ppermute | solution.py:247
  160.7 2.7 %pieces.12 = (f32[4,2,128,128]{3,2,1,0:T(8,128)S(1)}, f32[4,2,128,128]{3,2,1,0:T(8,128)S(1)}) custom-call(s32[2]{0:T(128)S(1)} %get-tuple-element.91.index_ref, s32[8]{0:T(128)S(1)} %and_select_fusion.1.lag_ref, bf16[16,128,1024]{2,1,0:T(8,128)(2,1)S(1)} %copy-done.2, bf16[16,128,256]{2,1,0:T(8,128)(2,1)S(1)} %collective-permute-done.3.halo_ref, ...), custom_call_target="tpu_custom_call" | custom-call | flops 1 | bytes 1 | tf_op jit(solution)/shard_map/pieces/pallas_call | solution.py:178
  163.5 2.7 %pieces.13 = (f32[4,2,128,128]{3,2,1,0:T(8,128)S(1)}, f32[4,2,128,128]{3,2,1,0:T(8,128)S(1)}) custom-call(s32[2]{0:T(128)S(1)} %get-tuple-element.94.index_ref, s32[8]{0:T(128)S(1)} %and_select_fusion.lag_ref, bf16[16,128,1024]{2,1,0:T(8,128)(2,1)S(1)} %copy-done.2, bf16[16,128,256]{2,1,0:T(8,128)(2,1)S(1)} %collective-permute-done.3.halo_ref, ...), custom_call_target="tpu_custom_call" | custom-call | flops 1 | bytes 1 | tf_op jit(solution)/shard_map/pieces/pallas_call | solution.py:178
  166.2 1.6 collective-permute-start.14
  169.3 2.7 %pieces.14 = (f32[4,2,128,128]{3,2,1,0:T(8,128)S(1)}, f32[4,2,128,128]{3,2,1,0:T(8,128)S(1)}) custom-call(s32[2]{0:T(128)S(1)} %get-tuple-element.92.index_ref, s32[8]{0:T(128)S(1)} %and_select_fusion.1.lag_ref, bf16[16,128,1024]{2,1,0:T(8,128)(2,1)S(1)} %copy-done.2, bf16[16,128,256]{2,1,0:T(8,128)(2,1)S(1)} %collective-permute-done.3.halo_ref, ...), custom_call_target="tpu_custom_call" | custom-call | flops 1 | bytes 1 | tf_op jit(solution)/shard_map/pieces/pallas_call | solution.py:178
  172.0 2.7 %pieces.15 = (f32[4,2,128,128]{3,2,1,0:T(8,128)S(1)}, f32[4,2,128,128]{3,2,1,0:T(8,128)S(1)}) custom-call(s32[2]{0:T(128)S(1)} %get-tuple-element.93.index_ref, s32[8]{0:T(128)S(1)} %and_select_fusion.lag_ref, bf16[16,128,1024]{2,1,0:T(8,128)(2,1)S(1)} %copy-done.2, bf16[16,128,256]{2,1,0:T(8,128)(2,1)S(1)} %collective-permute-done.3.halo_ref, ...), custom_call_target="tpu_custom_call" | custom-call | flops 1 | bytes 1 | tf_op jit(solution)/shard_map/pieces/pallas_call | solution.py:178
  176.0 4.0 %collective-permute-start.20 = (f32[2,4,128,128]{3,2,1,0:T(8,128)S(1)}, f32[2,4,128,128]{3,2,1,0:T(8,128)S(1)}, u32[]{:S(2)}, u32[]{:S(2)}) collective-permute-start(f32[2,4,128,128]{3,2,1,0:T(8,128)S(1)} %get-tuple-element.77), channel_id=1, source_target_pairs={{0,4},{1,5},{2,6},{3,7},{4,0},{5,1},{6,2},{7,3},{8,12},{9,13},{10,... | collective-permute-start | bytes 1572872 | tf_op jit(solution)/shard_map/ppermute | solution.py:247
  181.6 8.5 %collective-permute-done.22.refs_3_.refs_4_ = f32[4,2,128,128]{3,2,1,0:T(8,128)S(1)} collective-permute-done((f32[4,2,128,128]{3,2,1,0:T(8,128)S(1)}, f32[4,2,128,128]{3,2,1,0:T(8,128)S(1)}, u32[]{:S(2)}, u32[]{:S(2)}) %collective-permute-start.22) | collective-permute-done | bytes 524320 | tf_op jit(solution)/shard_map/ppermute | solution.py:247
  190.3 1.5 collective-permute-start.24
  192.1 3.6 %collective-permute-done.18.refs_2_ = f32[2,2,128,128]{3,2,1,0:T(8,128)S(1)} collective-permute-done((f32[2,2,128,128]{3,2,1,0:T(8,128)S(1)}, f32[2,2,128,128]{3,2,1,0:T(8,128)S(1)}, u32[]{:S(2)}, u32[]{:S(2)}) %collective-permute-start.18) | collective-permute-done | bytes 262176 | tf_op jit(solution)/shard_map/ppermute | solution.py:247
  196.0 5.9 %collective-permute-start.23 = (f32[2,2,128,128]{3,2,1,0:T(8,128)S(1)}, f32[2,2,128,128]{3,2,1,0:T(8,128)S(1)}, u32[]{:S(2)}, u32[]{:S(2)}) collective-permute-start(f32[2,2,128,128]{3,2,1,0:T(8,128)S(1)} %get-tuple-element.82), channel_id=1, source_target_pairs={{0,4},{1,5},{2,6},{3,7},{4,0},{5,1},{6,2},{7,3},{8,12},{9,13},{10,... | collective-permute-start | bytes 786440 | tf_op jit(solution)/shard_map/ppermute | solution.py:247
  202.2 5.3 %collective-permute-start.26 = (f32[2,2,128,128]{3,2,1,0:T(8,128)S(1)}, f32[2,2,128,128]{3,2,1,0:T(8,128)S(1)}, u32[]{:S(2)}, u32[]{:S(2)}) collective-permute-start(f32[2,2,128,128]{3,2,1,0:T(8,128)S(1)} %get-tuple-element.85), channel_id=1, source_target_pairs={{0,4},{1,5},{2,6},{3,7},{4,0},{5,1},{6,2},{7,3},{8,12},{9,13},{10,... | collective-permute-start | bytes 786440 | tf_op jit(solution)/shard_map/ppermute | solution.py:247
  207.7 6.6 %collective-permute-done.26.three_ref = f32[2,2,128,128]{3,2,1,0:T(8,128)S(1)} collective-permute-done((f32[2,2,128,128]{3,2,1,0:T(8,128)S(1)}, f32[2,2,128,128]{3,2,1,0:T(8,128)S(1)}, u32[]{:S(2)}, u32[]{:S(2)}) %collective-permute-start.26) | collective-permute-done | bytes 262176 | tf_op jit(solution)/shard_map/ppermute | solution.py:247
  (80 shorter events, 21.1 us)
Async XLA Ops:
  0.0 42.2 %copy-start = (s32[8]{0:T(128)S(1)}, s32[8]{0:T(128)}, u32[]{:S(2)}) copy-start(s32[8]{0:T(128)} %param.6) | copy-start | bytes 100
  0.7 18.0 %collective-permute-start = (s32[8]{0:T(128)S(1)}, s32[8]{0:T(128)S(1)}, u32[]{:S(2)}, u32[]{:S(2)}) collective-permute-start(s32[8]{0:T(128)S(1)} %slice_bitcast_fusion.10), channel_id=1, source_target_pairs={{0,104},{8,0},{16,120},{24,16},{32,8},{40,32},{48,24},{56,48},{64,... | collective-permute-start | bytes 104 | tf_op jit(solution)/shard_map/ppermute | solution.py:259
  2.2 16.6 %collective-permute-start.1 = (s32[8]{0:T(128)S(1)}, s32[8]{0:T(128)S(1)}, u32[]{:S(2)}, u32[]{:S(2)}) collective-permute-start(s32[8]{0:T(128)S(1)} %slice_bitcast_fusion.9), channel_id=1, source_target_pairs={{0,112},{8,120},{16,0},{24,8},{32,16},{40,24},{48,32},{56,40},{64,... | collective-permute-start | bytes 104 | tf_op jit(solution)/shard_map/ppermute | solution.py:259
  11.2 14.1 %all-to-all-start = ((f32[8,32,128]{2,1,0:T(8,128)}), f32[8,32,128]{2,1,0:T(8,128)S(1)}, u32[]{:S(2)}, u32[]{:S(2)}) async-start(f32[8,32,128]{2,1,0:T(8,128)} %local_sums.1), calls=%async_computation | async-start | bytes 262144 | tf_op jit(solution)/shard_map/all_to_all | solution.py:276
  18.4 3.1 %collective-permute-start.2 = (s32[8]{0:T(128)S(1)}, s32[8]{0:T(128)S(1)}, u32[]{:S(2)}, u32[]{:S(2)}) collective-permute-start(s32[8]{0:T(128)S(1)} %slice_bitcast_fusion.8), channel_id=1, source_target_pairs={{0,120},{8,112},{16,8},{24,0},{32,24},{40,16},{48,40},{56,32},{64,... | collective-permute-start | bytes 104 | tf_op jit(solution)/shard_map/ppermute | solution.py:259
  36.5 29.1 %collective-permute-start.6 = (bf16[8,128,1024]{2,1,0:T(8,128)(2,1)}, bf16[8,128,1024]{2,1,0:T(8,128)(2,1)S(1)}, u32[]{:S(2)}, u32[]{:S(2)}) collective-permute-start(bf16[8,128,1024]{2,1,0:T(8,128)(2,1)} %get-tuple-element.53), channel_id=1, source_target_pairs={{0,8},{8,32},{16,24},{24,48},{32,40},{40,64},{48,56},{56,80},{64,7... | collective-permute-start | bytes 6291464 | tf_op jit(solution)/shard_map/ppermute | solution.py:259
  39.3 25.4 %collective-permute-start.3 = (bf16[16,128,256]{2,1,0:T(8,128)(2,1)}, bf16[16,128,256]{2,1,0:T(8,128)(2,1)S(1)}, u32[]{:S(2)}, u32[]{:S(2)}) collective-permute-start(bf16[16,128,256]{2,1,0:T(8,128)(2,1)} %get-tuple-element.47), channel_id=1, source_target_pairs={{0,1},{1,2},{2,3},{3,4},{4,5},{5,6},{6,7},{8,9},{9,10},{10,11},{11... | collective-permute-start | bytes 3145736 | tf_op jit(solution)/shard_map/ppermute | solution.py:290
  64.8 53.8 %collective-permute-start.5 = (bf16[8,128,1024]{2,1,0:T(8,128)(2,1)}, bf16[8,128,1024]{2,1,0:T(8,128)(2,1)}, u32[]{:S(2)}, u32[]{:S(2)}) collective-permute-start(bf16[8,128,1024]{2,1,0:T(8,128)(2,1)} %get-tuple-element.52), channel_id=1, source_target_pairs={{0,16},{8,24},{16,32},{24,40},{32,48},{40,56},{48,64},{56,72},{64,... | collective-permute-start | bytes 6291464 | tf_op jit(solution)/shard_map/ppermute | solution.py:259
  65.5 2.2 %copy-start.1 = (bf16[16,128,1024]{2,1,0:T(8,128)(2,1)S(1)}, bf16[16,128,1024]{2,1,0:T(8,128)(2,1)}, u32[]{:S(2)}) copy-start(bf16[16,128,1024]{2,1,0:T(8,128)(2,1)} %get-tuple-element.46.a_ref.refs_0_) | copy-start | bytes 12582916
  77.5 26.1 %collective-permute-start.8 = (f32[4,4,128,128]{3,2,1,0:T(8,128)S(1)}, f32[4,4,128,128]{3,2,1,0:T(8,128)S(1)}, u32[]{:S(2)}, u32[]{:S(2)}) collective-permute-start(f32[4,4,128,128]{3,2,1,0:T(8,128)S(1)} %get-tuple-element.57), channel_id=1, source_target_pairs={{0,3},{1,2},{2,1},{3,0},{4,7},{5,6},{6,5},{7,4},{8,11},{9,10},{10,... | collective-permute-start | bytes 3145736 | tf_op jit(solution)/shard_map/ppermute | solution.py:247
  79.8 24.1 %collective-permute-start.7 = (f32[4,4,128,128]{3,2,1,0:T(8,128)S(1)}, f32[4,4,128,128]{3,2,1,0:T(8,128)S(1)}, u32[]{:S(2)}, u32[]{:S(2)}) collective-permute-start(f32[4,4,128,128]{3,2,1,0:T(8,128)S(1)} %get-tuple-element.55), channel_id=1, source_target_pairs={{0,1},{1,0},{2,3},{3,2},{4,5},{5,4},{6,7},{7,6},{8,9},{9,8},{10,11... | collective-permute-start | bytes 3145736 | tf_op jit(solution)/shard_map/ppermute | solution.py:247
  103.9 2.2 %copy-start.4 = (bf16[8,128,1024]{2,1,0:T(8,128)(2,1)S(1)}, bf16[8,128,1024]{2,1,0:T(8,128)(2,1)}, u32[]{:S(2)}) copy-start(bf16[8,128,1024]{2,1,0:T(8,128)(2,1)} %get-tuple-element.51) | copy-start | bytes 6291460
  104.4 12.1 %collective-permute-start.10 = (f32[2,4,128,128]{3,2,1,0:T(8,128)S(1)}, f32[2,4,128,128]{3,2,1,0:T(8,128)S(1)}, u32[]{:S(2)}, u32[]{:S(2)}) collective-permute-start(f32[2,4,128,128]{3,2,1,0:T(8,128)S(1)} %get-tuple-element.59), channel_id=1, source_target_pairs={{0,1},{1,0},{2,3},{3,2},{4,5},{5,4},{6,7},{7,6},{8,9},{9,8},{10,11... | collective-permute-start | bytes 1572872 | tf_op jit(solution)/shard_map/ppermute | solution.py:247
  104.8 13.2 %collective-permute-start.9 = (f32[2,4,128,128]{3,2,1,0:T(8,128)S(1)}, f32[2,4,128,128]{3,2,1,0:T(8,128)S(1)}, u32[]{:S(2)}, u32[]{:S(2)}) collective-permute-start(f32[2,4,128,128]{3,2,1,0:T(8,128)S(1)} %get-tuple-element.58.refs_6_), channel_id=1, source_target_pairs={{0,3},{1,2},{2,1},{3,0},{4,7},{5,6},{6,5},{7,4},{8,11},{9,10},{10,... | collective-permute-start | bytes 1572872 | tf_op jit(solution)/shard_map/ppermute | solution.py:247
  106.1 54.6 %collective-permute-start.4 = (bf16[8,128,1024]{2,1,0:T(8,128)(2,1)S(1)}, bf16[8,128,1024]{2,1,0:T(8,128)(2,1)S(1)}, u32[]{:S(2)}, u32[]{:S(2)}) collective-permute-start(bf16[8,128,1024]{2,1,0:T(8,128)(2,1)S(1)} %copy-done.4), channel_id=1, source_target_pairs={{0,24},{8,16},{16,40},{24,32},{32,56},{40,48},{48,72},{56,64},{64,... | collective-permute-start | bytes 6291464 | tf_op jit(solution)/shard_map/ppermute | solution.py:259
  107.3 11.3 %copy-start.2 = (bf16[16,128,1024]{2,1,0:T(8,128)(2,1)S(1)}, bf16[16,128,1024]{2,1,0:T(8,128)(2,1)}, u32[]{:S(2)}) copy-start(bf16[16,128,1024]{2,1,0:T(8,128)(2,1)} %get-tuple-element.46.a_ref.refs_0_) | copy-start | bytes 12582916
  130.4 23.6 %collective-permute-start.12 = (f32[4,4,128,128]{3,2,1,0:T(8,128)S(1)}, f32[4,4,128,128]{3,2,1,0:T(8,128)S(1)}, u32[]{:S(2)}, u32[]{:S(2)}) collective-permute-start(f32[4,4,128,128]{3,2,1,0:T(8,128)S(1)} %get-tuple-element.64), channel_id=1, source_target_pairs={{0,3},{1,2},{2,1},{3,0},{4,7},{5,6},{6,5},{7,4},{8,11},{9,10},{10,... | collective-permute-start | bytes 3145736 | tf_op jit(solution)/shard_map/ppermute | solution.py:247
  131.4 22.5 %collective-permute-start.11 = (f32[4,4,128,128]{3,2,1,0:T(8,128)S(1)}, f32[4,4,128,128]{3,2,1,0:T(8,128)S(1)}, u32[]{:S(2)}, u32[]{:S(2)}) collective-permute-start(f32[4,4,128,128]{3,2,1,0:T(8,128)S(1)} %get-tuple-element.62), channel_id=1, source_target_pairs={{0,1},{1,0},{2,3},{3,2},{4,5},{5,4},{6,7},{7,6},{8,9},{9,8},{10,11... | collective-permute-start | bytes 3145736 | tf_op jit(solution)/shard_map/ppermute | solution.py:247
  154.4 14.3 %collective-permute-start.16 = (f32[2,4,128,128]{3,2,1,0:T(8,128)S(1)}, f32[2,4,128,128]{3,2,1,0:T(8,128)S(1)}, u32[]{:S(2)}, u32[]{:S(2)}) collective-permute-start(f32[2,4,128,128]{3,2,1,0:T(8,128)S(1)} %get-tuple-element.65.refs_0_), channel_id=1, source_target_pairs={{0,3},{1,2},{2,1},{3,0},{4,7},{5,6},{6,5},{7,4},{8,11},{9,10},{10,... | collective-permute-start | bytes 1572872 | tf_op jit(solution)/shard_map/ppermute | solution.py:247
  155.7 13.0 %collective-permute-start.17 = (f32[2,4,128,128]{3,2,1,0:T(8,128)S(1)}, f32[2,4,128,128]{3,2,1,0:T(8,128)S(1)}, u32[]{:S(2)}, u32[]{:S(2)}) collective-permute-start(f32[2,4,128,128]{3,2,1,0:T(8,128)S(1)} %get-tuple-element.71), channel_id=1, source_target_pairs={{0,1},{1,0},{2,3},{3,2},{4,5},{5,4},{6,7},{7,6},{8,9},{9,8},{10,11... | collective-permute-start | bytes 1572872 | tf_op jit(solution)/shard_map/ppermute | solution.py:247
  155.7 20.4 %collective-permute-start.15 = (f32[2,4,128,128]{3,2,1,0:T(8,128)S(1)}, f32[2,4,128,128]{3,2,1,0:T(8,128)S(1)}, u32[]{:S(2)}, u32[]{:S(2)}) collective-permute-start(f32[2,4,128,128]{3,2,1,0:T(8,128)S(1)} %get-tuple-element.70), channel_id=1, source_target_pairs={{0,4},{1,5},{2,6},{3,7},{4,0},{5,1},{6,2},{7,3},{8,12},{9,13},{10,... | collective-permute-start | bytes 1572872 | tf_op jit(solution)/shard_map/ppermute | solution.py:247
  166.2 14.1 %collective-permute-start.14 = (f32[4,2,128,128]{3,2,1,0:T(8,128)S(1)}, f32[4,2,128,128]{3,2,1,0:T(8,128)S(1)}, u32[]{:S(2)}, u32[]{:S(2)}) collective-permute-start(f32[4,2,128,128]{3,2,1,0:T(8,128)S(1)} %get-tuple-element.69), channel_id=1, source_target_pairs={{0,3},{1,2},{2,1},{3,0},{4,7},{5,6},{6,5},{7,4},{8,11},{9,10},{10,... | collective-permute-start | bytes 1572872 | tf_op jit(solution)/shard_map/ppermute | solution.py:247
  167.8 12.5 %collective-permute-start.13 = (f32[4,2,128,128]{3,2,1,0:T(8,128)S(1)}, f32[4,2,128,128]{3,2,1,0:T(8,128)S(1)}, u32[]{:S(2)}, u32[]{:S(2)}) collective-permute-start(f32[4,2,128,128]{3,2,1,0:T(8,128)S(1)} %get-tuple-element.67), channel_id=1, source_target_pairs={{0,1},{1,0},{2,3},{3,2},{4,5},{5,4},{6,7},{7,6},{8,9},{9,8},{10,11... | collective-permute-start | bytes 1572872 | tf_op jit(solution)/shard_map/ppermute | solution.py:247
  174.8 15.3 %collective-permute-start.22 = (f32[4,2,128,128]{3,2,1,0:T(8,128)S(1)}, f32[4,2,128,128]{3,2,1,0:T(8,128)S(1)}, u32[]{:S(2)}, u32[]{:S(2)}) collective-permute-start(f32[4,2,128,128]{3,2,1,0:T(8,128)S(1)} %get-tuple-element.79), channel_id=1, source_target_pairs={{0,3},{1,2},{2,1},{3,0},{4,7},{5,6},{6,5},{7,4},{8,11},{9,10},{10,... | collective-permute-start | bytes 1572872 | tf_op jit(solution)/shard_map/ppermute | solution.py:247
  176.0 14.1 %collective-permute-start.21 = (f32[4,2,128,128]{3,2,1,0:T(8,128)S(1)}, f32[4,2,128,128]{3,2,1,0:T(8,128)S(1)}, u32[]{:S(2)}, u32[]{:S(2)}) collective-permute-start(f32[4,2,128,128]{3,2,1,0:T(8,128)S(1)} %get-tuple-element.78), channel_id=1, source_target_pairs={{0,1},{1,0},{2,3},{3,2},{4,5},{5,4},{6,7},{7,6},{8,9},{9,8},{10,11... | collective-permute-start | bytes 1572872 | tf_op jit(solution)/shard_map/ppermute | solution.py:247
  176.0 15.8 %collective-permute-start.20 = (f32[2,4,128,128]{3,2,1,0:T(8,128)S(1)}, f32[2,4,128,128]{3,2,1,0:T(8,128)S(1)}, u32[]{:S(2)}, u32[]{:S(2)}) collective-permute-start(f32[2,4,128,128]{3,2,1,0:T(8,128)S(1)} %get-tuple-element.77), channel_id=1, source_target_pairs={{0,4},{1,5},{2,6},{3,7},{4,0},{5,1},{6,2},{7,3},{8,12},{9,13},{10,... | collective-permute-start | bytes 1572872 | tf_op jit(solution)/shard_map/ppermute | solution.py:247
  180.6 15.1 %collective-permute-start.18 = (f32[2,2,128,128]{3,2,1,0:T(8,128)S(1)}, f32[2,2,128,128]{3,2,1,0:T(8,128)S(1)}, u32[]{:S(2)}, u32[]{:S(2)}) collective-permute-start(f32[2,2,128,128]{3,2,1,0:T(8,128)S(1)} %get-tuple-element.75.refs_4_), channel_id=1, source_target_pairs={{0,3},{1,2},{2,1},{3,0},{4,7},{5,6},{6,5},{7,4},{8,11},{9,10},{10,... | collective-permute-start | bytes 786440 | tf_op jit(solution)/shard_map/ppermute | solution.py:247
  181.4 14.3 %collective-permute-start.19 = (f32[2,2,128,128]{3,2,1,0:T(8,128)S(1)}, f32[2,2,128,128]{3,2,1,0:T(8,128)S(1)}, u32[]{:S(2)}, u32[]{:S(2)}) collective-permute-start(f32[2,2,128,128]{3,2,1,0:T(8,128)S(1)} %get-tuple-element.76), channel_id=1, source_target_pairs={{0,1},{1,0},{2,3},{3,2},{4,5},{5,4},{6,7},{7,6},{8,9},{9,8},{10,11... | collective-permute-start | bytes 786440 | tf_op jit(solution)/shard_map/ppermute | solution.py:247
  190.3 11.6 %collective-permute-start.24 = (f32[2,2,128,128]{3,2,1,0:T(8,128)S(1)}, f32[2,2,128,128]{3,2,1,0:T(8,128)S(1)}, u32[]{:S(2)}, u32[]{:S(2)}) collective-permute-start(f32[2,2,128,128]{3,2,1,0:T(8,128)S(1)} %get-tuple-element.80.refs_0_), channel_id=1, source_target_pairs={{0,3},{1,2},{2,1},{3,0},{4,7},{5,6},{6,5},{7,4},{8,11},{9,10},{10,... | collective-permute-start | bytes 786440 | tf_op jit(solution)/shard_map/ppermute | solution.py:247
  191.9 10.1 %collective-permute-start.25 = (f32[2,2,128,128]{3,2,1,0:T(8,128)S(1)}, f32[2,2,128,128]{3,2,1,0:T(8,128)S(1)}, u32[]{:S(2)}, u32[]{:S(2)}) collective-permute-start(f32[2,2,128,128]{3,2,1,0:T(8,128)S(1)} %get-tuple-element.83), channel_id=1, source_target_pairs={{0,1},{1,0},{2,3},{3,2},{4,5},{5,4},{6,7},{7,6},{8,9},{9,8},{10,11... | collective-permute-start | bytes 786440 | tf_op jit(solution)/shard_map/ppermute | solution.py:247
  196.0 11.6 %collective-permute-start.23 = (f32[2,2,128,128]{3,2,1,0:T(8,128)S(1)}, f32[2,2,128,128]{3,2,1,0:T(8,128)S(1)}, u32[]{:S(2)}, u32[]{:S(2)}) collective-permute-start(f32[2,2,128,128]{3,2,1,0:T(8,128)S(1)} %get-tuple-element.82), channel_id=1, source_target_pairs={{0,4},{1,5},{2,6},{3,7},{4,0},{5,1},{6,2},{7,3},{8,12},{9,13},{10,... | collective-permute-start | bytes 786440 | tf_op jit(solution)/shard_map/ppermute | solution.py:247
  202.2 12.1 %collective-permute-start.26 = (f32[2,2,128,128]{3,2,1,0:T(8,128)S(1)}, f32[2,2,128,128]{3,2,1,0:T(8,128)S(1)}, u32[]{:S(2)}, u32[]{:S(2)}) collective-permute-start(f32[2,2,128,128]{3,2,1,0:T(8,128)S(1)} %get-tuple-element.85), channel_id=1, source_target_pairs={{0,4},{1,5},{2,6},{3,7},{4,0},{5,1},{6,2},{7,3},{8,12},{9,13},{10,... | collective-permute-start | bytes 786440 | tf_op jit(solution)/shard_map/ppermute | solution.py:247
  (1 other events, 0.7 us)

commit v4 on v3

--- a/solution.py
+++ b/solution.py
@@ -10,6 +10,8 @@
 SUB = 128
 LANES = 128
 HALO = 256
+SPARE = 40
+PACK = 3
 STEPS = 3
 PAIRS = 8
 RING = 4
@@ -78,7 +80,7 @@
 
 
 def scale_kernel(counts, index_ref, x_ref, norm_ref, scaled_ref, tail_ref, *refs):
-    send_refs, (wide, narrow, came, went) = refs[:len(counts)], refs[len(counts):]
+    send_refs, (wide, narrow, ends, came, went) = refs[:len(counts)], refs[len(counts):]
     subs, _, hours = x_ref.shape
 
     def arriving(i):
@@ -93,7 +95,18 @@
             narrow[i, :, cols] = value
 
         scale_rows(wide.at[i], norm_ref[0, i:i + 1, :], norm_ref[1, i:i + 1, :], store)
-    leaving = [pltpu.make_async_copy(narrow.at[:, :, hours - HALO:], tail_ref, went.at[0])]
+    lane = lax.broadcasted_iota(jnp.int32, (SUB, LANES), 1)
+    for i in range(subs):
+        ends[i] = narrow[i, :, hours - LANES:]
+    for group in range(ends.shape[0] - subs):
+        tile = jnp.zeros((SUB, LANES), jnp.bfloat16)
+        for place in reversed(range(min(PACK, subs - group * PACK))):
+            spare = narrow[group * PACK + place, :, hours - HALO:hours - LANES]
+            if place:
+                spare = pltpu.roll(spare, LANES - place * SPARE, 1)
+            tile = jnp.where(lane >= LANES - (place + 1) * SPARE, spare, tile)
+        ends[subs + group] = tile
+    leaving = [pltpu.make_async_copy(ends, tail_ref, went.at[0])]
     for send_ref, count in zip(send_refs, counts):
         for i in range(count):
             number = len(leaving)
@@ -112,10 +125,12 @@
 def scaled_parts(index, counts, blocks, norm):
     subs, _, hours = blocks.shape
 
+    tails = subs + pl.cdiv(subs, PACK)
+
     def shape(count, width):
         return jax.ShapeDtypeStruct((count, SUB, width), jnp.bfloat16)
 
-    shapes = [shape(subs, hours), shape(subs, HALO)] + [shape(count, hours) for count in counts]
+    shapes = [shape(subs, hours), shape(tails, LANES)] + [shape(count, hours) for count in counts]
     return pl.pallas_call(
         functools.partial(scale_kernel, counts),
         in_specs=[
@@ -128,6 +143,7 @@
         scratch_shapes=[
             pltpu.VMEM((subs, SUB, hours), jnp.float32),
             pltpu.VMEM((subs, SUB, hours), jnp.bfloat16),
+            pltpu.VMEM((tails, SUB, LANES), jnp.bfloat16),
             pltpu.SemaphoreType.DMA((subs,)),
             pltpu.SemaphoreType.DMA((sum(counts) + 2,)),
         ],
@@ -139,11 +155,13 @@
     )(index, blocks, norm)
 
 
-def piece_kernel(index_ref, lag_ref, a_ref, halo_ref, b_ref, *refs):
+def piece_kernel(index_ref, lag_ref, a_ref, halo_ref, spare_ref, b_ref, *refs):
     keep_ref, send_ref, long_ref, shift_ref = refs[-4:]
     hours = a_ref.shape[2]
     lags = lag_ref.shape[0]
-    long_ref[:, :HALO] = halo_ref[0]
+    place = lax.rem(index_ref[pl.program_id(0)], PACK)
+    long_ref[:, :LANES] = pltpu.roll(spare_ref[0], place * SPARE, 1)
+    long_ref[:, LANES:HALO] = halo_ref[0]
     long_ref[:, HALO:] = a_ref[0]
     lane = lax.broadcasted_iota(jnp.int32, (SUB, LANES), 1)
     for slot in range(lags):
@@ -171,7 +189,7 @@
 
 
 def pieces(index, lags, scaled, halo, partner, start, deps):
-    count, hours = index.shape[0], scaled.shape[2]
+    count, subs, hours = index.shape[0], scaled.shape[0], scaled.shape[2]
     half = lags.shape[0] // 2
     out = jax.ShapeDtypeStruct((half, count, SUB, SUB), jnp.float32)
 
@@ -182,7 +200,10 @@
             grid=(count,),
             in_specs=[
                 pl.BlockSpec((1, SUB, hours), lambda i, index, lags: (index[i], 0, 0)),
-                pl.BlockSpec((1, SUB, HALO), lambda i, index, lags: (index[i], 0, 0)),
+                pl.BlockSpec((1, SUB, LANES), lambda i, index, lags: (index[i], 0, 0)),
+                pl.BlockSpec(
+                    (1, SUB, LANES), lambda i, index, lags: (subs + lax.div(index[i], PACK), 0, 0)
+                ),
                 pl.BlockSpec((1, SUB, hours), lambda i, index, lags: (start + i, 0, 0)),
                 *[pl.BlockSpec(memory_space=pl.ANY)] * len(deps),
             ],
@@ -196,7 +217,7 @@
         compiler_params=pltpu.CompilerParams(vmem_limit_bytes=FEW),
         cost_estimate=pl.CostEstimate(flops=1, bytes_accessed=1, transcendentals=0),
         name="pieces",
-    )(index, lags, scaled, halo, partner, *deps)
+    )(index, lags, scaled, halo, halo, partner, *deps)
 
 
 def tile_call(kernel, name, count, inputs, outputs, scalars=(), deps=()):
@@ -219,10 +240,8 @@
     )(*[array for array, _ in inputs], *scalars, *deps)
 
 
-def forward_kernel(*refs):
-    for order in range(2):
-        keep_ref, one_ref = refs[2 * order:2 * order + 2]
-        refs[order - 2][...] = keep_ref[...] + one_ref[...]
+def forward_kernel(keep_ref, one_ref, *refs):
+    refs[-1][...] = keep_ref[...] + one_ref[...]
 
 
 def across_kernel(*refs):
@@ -271,9 +290,11 @@
     even = lax.axis_index("grid") % 2 == 0
     plan = pair_plan[0]
     plans = (jnp.where(even, plan[2], plan[0]), plan[1], jnp.where(even, plan[0], plan[2]))
-    wanted = jnp.concatenate([along_grid(one[:, 1], route) for one, route in zip(plans, back)])
-
-    norm = norms(lax.all_to_all(local_sums(anomalies, n_tm), "tm", 0, 0), all_hours)
+    sums, *seconds = lax.optimization_barrier(
+        (local_sums(anomalies, n_tm), *[one[:, 1] for one in plans])
+    )
+    wanted = jnp.concatenate([along_grid(one, route) for one, route in zip(seconds, back)])
+    norm = norms(lax.all_to_all(sums, "tm", 0, 0), all_hours)
 
     me = lax.axis_index("tm")
     place, part = me % RING, me // RING
@@ -286,18 +307,20 @@
     lag_slots = [jnp.take(lag_list, (order[:, None] + parts[None, :]).reshape(-1)) for order in orders]
     divisor = (all_hours - lag_slots[0][0]).astype(jnp.float32)
 
-    scaled, tail, *picked = scaled_parts(wanted, (8, 8, 8), blocks, norm)
+    scaled, tail, *picked = scaled_parts(wanted, (4, 4, 8, 4, 4), blocks, norm)
     halo = lax.ppermute(tail, "tm", [(i, i + 1) for i in range(n_tm - 1)])
     beside = along_grid(picked[0], routes[0])
-    halo, *picked = lax.optimization_barrier((halo, *picked[1:]))
-    over, last = [along_grid(one, route) for one, route in zip(picked, routes[1:])]
+    beside, waiting = lax.optimization_barrier((beside, picked[1]))
+    beside = [beside, along_grid(waiting, routes[0])]
+    halo, waiting = lax.optimization_barrier((halo, picked[2]))
+    over = along_grid(waiting, routes[1])
     divisor = divisor.reshape(1)
 
     recent = [scaled]
 
-    def step_one(groups):
+    def step_one(groups, orders=(0, 1)):
         group = []
-        for order, (which, first, count, partner, start) in enumerate(groups):
+        for order, (which, first, count, partner, start) in zip(orders, groups):
             index = plans[which][first:first + count, 0]
             keep, send = pieces(index, lag_slots[order], scaled, halo, partner, start, recent)
             recent[:] = [keep]
@@ -305,14 +328,15 @@
         return group
 
     def step_two(group):
-        count = group[0][0].shape[1]
-        inputs = [(array, 1) for pair in group for array in pair]
-        forward = tile_call(forward_kernel, "forward", count, inputs, 2, deps=recent)
-        recent[:] = [forward[0]]
-        return [
-            (*group[order], along_tm(forward[order], (ring_far, ring_near)[order]))
-            for order in range(2)
-        ]
+        result = []
+        for order, (keep, one) in enumerate(group):
+            inputs = [(keep, 1), (one, 1)]
+            (forward,) = tile_call(
+                forward_kernel, "forward", keep.shape[1], inputs, 1, deps=recent
+            )
+            recent[:] = [forward]
+            result.append((keep, one, along_tm(forward, (ring_far, ring_near)[order])))
+        return result
 
     def step_three(group):
         count = group[0][0].shape[1]
@@ -329,19 +353,22 @@
         recent[:] = [out]
         return out.reshape(-1, SUB, SUB)
 
-    a = step_one([(0, 0, 4, beside, 0), (0, 4, 4, beside, 4)])
+    a = step_one([(0, 0, 4, beside[0], 0), (0, 4, 4, beside[1], 0)])
     a = step_two(a)
+    recent[0], *waiting = lax.optimization_barrier((recent[0], *picked[3:]))
+    last = [along_grid(one, routes[2]) for one in waiting]
+    b = step_one([(1, 0, 4, over, 0)], (0,))
     a = step_three(a)
-    b = step_one([(1, 0, 4, over, 0), (1, 4, 4, over, 4)])
+    b += step_one([(1, 4, 4, over, 4)], (1,))
+    c = step_one([(2, 0, 2, last[0], 0), (2, 2, 2, last[0], 2)])
     b = step_two(b)
-    c = step_one([(2, 0, 2, last, 0), (2, 2, 2, last, 2)])
+    d = step_one([(2, 4, 2, last[1], 0), (2, 6, 2, last[1], 2)])
+    c = step_two(c)
     b = step_three(b)
-    d = step_one([(2, 4, 2, last, 4), (2, 6, 2, last, 6)])
+    d = step_two(d)
+    c = step_three(c)
     a = step_four(*a)
-    c = step_two(c)
-    d = step_two(d)
     b = step_four(*b)
-    c = step_three(c)
     d = step_three(d)
     c = step_four(*c)
     d = step_four(*d)

time: 217 us -> 205 us (0.945)
  waiting for transfers between devices: 104 us -> 74.8 us
  starting transfers between devices: 52.1 us -> 66.5 us
  local copies, waits for them, and re-layouts: 4.54 us -> 6.74 us
    ppermute x20, waiting for transfers between devices: 76.1 us -> 41.5 us  [along_tm(): return lax.ppermute(value, 'tm', [(i, target(i)) for i in range(n_tm)])]
    ppermute x6 -> x8, waiting for transfers between devices: 2.8 us -> 30.7 us  [along_grid(): lax.ppermute(value, 'grid', [(i, route(i) % n_grid) for i in range(n_grid)])]
    ppermute x1, waiting for transfers between devices: 21.9 us -> 2.64 us  [per_device(): halo = lax.ppermute(tail, 'tm', [(i, i + 1) for i in range(n_tm - 1)])]
    ppermute x6 -> x8, starting transfers between devices: 9.58 us -> 19.8 us  [along_grid(): lax.ppermute(value, 'grid', [(i, route(i) % n_grid) for i in range(n_grid)])]
    all_to_all x1, waiting for transfers between devices: 3.21 us -> 0.01 us  [per_device(): norm = norms(lax.all_to_all(sums, 'tm', 0, 0), all_hours)]
    ppermute x20, starting transfers between devices: 32.8 us -> 35.8 us  [along_tm(): return lax.ppermute(value, 'tm', [(i, target(i)) for i in range(n_tm)])]
    unnamed x10 -> x16, local copies, waits for them, and re-layouts: 2.86 us -> 5.06 us
  transfers between devices with their start and end apart: 28 -> 30, of which waited for: 11 -> 15; matrix products, arithmetic and copies ran while one was open for 1% -> 1% of each run, Pallas kernels for 19% -> 18%
where the time goes in v4:
time: 205 us; the launch traced here: 204 us
  waiting for transfers between devices  74.8 us (36%)
  starting transfers between devices  66.5 us (32%)
  Pallas kernels  52.9 us (26%)
  local copies, waits for them, and re-layouts  6.74 us (3%)
  other arithmetic  2.94 us (1%)
    ppermute x20, waiting for transfers between devices, along_tm(): return lax.ppermute(value, 'tm', [(i, target(i)) for i in range(n_tm)])  41.5 us
    ppermute x20, starting transfers between devices, along_tm(): return lax.ppermute(value, 'tm', [(i, target(i)) for i in range(n_tm)])  35.8 us
    pallas_call x8, Pallas kernels, pieces(): pl.pallas_call(piece_kernel, grid_spec=pltpu.PrefetchScalarGridSpec(num_s...  33.1 us
    ppermute x8, waiting for transfers between devices, along_grid(): lax.ppermute(value, 'grid', [(i, route(i) % n_grid) for i in range(n_grid)])  30.7 us
    ppermute x8, starting transfers between devices, along_grid(): lax.ppermute(value, 'grid', [(i, route(i) % n_grid) for i in range(n_grid)])  19.8 us
    pallas_call x1, Pallas kernels, scaled_parts(): pl.pallas_call(functools.partial(scale_kernel, counts), in_specs=[pl.Bloc...  8.98 us
    all_to_all x1, starting transfers between devices, per_device(): norm = norms(lax.all_to_all(sums, 'tm', 0, 0), all_hours)  8.33 us
    pallas_call x1, Pallas kernels, local_sums(): pl.pallas_call(sums_kernel, grid=(steps,), in_specs=[pl.BlockSpec((4 * SU...  5.15 us
  transfers between devices with their start and end apart: 30, of which 15 were waited for; matrix products, arithmetic and copies ran while one was open for 1% of the time, Pallas kernels for 18%

profile of v4, /device:TPU:1, one launch (start us, length us, event | category | flops | bytes accessed | tf_op | source)
XLA Modules:
  0.0 204.2 jit_solution(14069333332703530212)
XLA Ops:
  0.7 5.1 %local_sums.1 = f32[8,32,128]{2,1,0:T(8,128)} custom-call(f32[2048,1024]{1,0:T(8,128)} %x_ref.1), custom_call_target="tpu_custom_call" | custom-call | flops 6291456 | bytes 8388608 | tf_op jit(solution)/shard_map/local_sums/pallas_call | solution.py:40
  5.9 8.3 %all-to-all-start = ((f32[8,32,128]{2,1,0:T(8,128)}), f32[8,32,128]{2,1,0:T(8,128)S(1)}, u32[]{:S(2)}, u32[]{:S(2)}) async-start(f32[8,32,128]{2,1,0:T(8,128)} %local_sums.1), calls=%async_computation | async-start | bytes 262144 | tf_op jit(solution)/shard_map/all_to_all | solution.py:297
  15.2 2.9 %collective-permute-start.1 = (s32[8]{0:T(128)S(1)}, s32[8]{0:T(128)S(1)}, u32[]{:S(2)}, u32[]{:S(2)}) collective-permute-start(s32[8]{0:T(128)S(1)} %get-tuple-element.49), channel_id=1, source_target_pairs={{0,112},{8,120},{16,0},{24,8},{32,16},{40,24},{48,32},{56,40},{64,... | collective-permute-start | bytes 104 | tf_op jit(solution)/shard_map/ppermute | solution.py:278
  24.2 9.0 %scaled_parts.1 = (bf16[16,128,1024]{2,1,0:T(8,128)(2,1)}, bf16[22,128,128]{2,1,0:T(8,128)(2,1)}, bf16[4,128,1024]{2,1,0:T(8,128)(2,1)}, bf16[4,128,1024]{2,1,0:...) custom-call(s32[24]{0:T(128)} %pad_add_fusion.1.index_ref, ...), custom_call_target="tpu_custom_call" | custom-call | flops 1 | bytes 1 | tf_op jit(solution)/shard_map/scaled_parts/pallas_call | solution.py:134
  33.2 2.4 %collective-permute-start.4 = (bf16[4,128,1024]{2,1,0:T(8,128)(2,1)}, bf16[4,128,1024]{2,1,0:T(8,128)(2,1)S(1)}, u32[]{:S(2)}, u32[]{:S(2)}) collective-permute-start(bf16[4,128,1024]{2,1,0:T(8,128)(2,1)} %get-tuple-element.56), channel_id=1, source_target_pairs={{0,8},{8,32},{16,24},{24,48},{32,40},{40,64},{48,56},{56,80},{64,7... | collective-permute-start | bytes 3145736 | tf_op jit(solution)/shard_map/ppermute | solution.py:278
  35.9 2.5 %collective-permute-start.3 = (bf16[22,128,128]{2,1,0:T(8,128)(2,1)}, bf16[22,128,128]{2,1,0:T(8,128)(2,1)S(1)}, u32[]{:S(2)}, u32[]{:S(2)}) collective-permute-start(bf16[22,128,128]{2,1,0:T(8,128)(2,1)} %get-tuple-element.53), channel_id=1, source_target_pairs={{0,1},{1,2},{2,3},{3,4},{4,5},{5,6},{6,7},{8,9},{9,10},{10,11},{11... | collective-permute-start | bytes 2162696 | tf_op jit(solution)/shard_map/ppermute | solution.py:311
  38.4 9.2 %collective-permute-done.4.b_ref = bf16[4,128,1024]{2,1,0:T(8,128)(2,1)S(1)} collective-permute-done((bf16[4,128,1024]{2,1,0:T(8,128)(2,1)}, bf16[4,128,1024]{2,1,0:T(8,128)(2,1)S(1)}, u32[]{:S(2)}, u32[]{:S(2)}) %collective-permute-start.4) | collective-permute-done | bytes 1048608 | tf_op jit(solution)/shard_map/ppermute | solution.py:278
  48.6 2.4 %collective-permute-start.5 = (bf16[4,128,1024]{2,1,0:T(8,128)(2,1)}, bf16[4,128,1024]{2,1,0:T(8,128)(2,1)}, u32[]{:S(2)}, u32[]{:S(2)}) collective-permute-start(bf16[4,128,1024]{2,1,0:T(8,128)(2,1)} %get-tuple-element.58), channel_id=1, source_target_pairs={{0,8},{8,32},{16,24},{24,48},{32,40},{40,64},{48,56},{56,80},{64,7... | collective-permute-start | bytes 3145736 | tf_op jit(solution)/shard_map/ppermute | solution.py:278
  51.7 2.6 %collective-permute-done.3.halo_ref.spare_ref = bf16[22,128,128]{2,1,0:T(8,128)(2,1)S(1)} collective-permute-done((bf16[22,128,128]{2,1,0:T(8,128)(2,1)}, bf16[22,128,128]{2,1,0:T(8,128)(2,1)S(1)}, u32[]{:S(2)}, u32[]{:S(2)}) %collective-permute-start.3) | collective-permute-done | bytes 720928 | tf_op jit(solution)/shard_map/ppermute | solution.py:311
  59.1 5.2 %pieces.8 = (f32[4,4,128,128]{3,2,1,0:T(8,128)S(1)}, f32[4,4,128,128]{3,2,1,0:T(8,128)S(1)}) custom-call(s32[4]{0:T(128)S(1)} %get-tuple-element.102.index_ref, s32[8]{0:T(128)S(1)} %and_select_fusion.1.lag_ref, bf16[16,128,1024]{2,1,0:T(8,128)(2,1)S(1)} %copy-done.1, bf16[22,128,128]{2,1,0:T(8,128)(2,1)S(1)} %collective-permute-done.3.halo_ref.spare_ref, ...), custom_call_target="tpu_custom_call" | custom-call | flops 1 | bytes 1 | tf_op jit(solution)/shard_map/pieces/pallas_call | solution.py:196
  66.5 6.1 %pieces.9 = (f32[4,4,128,128]{3,2,1,0:T(8,128)S(1)}, f32[4,4,128,128]{3,2,1,0:T(8,128)S(1)}) custom-call(s32[4]{0:T(128)S(1)} %get-tuple-element.101.index_ref, s32[8]{0:T(128)S(1)} %and_select_fusion.lag_ref, bf16[16,128,1024]{2,1,0:T(8,128)(2,1)S(1)} %copy-done.1, bf16[22,128,128]{2,1,0:T(8,128)(2,1)S(1)} %collective-permute-done.3.halo_ref.spare_ref, ...), custom_call_target="tpu_custom_call" | custom-call | flops 1 | bytes 1 | tf_op jit(solution)/shard_map/pieces/pallas_call | solution.py:196
  73.8 16.1 %collective-permute-done.7.one_ref.refs_1_ = f32[4,4,128,128]{3,2,1,0:T(8,128)S(1)} collective-permute-done((f32[4,4,128,128]{3,2,1,0:T(8,128)S(1)}, f32[4,4,128,128]{3,2,1,0:T(8,128)S(1)}, u32[]{:S(2)}, u32[]{:S(2)}) %collective-permute-start.7) | collective-permute-done | bytes 1048608 | tf_op jit(solution)/shard_map/ppermute | solution.py:266
  92.1 6.0 %collective-permute-done.6.one_ref.refs_4_ = f32[4,4,128,128]{3,2,1,0:T(8,128)S(1)} collective-permute-done((f32[4,4,128,128]{3,2,1,0:T(8,128)S(1)}, f32[4,4,128,128]{3,2,1,0:T(8,128)S(1)}, u32[]{:S(2)}, u32[]{:S(2)}) %collective-permute-start.6) | collective-permute-done | bytes 1048608 | tf_op jit(solution)/shard_map/ppermute | solution.py:266
  98.5 9.6 %collective-permute-start.8 = (bf16[4,128,1024]{2,1,0:T(8,128)(2,1)S(1)}, bf16[4,128,1024]{2,1,0:T(8,128)(2,1)S(1)}, u32[]{:S(2)}, u32[]{:S(2)}) collective-permute-start(bf16[4,128,1024]{2,1,0:T(8,128)(2,1)S(1)} %copy-done.7), channel_id=1, source_target_pairs={{0,24},{8,16},{16,40},{24,32},{32,56},{40,48},{48,72},{56,64},{64,... | collective-permute-start | bytes 3145736 | tf_op jit(solution)/shard_map/ppermute | solution.py:278
  108.2 6.3 %collective-permute-done.9.b_ref = bf16[8,128,1024]{2,1,0:T(8,128)(2,1)S(1)} collective-permute-done((bf16[8,128,1024]{2,1,0:T(8,128)(2,1)}, bf16[8,128,1024]{2,1,0:T(8,128)(2,1)S(1)}, u32[]{:S(2)}, u32[]{:S(2)}) %collective-permute-start.9) | collective-permute-done | bytes 2097184 | tf_op jit(solution)/shard_map/ppermute | solution.py:278
  114.4 5.2 %pieces.10 = (f32[4,4,128,128]{3,2,1,0:T(8,128)S(1)}, f32[4,4,128,128]{3,2,1,0:T(8,128)S(1)}) custom-call(s32[4]{0:T(128)S(1)} %get-tuple-element.100.index_ref, s32[8]{0:T(128)S(1)} %and_select_fusion.1.lag_ref, bf16[16,128,1024]{2,1,0:T(8,128)(2,1)S(1)} %copy-done.2, bf16[22,128,128]{2,1,0:T(8,128)(2,1)S(1)} %collective-permute-done.3.halo_ref.spare_ref, ...), custom_call_target="tpu_custom_call" | custom-call | flops 1 | bytes 1 | tf_op jit(solution)/shard_map/pieces/pallas_call | solution.py:196
  120.3 5.2 %pieces.11 = (f32[4,4,128,128]{3,2,1,0:T(8,128)S(1)}, f32[4,4,128,128]{3,2,1,0:T(8,128)S(1)}) custom-call(s32[4]{0:T(128)S(1)} %get-tuple-element.99.index_ref, s32[8]{0:T(128)S(1)} %and_select_fusion.lag_ref, bf16[16,128,1024]{2,1,0:T(8,128)(2,1)S(1)} %copy-done.2, bf16[22,128,128]{2,1,0:T(8,128)(2,1)S(1)} %collective-permute-done.3.halo_ref.spare_ref, ...), custom_call_target="tpu_custom_call" | custom-call | flops 1 | bytes 1 | tf_op jit(solution)/shard_map/pieces/pallas_call | solution.py:196
  125.5 3.1 %collective-permute-start.14 = (f32[4,4,128,128]{3,2,1,0:T(8,128)S(1)}, f32[4,4,128,128]{3,2,1,0:T(8,128)S(1)}, u32[]{:S(2)}, u32[]{:S(2)}) collective-permute-start(f32[4,4,128,128]{3,2,1,0:T(8,128)S(1)} %get-tuple-element.75), channel_id=1, source_target_pairs={{0,3},{1,2},{2,1},{3,0},{4,7},{5,6},{6,5},{7,4},{8,11},{9,10},{10,... | collective-permute-start | bytes 3145736 | tf_op jit(solution)/shard_map/ppermute | solution.py:266
  128.7 2.5 %collective-permute-done.8.b_ref = bf16[4,128,1024]{2,1,0:T(8,128)(2,1)S(1)} collective-permute-done((bf16[4,128,1024]{2,1,0:T(8,128)(2,1)S(1)}, bf16[4,128,1024]{2,1,0:T(8,128)(2,1)S(1)}, u32[]{:S(2)}, u32[]{:S(2)}) %collective-permute-start.8) | collective-permute-done | bytes 1048608 | tf_op jit(solution)/shard_map/ppermute | solution.py:278
  131.2 2.9 %pieces.12 = (f32[4,2,128,128]{3,2,1,0:T(8,128)S(1)}, f32[4,2,128,128]{3,2,1,0:T(8,128)S(1)}) custom-call(s32[2]{0:T(128)S(1)} %get-tuple-element.98.index_ref, s32[8]{0:T(128)S(1)} %and_select_fusion.1.lag_ref, bf16[16,128,1024]{2,1,0:T(8,128)(2,1)S(1)} %copy-done.2, bf16[22,128,128]{2,1,0:T(8,128)(2,1)S(1)} %collective-permute-done.3.halo_ref.spare_ref, ...), custom_call_target="tpu_custom_call" | custom-call | flops 1 | bytes 1 | tf_op jit(solution)/shard_map/pieces/pallas_call | solution.py:196
  136.0 2.9 %pieces.13 = (f32[4,2,128,128]{3,2,1,0:T(8,128)S(1)}, f32[4,2,128,128]{3,2,1,0:T(8,128)S(1)}) custom-call(s32[2]{0:T(128)S(1)} %get-tuple-element.95.index_ref, s32[8]{0:T(128)S(1)} %and_select_fusion.lag_ref, bf16[16,128,1024]{2,1,0:T(8,128)(2,1)S(1)} %copy-done.2, bf16[22,128,128]{2,1,0:T(8,128)(2,1)S(1)} %collective-permute-done.3.halo_ref.spare_ref, ...), custom_call_target="tpu_custom_call" | custom-call | flops 1 | bytes 1 | tf_op jit(solution)/shard_map/pieces/pallas_call | solution.py:196
  141.9 3.7 %collective-permute-done.14.one_ref.refs_4_ = f32[4,4,128,128]{3,2,1,0:T(8,128)S(1)} collective-permute-done((f32[4,4,128,128]{3,2,1,0:T(8,128)S(1)}, f32[4,4,128,128]{3,2,1,0:T(8,128)S(1)}, u32[]{:S(2)}, u32[]{:S(2)}) %collective-permute-start.14) | collective-permute-done | bytes 1048608 | tf_op jit(solution)/shard_map/ppermute | solution.py:266
  146.1 10.4 %collective-permute-done.13.b_ref = bf16[4,128,1024]{2,1,0:T(8,128)(2,1)S(1)} collective-permute-done((bf16[4,128,1024]{2,1,0:T(8,128)(2,1)S(1)}, bf16[4,128,1024]{2,1,0:T(8,128)(2,1)S(1)}, u32[]{:S(2)}, u32[]{:S(2)}) %collective-permute-start.13) | collective-permute-done | bytes 1048608 | tf_op jit(solution)/shard_map/ppermute | solution.py:278
  156.5 2.9 %pieces.14 = (f32[4,2,128,128]{3,2,1,0:T(8,128)S(1)}, f32[4,2,128,128]{3,2,1,0:T(8,128)S(1)}) custom-call(s32[2]{0:T(128)S(1)} %get-tuple-element.96.index_ref, s32[8]{0:T(128)S(1)} %and_select_fusion.1.lag_ref, bf16[16,128,1024]{2,1,0:T(8,128)(2,1)S(1)} %copy-done.2, bf16[22,128,128]{2,1,0:T(8,128)(2,1)S(1)} %collective-permute-done.3.halo_ref.spare_ref, ...), custom_call_target="tpu_custom_call" | custom-call | flops 1 | bytes 1 | tf_op jit(solution)/shard_map/pieces/pallas_call | solution.py:196
  160.3 2.9 %pieces.15 = (f32[4,2,128,128]{3,2,1,0:T(8,128)S(1)}, f32[4,2,128,128]{3,2,1,0:T(8,128)S(1)}) custom-call(s32[2]{0:T(128)S(1)} %get-tuple-element.97.index_ref, s32[8]{0:T(128)S(1)} %and_select_fusion.lag_ref, bf16[16,128,1024]{2,1,0:T(8,128)(2,1)S(1)} %copy-done.2, bf16[22,128,128]{2,1,0:T(8,128)(2,1)S(1)} %collective-permute-done.3.halo_ref.spare_ref, ...), custom_call_target="tpu_custom_call" | custom-call | flops 1 | bytes 1 | tf_op jit(solution)/shard_map/pieces/pallas_call | solution.py:196
  164.1 2.5 %collective-permute-start.27 = (f32[2,4,128,128]{3,2,1,0:T(8,128)S(1)}, f32[2,4,128,128]{3,2,1,0:T(8,128)S(1)}, u32[]{:S(2)}, u32[]{:S(2)}) collective-permute-start(f32[2,4,128,128]{3,2,1,0:T(8,128)S(1)} %get-tuple-element.87), channel_id=1, source_target_pairs={{0,4},{1,5},{2,6},{3,7},{4,0},{5,1},{6,2},{7,3},{8,12},{9,13},{10,... | collective-permute-start | bytes 1572872 | tf_op jit(solution)/shard_map/ppermute | solution.py:266
  168.2 6.6 %collective-permute-start.26 = (f32[2,4,128,128]{3,2,1,0:T(8,128)S(1)}, f32[2,4,128,128]{3,2,1,0:T(8,128)S(1)}, u32[]{:S(2)}, u32[]{:S(2)}) collective-permute-start(f32[2,4,128,128]{3,2,1,0:T(8,128)S(1)} %get-tuple-element.86), channel_id=1, source_target_pairs={{0,4},{1,5},{2,6},{3,7},{4,0},{5,1},{6,2},{7,3},{8,12},{9,13},{10,... | collective-permute-start | bytes 1572872 | tf_op jit(solution)/shard_map/ppermute | solution.py:266
  176.3 2.6 %collective-permute-done.19.one_ref.refs_4_ = f32[4,2,128,128]{3,2,1,0:T(8,128)S(1)} collective-permute-done((f32[4,2,128,128]{3,2,1,0:T(8,128)S(1)}, f32[4,2,128,128]{3,2,1,0:T(8,128)S(1)}, u32[]{:S(2)}, u32[]{:S(2)}) %collective-permute-start.19) | collective-permute-done | bytes 524320 | tf_op jit(solution)/shard_map/ppermute | solution.py:266
  179.1 4.0 %collective-permute-done.18.refs_5_ = f32[2,2,128,128]{3,2,1,0:T(8,128)S(1)} collective-permute-done((f32[2,2,128,128]{3,2,1,0:T(8,128)S(1)}, f32[2,2,128,128]{3,2,1,0:T(8,128)S(1)}, u32[]{:S(2)}, u32[]{:S(2)}) %collective-permute-start.18) | collective-permute-done | bytes 262176 | tf_op jit(solution)/shard_map/ppermute | solution.py:266
  185.3 6.1 %collective-permute-start.23 = (f32[2,2,128,128]{3,2,1,0:T(8,128)S(1)}, f32[2,2,128,128]{3,2,1,0:T(8,128)S(1)}, u32[]{:S(2)}, u32[]{:S(2)}) collective-permute-start(f32[2,2,128,128]{3,2,1,0:T(8,128)S(1)} %get-tuple-element.85), channel_id=1, source_target_pairs={{0,4},{1,5},{2,6},{3,7},{4,0},{5,1},{6,2},{7,3},{8,12},{9,13},{10,... | collective-permute-start | bytes 786440 | tf_op jit(solution)/shard_map/ppermute | solution.py:266
  192.3 3.9 %collective-permute-start.28 = (f32[2,2,128,128]{3,2,1,0:T(8,128)S(1)}, f32[2,2,128,128]{3,2,1,0:T(8,128)S(1)}, u32[]{:S(2)}, u32[]{:S(2)}) collective-permute-start(f32[2,2,128,128]{3,2,1,0:T(8,128)S(1)} %get-tuple-element.89), channel_id=1, source_target_pairs={{0,4},{1,5},{2,6},{3,7},{4,0},{5,1},{6,2},{7,3},{8,12},{9,13},{10,... | collective-permute-start | bytes 786440 | tf_op jit(solution)/shard_map/ppermute | solution.py:266
  197.4 5.3 %collective-permute-done.28.three_ref = f32[2,2,128,128]{3,2,1,0:T(8,128)S(1)} collective-permute-done((f32[2,2,128,128]{3,2,1,0:T(8,128)S(1)}, f32[2,2,128,128]{3,2,1,0:T(8,128)S(1)}, u32[]{:S(2)}, u32[]{:S(2)}) %collective-permute-start.28) | collective-permute-done | bytes 262176 | tf_op jit(solution)/shard_map/ppermute | solution.py:266
  (93 shorter events, 37.6 us)
Async XLA Ops:
  0.0 51.0 %copy-start = (s32[8]{0:T(128)S(1)}, s32[8]{0:T(128)}, u32[]{:S(2)}) copy-start(s32[8]{0:T(128)} %param.6) | copy-start | bytes 100
  5.9 16.1 %all-to-all-start = ((f32[8,32,128]{2,1,0:T(8,128)}), f32[8,32,128]{2,1,0:T(8,128)S(1)}, u32[]{:S(2)}, u32[]{:S(2)}) async-start(f32[8,32,128]{2,1,0:T(8,128)} %local_sums.1), calls=%async_computation | async-start | bytes 262144 | tf_op jit(solution)/shard_map/all_to_all | solution.py:297
  14.2 4.9 %collective-permute-start = (s32[8]{0:T(128)S(1)}, s32[8]{0:T(128)S(1)}, u32[]{:S(2)}, u32[]{:S(2)}) collective-permute-start(s32[8]{0:T(128)S(1)} %slice_bitcast_fusion.10), channel_id=1, source_target_pairs={{0,104},{8,0},{16,120},{24,16},{32,8},{40,32},{48,24},{56,48},{64,... | collective-permute-start | bytes 104 | tf_op jit(solution)/shard_map/ppermute | solution.py:278
  15.2 3.9 %collective-permute-start.1 = (s32[8]{0:T(128)S(1)}, s32[8]{0:T(128)S(1)}, u32[]{:S(2)}, u32[]{:S(2)}) collective-permute-start(s32[8]{0:T(128)S(1)} %get-tuple-element.49), channel_id=1, source_target_pairs={{0,112},{8,120},{16,0},{24,8},{32,16},{40,24},{48,32},{56,40},{64,... | collective-permute-start | bytes 104 | tf_op jit(solution)/shard_map/ppermute | solution.py:278
  18.1 3.3 %collective-permute-start.2 = (s32[8]{0:T(128)S(1)}, s32[8]{0:T(128)S(1)}, u32[]{:S(2)}, u32[]{:S(2)}) collective-permute-start(s32[8]{0:T(128)S(1)} %get-tuple-element.50), channel_id=1, source_target_pairs={{0,120},{8,112},{16,8},{24,0},{32,24},{40,16},{48,40},{56,32},{64,... | collective-permute-start | bytes 104 | tf_op jit(solution)/shard_map/ppermute | solution.py:278
  33.2 14.4 %collective-permute-start.4 = (bf16[4,128,1024]{2,1,0:T(8,128)(2,1)}, bf16[4,128,1024]{2,1,0:T(8,128)(2,1)S(1)}, u32[]{:S(2)}, u32[]{:S(2)}) collective-permute-start(bf16[4,128,1024]{2,1,0:T(8,128)(2,1)} %get-tuple-element.56), channel_id=1, source_target_pairs={{0,8},{8,32},{16,24},{24,48},{32,40},{40,64},{48,56},{56,80},{64,7... | collective-permute-start | bytes 3145736 | tf_op jit(solution)/shard_map/ppermute | solution.py:278
  35.9 18.5 %collective-permute-start.3 = (bf16[22,128,128]{2,1,0:T(8,128)(2,1)}, bf16[22,128,128]{2,1,0:T(8,128)(2,1)S(1)}, u32[]{:S(2)}, u32[]{:S(2)}) collective-permute-start(bf16[22,128,128]{2,1,0:T(8,128)(2,1)} %get-tuple-element.53), channel_id=1, source_target_pairs={{0,1},{1,2},{2,3},{3,4},{4,5},{5,6},{6,7},{8,9},{9,10},{10,11},{11... | collective-permute-start | bytes 2162696 | tf_op jit(solution)/shard_map/ppermute | solution.py:311
  48.6 17.9 %collective-permute-start.5 = (bf16[4,128,1024]{2,1,0:T(8,128)(2,1)}, bf16[4,128,1024]{2,1,0:T(8,128)(2,1)}, u32[]{:S(2)}, u32[]{:S(2)}) collective-permute-start(bf16[4,128,1024]{2,1,0:T(8,128)(2,1)} %get-tuple-element.58), channel_id=1, source_target_pairs={{0,8},{8,32},{16,24},{24,48},{32,40},{40,64},{48,56},{56,80},{64,7... | collective-permute-start | bytes 3145736 | tf_op jit(solution)/shard_map/ppermute | solution.py:278
  54.3 60.1 %collective-permute-start.9 = (bf16[8,128,1024]{2,1,0:T(8,128)(2,1)}, bf16[8,128,1024]{2,1,0:T(8,128)(2,1)S(1)}, u32[]{:S(2)}, u32[]{:S(2)}) collective-permute-start(bf16[8,128,1024]{2,1,0:T(8,128)(2,1)} %get-tuple-element.67), channel_id=1, source_target_pairs={{0,16},{8,24},{16,32},{24,40},{32,48},{40,56},{48,64},{56,72},{64,... | collective-permute-start | bytes 6291464 | tf_op jit(solution)/shard_map/ppermute | solution.py:278
  64.2 25.6 %collective-permute-start.7 = (f32[4,4,128,128]{3,2,1,0:T(8,128)S(1)}, f32[4,4,128,128]{3,2,1,0:T(8,128)S(1)}, u32[]{:S(2)}, u32[]{:S(2)}) collective-permute-start(f32[4,4,128,128]{3,2,1,0:T(8,128)S(1)} %get-tuple-element.63), channel_id=1, source_target_pairs={{0,1},{1,0},{2,3},{3,2},{4,5},{5,4},{6,7},{7,6},{8,9},{9,8},{10,11... | collective-permute-start | bytes 3145736 | tf_op jit(solution)/shard_map/ppermute | solution.py:266
  72.6 25.5 %collective-permute-start.6 = (f32[4,4,128,128]{3,2,1,0:T(8,128)S(1)}, f32[4,4,128,128]{3,2,1,0:T(8,128)S(1)}, u32[]{:S(2)}, u32[]{:S(2)}) collective-permute-start(f32[4,4,128,128]{3,2,1,0:T(8,128)S(1)} %get-tuple-element.62), channel_id=1, source_target_pairs={{0,3},{1,2},{2,1},{3,0},{4,7},{5,6},{6,5},{7,4},{8,11},{9,10},{10,... | collective-permute-start | bytes 3145736 | tf_op jit(solution)/shard_map/ppermute | solution.py:266
  89.9 24.5 %copy-start.2 = (bf16[16,128,1024]{2,1,0:T(8,128)(2,1)S(1)}, bf16[16,128,1024]{2,1,0:T(8,128)(2,1)}, u32[]{:S(2)}) copy-start(bf16[16,128,1024]{2,1,0:T(8,128)(2,1)} %get-tuple-element.52.a_ref.refs_0_) | copy-start | bytes 12582916
  90.2 29.5 %collective-permute-start.10 = (f32[2,4,128,128]{3,2,1,0:T(8,128)S(1)}, f32[2,4,128,128]{3,2,1,0:T(8,128)S(1)}, u32[]{:S(2)}, u32[]{:S(2)}) collective-permute-start(f32[2,4,128,128]{3,2,1,0:T(8,128)S(1)} %forward.8.refs_0_), channel_id=1, source_target_pairs={{0,3},{1,2},{2,1},{3,0},{4,7},{5,6},{6,5},{7,4},{8,11},{9,10},{10,... | collective-permute-start | bytes 1572872 | tf_op jit(solution)/shard_map/ppermute | solution.py:266
  98.4 21.3 %collective-permute-start.11 = (f32[2,4,128,128]{3,2,1,0:T(8,128)S(1)}, f32[2,4,128,128]{3,2,1,0:T(8,128)S(1)}, u32[]{:S(2)}, u32[]{:S(2)}) collective-permute-start(f32[2,4,128,128]{3,2,1,0:T(8,128)S(1)} %forward.9.refs_0_), channel_id=1, source_target_pairs={{0,1},{1,0},{2,3},{3,2},{4,5},{5,4},{6,7},{7,6},{8,9},{9,8},{10,11... | collective-permute-start | bytes 1572872 | tf_op jit(solution)/shard_map/ppermute | solution.py:266
  98.5 32.7 %collective-permute-start.8 = (bf16[4,128,1024]{2,1,0:T(8,128)(2,1)S(1)}, bf16[4,128,1024]{2,1,0:T(8,128)(2,1)S(1)}, u32[]{:S(2)}, u32[]{:S(2)}) collective-permute-start(bf16[4,128,1024]{2,1,0:T(8,128)(2,1)S(1)} %copy-done.7), channel_id=1, source_target_pairs={{0,24},{8,16},{16,40},{24,32},{32,56},{40,48},{48,72},{56,64},{64,... | collective-permute-start | bytes 3145736 | tf_op jit(solution)/shard_map/ppermute | solution.py:278
  119.6 19.8 %collective-permute-start.15 = (f32[4,4,128,128]{3,2,1,0:T(8,128)S(1)}, f32[4,4,128,128]{3,2,1,0:T(8,128)S(1)}, u32[]{:S(2)}, u32[]{:S(2)}) collective-permute-start(f32[4,4,128,128]{3,2,1,0:T(8,128)S(1)} %get-tuple-element.76), channel_id=1, source_target_pairs={{0,1},{1,0},{2,3},{3,2},{4,5},{5,4},{6,7},{7,6},{8,9},{9,8},{10,11... | collective-permute-start | bytes 3145736 | tf_op jit(solution)/shard_map/ppermute | solution.py:266
  125.5 20.2 %collective-permute-start.14 = (f32[4,4,128,128]{3,2,1,0:T(8,128)S(1)}, f32[4,4,128,128]{3,2,1,0:T(8,128)S(1)}, u32[]{:S(2)}, u32[]{:S(2)}) collective-permute-start(f32[4,4,128,128]{3,2,1,0:T(8,128)S(1)} %get-tuple-element.75), channel_id=1, source_target_pairs={{0,3},{1,2},{2,1},{3,0},{4,7},{5,6},{6,5},{7,4},{8,11},{9,10},{10,... | collective-permute-start | bytes 3145736 | tf_op jit(solution)/shard_map/ppermute | solution.py:266
  128.6 27.9 %collective-permute-start.13 = (bf16[4,128,1024]{2,1,0:T(8,128)(2,1)S(1)}, bf16[4,128,1024]{2,1,0:T(8,128)(2,1)S(1)}, u32[]{:S(2)}, u32[]{:S(2)}) collective-permute-start(bf16[4,128,1024]{2,1,0:T(8,128)(2,1)S(1)} %copy-done.6), channel_id=1, source_target_pairs={{0,24},{8,16},{16,40},{24,32},{32,56},{40,48},{48,72},{56,64},{64,... | collective-permute-start | bytes 3145736 | tf_op jit(solution)/shard_map/ppermute | solution.py:278
  134.0 29.1 %collective-permute-start.12 = (f32[4,2,128,128]{3,2,1,0:T(8,128)S(1)}, f32[4,2,128,128]{3,2,1,0:T(8,128)S(1)}, u32[]{:S(2)}, u32[]{:S(2)}) collective-permute-start(f32[4,2,128,128]{3,2,1,0:T(8,128)S(1)} %get-tuple-element.73), channel_id=1, source_target_pairs={{0,1},{1,0},{2,3},{3,2},{4,5},{5,4},{6,7},{7,6},{8,9},{9,8},{10,11... | collective-permute-start | bytes 1572872 | tf_op jit(solution)/shard_map/ppermute | solution.py:266
  138.8 25.3 %collective-permute-start.17 = (f32[4,2,128,128]{3,2,1,0:T(8,128)S(1)}, f32[4,2,128,128]{3,2,1,0:T(8,128)S(1)}, u32[]{:S(2)}, u32[]{:S(2)}) collective-permute-start(f32[4,2,128,128]{3,2,1,0:T(8,128)S(1)} %get-tuple-element.80), channel_id=1, source_target_pairs={{0,3},{1,2},{2,1},{3,0},{4,7},{5,6},{6,5},{7,4},{8,11},{9,10},{10,... | collective-permute-start | bytes 1572872 | tf_op jit(solution)/shard_map/ppermute | solution.py:266
  139.6 28.0 %collective-permute-start.21 = (f32[2,4,128,128]{3,2,1,0:T(8,128)S(1)}, f32[2,4,128,128]{3,2,1,0:T(8,128)S(1)}, u32[]{:S(2)}, u32[]{:S(2)}) collective-permute-start(f32[2,4,128,128]{3,2,1,0:T(8,128)S(1)} %forward.10.refs_0_), channel_id=1, source_target_pairs={{0,3},{1,2},{2,1},{3,0},{4,7},{5,6},{6,5},{7,4},{8,11},{9,10},{10,... | collective-permute-start | bytes 1572872 | tf_op jit(solution)/shard_map/ppermute | solution.py:266
  145.9 21.7 %collective-permute-start.22 = (f32[2,4,128,128]{3,2,1,0:T(8,128)S(1)}, f32[2,4,128,128]{3,2,1,0:T(8,128)S(1)}, u32[]{:S(2)}, u32[]{:S(2)}) collective-permute-start(f32[2,4,128,128]{3,2,1,0:T(8,128)S(1)} %forward.11.refs_0_), channel_id=1, source_target_pairs={{0,1},{1,0},{2,3},{3,2},{4,5},{5,4},{6,7},{7,6},{8,9},{9,8},{10,11... | collective-permute-start | bytes 1572872 | tf_op jit(solution)/shard_map/ppermute | solution.py:266
  159.4 16.7 %collective-permute-start.20 = (f32[4,2,128,128]{3,2,1,0:T(8,128)S(1)}, f32[4,2,128,128]{3,2,1,0:T(8,128)S(1)}, u32[]{:S(2)}, u32[]{:S(2)}) collective-permute-start(f32[4,2,128,128]{3,2,1,0:T(8,128)S(1)} %get-tuple-element.82), channel_id=1, source_target_pairs={{0,1},{1,0},{2,3},{3,2},{4,5},{5,4},{6,7},{7,6},{8,9},{9,8},{10,11... | collective-permute-start | bytes 1572872 | tf_op jit(solution)/shard_map/ppermute | solution.py:266
  163.2 15.6 %collective-permute-start.19 = (f32[4,2,128,128]{3,2,1,0:T(8,128)S(1)}, f32[4,2,128,128]{3,2,1,0:T(8,128)S(1)}, u32[]{:S(2)}, u32[]{:S(2)}) collective-permute-start(f32[4,2,128,128]{3,2,1,0:T(8,128)S(1)} %get-tuple-element.81), channel_id=1, source_target_pairs={{0,3},{1,2},{2,1},{3,0},{4,7},{5,6},{6,5},{7,4},{8,11},{9,10},{10,... | collective-permute-start | bytes 1572872 | tf_op jit(solution)/shard_map/ppermute | solution.py:266
  164.1 27.2 %collective-permute-start.27 = (f32[2,4,128,128]{3,2,1,0:T(8,128)S(1)}, f32[2,4,128,128]{3,2,1,0:T(8,128)S(1)}, u32[]{:S(2)}, u32[]{:S(2)}) collective-permute-start(f32[2,4,128,128]{3,2,1,0:T(8,128)S(1)} %get-tuple-element.87), channel_id=1, source_target_pairs={{0,4},{1,5},{2,6},{3,7},{4,0},{5,1},{6,2},{7,3},{8,12},{9,13},{10,... | collective-permute-start | bytes 1572872 | tf_op jit(solution)/shard_map/ppermute | solution.py:266
  168.2 23.5 %collective-permute-start.26 = (f32[2,4,128,128]{3,2,1,0:T(8,128)S(1)}, f32[2,4,128,128]{3,2,1,0:T(8,128)S(1)}, u32[]{:S(2)}, u32[]{:S(2)}) collective-permute-start(f32[2,4,128,128]{3,2,1,0:T(8,128)S(1)} %get-tuple-element.86), channel_id=1, source_target_pairs={{0,4},{1,5},{2,6},{3,7},{4,0},{5,1},{6,2},{7,3},{8,12},{9,13},{10,... | collective-permute-start | bytes 1572872 | tf_op jit(solution)/shard_map/ppermute | solution.py:266
  174.8 8.2 %collective-permute-start.18 = (f32[2,2,128,128]{3,2,1,0:T(8,128)S(1)}, f32[2,2,128,128]{3,2,1,0:T(8,128)S(1)}, u32[]{:S(2)}, u32[]{:S(2)}) collective-permute-start(f32[2,2,128,128]{3,2,1,0:T(8,128)S(1)} %forward.13.refs_6_), channel_id=1, source_target_pairs={{0,1},{1,0},{2,3},{3,2},{4,5},{5,4},{6,7},{7,6},{8,9},{9,8},{10,11... | collective-permute-start | bytes 786440 | tf_op jit(solution)/shard_map/ppermute | solution.py:266
  176.1 8.9 %collective-permute-start.16 = (f32[2,2,128,128]{3,2,1,0:T(8,128)S(1)}, f32[2,2,128,128]{3,2,1,0:T(8,128)S(1)}, u32[]{:S(2)}, u32[]{:S(2)}) collective-permute-start(f32[2,2,128,128]{3,2,1,0:T(8,128)S(1)} %forward.12.refs_0_), channel_id=1, source_target_pairs={{0,3},{1,2},{2,1},{3,0},{4,7},{5,6},{6,5},{7,4},{8,11},{9,10},{10,... | collective-permute-start | bytes 786440 | tf_op jit(solution)/shard_map/ppermute | solution.py:266
  179.0 13.0 %collective-permute-start.25 = (f32[2,2,128,128]{3,2,1,0:T(8,128)S(1)}, f32[2,2,128,128]{3,2,1,0:T(8,128)S(1)}, u32[]{:S(2)}, u32[]{:S(2)}) collective-permute-start(f32[2,2,128,128]{3,2,1,0:T(8,128)S(1)} %forward.15.refs_6_), channel_id=1, source_target_pairs={{0,1},{1,0},{2,3},{3,2},{4,5},{5,4},{6,7},{7,6},{8,9},{9,8},{10,11... | collective-permute-start | bytes 786440 | tf_op jit(solution)/shard_map/ppermute | solution.py:266
  183.0 8.9 %collective-permute-start.24 = (f32[2,2,128,128]{3,2,1,0:T(8,128)S(1)}, f32[2,2,128,128]{3,2,1,0:T(8,128)S(1)}, u32[]{:S(2)}, u32[]{:S(2)}) collective-permute-start(f32[2,2,128,128]{3,2,1,0:T(8,128)S(1)} %forward.14.refs_0_), channel_id=1, source_target_pairs={{0,3},{1,2},{2,1},{3,0},{4,7},{5,6},{6,5},{7,4},{8,11},{9,10},{10,... | collective-permute-start | bytes 786440 | tf_op jit(solution)/shard_map/ppermute | solution.py:266
  185.3 12.0 %collective-permute-start.23 = (f32[2,2,128,128]{3,2,1,0:T(8,128)S(1)}, f32[2,2,128,128]{3,2,1,0:T(8,128)S(1)}, u32[]{:S(2)}, u32[]{:S(2)}) collective-permute-start(f32[2,2,128,128]{3,2,1,0:T(8,128)S(1)} %get-tuple-element.85), channel_id=1, source_target_pairs={{0,4},{1,5},{2,6},{3,7},{4,0},{5,1},{6,2},{7,3},{8,12},{9,13},{10,... | collective-permute-start | bytes 786440 | tf_op jit(solution)/shard_map/ppermute | solution.py:266
  192.3 10.4 %collective-permute-start.28 = (f32[2,2,128,128]{3,2,1,0:T(8,128)S(1)}, f32[2,2,128,128]{3,2,1,0:T(8,128)S(1)}, u32[]{:S(2)}, u32[]{:S(2)}) collective-permute-start(f32[2,2,128,128]{3,2,1,0:T(8,128)S(1)} %get-tuple-element.89), channel_id=1, source_target_pairs={{0,4},{1,5},{2,6},{3,7},{4,0},{5,1},{6,2},{7,3},{8,12},{9,13},{10,... | collective-permute-start | bytes 786440 | tf_op jit(solution)/shard_map/ppermute | solution.py:266
  (6 other events, 21.7 us)

commit v5 on v4

--- a/solution.py
+++ b/solution.py
@@ -80,7 +80,7 @@
 
 
 def scale_kernel(counts, index_ref, x_ref, norm_ref, scaled_ref, tail_ref, *refs):
-    send_refs, (wide, narrow, ends, came, went) = refs[:len(counts)], refs[len(counts):]
+    send_refs, (wide, narrow, ends, came, went, stays) = refs[:len(counts)], refs[len(counts):]
     subs, _, hours = x_ref.shape
 
     def arriving(i):
@@ -95,6 +95,8 @@
             narrow[i, :, cols] = value
 
         scale_rows(wide.at[i], norm_ref[0, i:i + 1, :], norm_ref[1, i:i + 1, :], store)
+        kept = pltpu.make_async_copy(narrow.at[i], scaled_ref.at[i], stays.at[i])
+        kept.start()
     lane = lax.broadcasted_iota(jnp.int32, (SUB, LANES), 1)
     for i in range(subs):
         ends[i] = narrow[i, :, hours - LANES:]
@@ -115,11 +117,12 @@
                     narrow.at[index_ref[number - 1]], send_ref.at[i], went.at[number]
                 )
             )
-    leaving.append(pltpu.make_async_copy(narrow, scaled_ref, went.at[len(leaving)]))
     for copy in leaving:
         copy.start()
     for copy in leaving:
         copy.wait()
+    for i in range(subs):
+        pltpu.make_async_copy(narrow.at[i], scaled_ref.at[i], stays.at[i]).wait()
 
 
 def scaled_parts(index, counts, blocks, norm):
@@ -145,7 +148,8 @@
             pltpu.VMEM((subs, SUB, hours), jnp.bfloat16),
             pltpu.VMEM((tails, SUB, LANES), jnp.bfloat16),
             pltpu.SemaphoreType.DMA((subs,)),
-            pltpu.SemaphoreType.DMA((sum(counts) + 2,)),
+            pltpu.SemaphoreType.DMA((sum(counts) + 1,)),
+            pltpu.SemaphoreType.DMA((subs,)),
         ],
         compiler_params=pltpu.CompilerParams(vmem_limit_bytes=MANY),
         cost_estimate=pl.CostEstimate(

time: 205 us -> 204 us (level)
  no operation moved by 1% of the time
where the time goes in v5:
time: 204 us
  waiting for transfers between devices  74.8 us (37%)
  starting transfers between devices  66.5 us (33%)
  Pallas kernels  52.6 us (26%)
  local copies, waits for them, and re-layouts  6.74 us (3%)
  other arithmetic  2.94 us (1%)
    ppermute x20, waiting for transfers between devices, along_tm(): return lax.ppermute(value, 'tm', [(i, target(i)) for i in range(n_tm)])  41.5 us
    ppermute x20, starting transfers between devices, along_tm(): return lax.ppermute(value, 'tm', [(i, target(i)) for i in range(n_tm)])  35.9 us
    pallas_call x8, Pallas kernels, pieces(): pl.pallas_call(piece_kernel, grid_spec=pltpu.PrefetchScalarGridSpec(num_s...  33 us
    ppermute x8, waiting for transfers between devices, along_grid(): lax.ppermute(value, 'grid', [(i, route(i) % n_grid) for i in range(n_grid)])  30.7 us
    ppermute x8, starting transfers between devices, along_grid(): lax.ppermute(value, 'grid', [(i, route(i) % n_grid) for i in range(n_grid)])  19.8 us
    pallas_call x1, Pallas kernels, scaled_parts(): pl.pallas_call(functools.partial(scale_kernel, counts), in_specs=[pl.Bloc...  8.72 us
    all_to_all x1, starting transfers between devices, per_device(): norm = norms(lax.all_to_all(sums, 'tm', 0, 0), all_hours)  8.33 us
    pallas_call x1, Pallas kernels, local_sums(): pl.pallas_call(sums_kernel, grid=(steps,), in_specs=[pl.BlockSpec((4 * SU...  5.15 us
  transfers between devices with their start and end apart: 30, of which 15 were waited for; matrix products, arithmetic and copies ran while one was open for 1% of the time, Pallas kernels for 18%

profile of v5, /device:TPU:1, one launch (start us, length us, event | category | flops | bytes accessed | tf_op | source)
XLA Modules:
  0.0 204.0 jit_solution(13501443682792739352)
XLA Ops:
  0.7 5.1 %local_sums.1 = f32[8,32,128]{2,1,0:T(8,128)} custom-call(f32[2048,1024]{1,0:T(8,128)} %x_ref.1), custom_call_target="tpu_custom_call" | custom-call | flops 6291456 | bytes 8388608 | tf_op jit(solution)/shard_map/local_sums/pallas_call | solution.py:40
  5.9 8.3 %all-to-all-start = ((f32[8,32,128]{2,1,0:T(8,128)}), f32[8,32,128]{2,1,0:T(8,128)S(1)}, u32[]{:S(2)}, u32[]{:S(2)}) async-start(f32[8,32,128]{2,1,0:T(8,128)} %local_sums.1), calls=%async_computation | async-start | bytes 262144 | tf_op jit(solution)/shard_map/all_to_all | solution.py:301
  15.2 2.9 %collective-permute-start.1 = (s32[8]{0:T(128)S(1)}, s32[8]{0:T(128)S(1)}, u32[]{:S(2)}, u32[]{:S(2)}) collective-permute-start(s32[8]{0:T(128)S(1)} %get-tuple-element.49), channel_id=1, source_target_pairs={{0,112},{8,120},{16,0},{24,8},{32,16},{40,24},{48,32},{56,40},{64,... | collective-permute-start | bytes 104 | tf_op jit(solution)/shard_map/ppermute | solution.py:282
  24.2 8.7 %scaled_parts.1 = (bf16[16,128,1024]{2,1,0:T(8,128)(2,1)}, bf16[22,128,128]{2,1,0:T(8,128)(2,1)}, bf16[4,128,1024]{2,1,0:T(8,128)(2,1)}, bf16[4,128,1024]{2,1,0:...) custom-call(s32[24]{0:T(128)} %pad_add_fusion.1.index_ref, ...), custom_call_target="tpu_custom_call" | custom-call | flops 1 | bytes 1 | tf_op jit(solution)/shard_map/scaled_parts/pallas_call | solution.py:137
  32.9 2.4 %collective-permute-start.4 = (bf16[4,128,1024]{2,1,0:T(8,128)(2,1)}, bf16[4,128,1024]{2,1,0:T(8,128)(2,1)S(1)}, u32[]{:S(2)}, u32[]{:S(2)}) collective-permute-start(bf16[4,128,1024]{2,1,0:T(8,128)(2,1)} %get-tuple-element.56), channel_id=1, source_target_pairs={{0,8},{8,32},{16,24},{24,48},{32,40},{40,64},{48,56},{56,80},{64,7... | collective-permute-start | bytes 3145736 | tf_op jit(solution)/shard_map/ppermute | solution.py:282
  35.6 2.5 %collective-permute-start.3 = (bf16[22,128,128]{2,1,0:T(8,128)(2,1)}, bf16[22,128,128]{2,1,0:T(8,128)(2,1)S(1)}, u32[]{:S(2)}, u32[]{:S(2)}) collective-permute-start(bf16[22,128,128]{2,1,0:T(8,128)(2,1)} %get-tuple-element.53), channel_id=1, source_target_pairs={{0,1},{1,2},{2,3},{3,4},{4,5},{5,6},{6,7},{8,9},{9,10},{10,11},{11... | collective-permute-start | bytes 2162696 | tf_op jit(solution)/shard_map/ppermute | solution.py:315
  38.1 9.2 %collective-permute-done.4.b_ref = bf16[4,128,1024]{2,1,0:T(8,128)(2,1)S(1)} collective-permute-done((bf16[4,128,1024]{2,1,0:T(8,128)(2,1)}, bf16[4,128,1024]{2,1,0:T(8,128)(2,1)S(1)}, u32[]{:S(2)}, u32[]{:S(2)}) %collective-permute-start.4) | collective-permute-done | bytes 1048608 | tf_op jit(solution)/shard_map/ppermute | solution.py:282
  48.3 2.4 %collective-permute-start.5 = (bf16[4,128,1024]{2,1,0:T(8,128)(2,1)}, bf16[4,128,1024]{2,1,0:T(8,128)(2,1)}, u32[]{:S(2)}, u32[]{:S(2)}) collective-permute-start(bf16[4,128,1024]{2,1,0:T(8,128)(2,1)} %get-tuple-element.58), channel_id=1, source_target_pairs={{0,8},{8,32},{16,24},{24,48},{32,40},{40,64},{48,56},{56,80},{64,7... | collective-permute-start | bytes 3145736 | tf_op jit(solution)/shard_map/ppermute | solution.py:282
  51.4 2.6 %collective-permute-done.3.halo_ref.spare_ref = bf16[22,128,128]{2,1,0:T(8,128)(2,1)S(1)} collective-permute-done((bf16[22,128,128]{2,1,0:T(8,128)(2,1)}, bf16[22,128,128]{2,1,0:T(8,128)(2,1)S(1)}, u32[]{:S(2)}, u32[]{:S(2)}) %collective-permute-start.3) | collective-permute-done | bytes 720928 | tf_op jit(solution)/shard_map/ppermute | solution.py:315
  58.8 5.2 %pieces.8 = (f32[4,4,128,128]{3,2,1,0:T(8,128)S(1)}, f32[4,4,128,128]{3,2,1,0:T(8,128)S(1)}) custom-call(s32[4]{0:T(128)S(1)} %get-tuple-element.102.index_ref, s32[8]{0:T(128)S(1)} %and_select_fusion.1.lag_ref, bf16[16,128,1024]{2,1,0:T(8,128)(2,1)S(1)} %copy-done.1, bf16[22,128,128]{2,1,0:T(8,128)(2,1)S(1)} %collective-permute-done.3.halo_ref.spare_ref, ...), custom_call_target="tpu_custom_call" | custom-call | flops 1 | bytes 1 | tf_op jit(solution)/shard_map/pieces/pallas_call | solution.py:200
  66.3 6.1 %pieces.9 = (f32[4,4,128,128]{3,2,1,0:T(8,128)S(1)}, f32[4,4,128,128]{3,2,1,0:T(8,128)S(1)}) custom-call(s32[4]{0:T(128)S(1)} %get-tuple-element.101.index_ref, s32[8]{0:T(128)S(1)} %and_select_fusion.lag_ref, bf16[16,128,1024]{2,1,0:T(8,128)(2,1)S(1)} %copy-done.1, bf16[22,128,128]{2,1,0:T(8,128)(2,1)S(1)} %collective-permute-done.3.halo_ref.spare_ref, ...), custom_call_target="tpu_custom_call" | custom-call | flops 1 | bytes 1 | tf_op jit(solution)/shard_map/pieces/pallas_call | solution.py:200
  73.5 16.1 %collective-permute-done.7.one_ref.refs_1_ = f32[4,4,128,128]{3,2,1,0:T(8,128)S(1)} collective-permute-done((f32[4,4,128,128]{3,2,1,0:T(8,128)S(1)}, f32[4,4,128,128]{3,2,1,0:T(8,128)S(1)}, u32[]{:S(2)}, u32[]{:S(2)}) %collective-permute-start.7) | collective-permute-done | bytes 1048608 | tf_op jit(solution)/shard_map/ppermute | solution.py:270
  91.8 6.0 %collective-permute-done.6.one_ref.refs_4_ = f32[4,4,128,128]{3,2,1,0:T(8,128)S(1)} collective-permute-done((f32[4,4,128,128]{3,2,1,0:T(8,128)S(1)}, f32[4,4,128,128]{3,2,1,0:T(8,128)S(1)}, u32[]{:S(2)}, u32[]{:S(2)}) %collective-permute-start.6) | collective-permute-done | bytes 1048608 | tf_op jit(solution)/shard_map/ppermute | solution.py:270
  98.2 9.6 %collective-permute-start.8 = (bf16[4,128,1024]{2,1,0:T(8,128)(2,1)S(1)}, bf16[4,128,1024]{2,1,0:T(8,128)(2,1)S(1)}, u32[]{:S(2)}, u32[]{:S(2)}) collective-permute-start(bf16[4,128,1024]{2,1,0:T(8,128)(2,1)S(1)} %copy-done.7), channel_id=1, source_target_pairs={{0,24},{8,16},{16,40},{24,32},{32,56},{40,48},{48,72},{56,64},{64,... | collective-permute-start | bytes 3145736 | tf_op jit(solution)/shard_map/ppermute | solution.py:282
  107.9 6.3 %collective-permute-done.9.b_ref = bf16[8,128,1024]{2,1,0:T(8,128)(2,1)S(1)} collective-permute-done((bf16[8,128,1024]{2,1,0:T(8,128)(2,1)}, bf16[8,128,1024]{2,1,0:T(8,128)(2,1)S(1)}, u32[]{:S(2)}, u32[]{:S(2)}) %collective-permute-start.9) | collective-permute-done | bytes 2097184 | tf_op jit(solution)/shard_map/ppermute | solution.py:282
  114.2 5.2 %pieces.10 = (f32[4,4,128,128]{3,2,1,0:T(8,128)S(1)}, f32[4,4,128,128]{3,2,1,0:T(8,128)S(1)}) custom-call(s32[4]{0:T(128)S(1)} %get-tuple-element.100.index_ref, s32[8]{0:T(128)S(1)} %and_select_fusion.1.lag_ref, bf16[16,128,1024]{2,1,0:T(8,128)(2,1)S(1)} %copy-done.2, bf16[22,128,128]{2,1,0:T(8,128)(2,1)S(1)} %collective-permute-done.3.halo_ref.spare_ref, ...), custom_call_target="tpu_custom_call" | custom-call | flops 1 | bytes 1 | tf_op jit(solution)/shard_map/pieces/pallas_call | solution.py:200
  120.0 5.2 %pieces.11 = (f32[4,4,128,128]{3,2,1,0:T(8,128)S(1)}, f32[4,4,128,128]{3,2,1,0:T(8,128)S(1)}) custom-call(s32[4]{0:T(128)S(1)} %get-tuple-element.99.index_ref, s32[8]{0:T(128)S(1)} %and_select_fusion.lag_ref, bf16[16,128,1024]{2,1,0:T(8,128)(2,1)S(1)} %copy-done.2, bf16[22,128,128]{2,1,0:T(8,128)(2,1)S(1)} %collective-permute-done.3.halo_ref.spare_ref, ...), custom_call_target="tpu_custom_call" | custom-call | flops 1 | bytes 1 | tf_op jit(solution)/shard_map/pieces/pallas_call | solution.py:200
  125.2 3.1 %collective-permute-start.14 = (f32[4,4,128,128]{3,2,1,0:T(8,128)S(1)}, f32[4,4,128,128]{3,2,1,0:T(8,128)S(1)}, u32[]{:S(2)}, u32[]{:S(2)}) collective-permute-start(f32[4,4,128,128]{3,2,1,0:T(8,128)S(1)} %get-tuple-element.75), channel_id=1, source_target_pairs={{0,3},{1,2},{2,1},{3,0},{4,7},{5,6},{6,5},{7,4},{8,11},{9,10},{10,... | collective-permute-start | bytes 3145736 | tf_op jit(solution)/shard_map/ppermute | solution.py:270
  128.4 2.5 %collective-permute-done.8.b_ref = bf16[4,128,1024]{2,1,0:T(8,128)(2,1)S(1)} collective-permute-done((bf16[4,128,1024]{2,1,0:T(8,128)(2,1)S(1)}, bf16[4,128,1024]{2,1,0:T(8,128)(2,1)S(1)}, u32[]{:S(2)}, u32[]{:S(2)}) %collective-permute-start.8) | collective-permute-done | bytes 1048608 | tf_op jit(solution)/shard_map/ppermute | solution.py:282
  130.9 2.9 %pieces.12 = (f32[4,2,128,128]{3,2,1,0:T(8,128)S(1)}, f32[4,2,128,128]{3,2,1,0:T(8,128)S(1)}) custom-call(s32[2]{0:T(128)S(1)} %get-tuple-element.98.index_ref, s32[8]{0:T(128)S(1)} %and_select_fusion.1.lag_ref, bf16[16,128,1024]{2,1,0:T(8,128)(2,1)S(1)} %copy-done.2, bf16[22,128,128]{2,1,0:T(8,128)(2,1)S(1)} %collective-permute-done.3.halo_ref.spare_ref, ...), custom_call_target="tpu_custom_call" | custom-call | flops 1 | bytes 1 | tf_op jit(solution)/shard_map/pieces/pallas_call | solution.py:200
  135.7 2.9 %pieces.13 = (f32[4,2,128,128]{3,2,1,0:T(8,128)S(1)}, f32[4,2,128,128]{3,2,1,0:T(8,128)S(1)}) custom-call(s32[2]{0:T(128)S(1)} %get-tuple-element.95.index_ref, s32[8]{0:T(128)S(1)} %and_select_fusion.lag_ref, bf16[16,128,1024]{2,1,0:T(8,128)(2,1)S(1)} %copy-done.2, bf16[22,128,128]{2,1,0:T(8,128)(2,1)S(1)} %collective-permute-done.3.halo_ref.spare_ref, ...), custom_call_target="tpu_custom_call" | custom-call | flops 1 | bytes 1 | tf_op jit(solution)/shard_map/pieces/pallas_call | solution.py:200
  141.7 3.7 %collective-permute-done.14.one_ref.refs_4_ = f32[4,4,128,128]{3,2,1,0:T(8,128)S(1)} collective-permute-done((f32[4,4,128,128]{3,2,1,0:T(8,128)S(1)}, f32[4,4,128,128]{3,2,1,0:T(8,128)S(1)}, u32[]{:S(2)}, u32[]{:S(2)}) %collective-permute-start.14) | collective-permute-done | bytes 1048608 | tf_op jit(solution)/shard_map/ppermute | solution.py:270
  145.9 10.4 %collective-permute-done.13.b_ref = bf16[4,128,1024]{2,1,0:T(8,128)(2,1)S(1)} collective-permute-done((bf16[4,128,1024]{2,1,0:T(8,128)(2,1)S(1)}, bf16[4,128,1024]{2,1,0:T(8,128)(2,1)S(1)}, u32[]{:S(2)}, u32[]{:S(2)}) %collective-permute-start.13) | collective-permute-done | bytes 1048608 | tf_op jit(solution)/shard_map/ppermute | solution.py:282
  156.3 2.9 %pieces.14 = (f32[4,2,128,128]{3,2,1,0:T(8,128)S(1)}, f32[4,2,128,128]{3,2,1,0:T(8,128)S(1)}) custom-call(s32[2]{0:T(128)S(1)} %get-tuple-element.96.index_ref, s32[8]{0:T(128)S(1)} %and_select_fusion.1.lag_ref, bf16[16,128,1024]{2,1,0:T(8,128)(2,1)S(1)} %copy-done.2, bf16[22,128,128]{2,1,0:T(8,128)(2,1)S(1)} %collective-permute-done.3.halo_ref.spare_ref, ...), custom_call_target="tpu_custom_call" | custom-call | flops 1 | bytes 1 | tf_op jit(solution)/shard_map/pieces/pallas_call | solution.py:200
  160.0 2.9 %pieces.15 = (f32[4,2,128,128]{3,2,1,0:T(8,128)S(1)}, f32[4,2,128,128]{3,2,1,0:T(8,128)S(1)}) custom-call(s32[2]{0:T(128)S(1)} %get-tuple-element.97.index_ref, s32[8]{0:T(128)S(1)} %and_select_fusion.lag_ref, bf16[16,128,1024]{2,1,0:T(8,128)(2,1)S(1)} %copy-done.2, bf16[22,128,128]{2,1,0:T(8,128)(2,1)S(1)} %collective-permute-done.3.halo_ref.spare_ref, ...), custom_call_target="tpu_custom_call" | custom-call | flops 1 | bytes 1 | tf_op jit(solution)/shard_map/pieces/pallas_call | solution.py:200
  163.9 2.5 %collective-permute-start.27 = (f32[2,4,128,128]{3,2,1,0:T(8,128)S(1)}, f32[2,4,128,128]{3,2,1,0:T(8,128)S(1)}, u32[]{:S(2)}, u32[]{:S(2)}) collective-permute-start(f32[2,4,128,128]{3,2,1,0:T(8,128)S(1)} %get-tuple-element.87), channel_id=1, source_target_pairs={{0,4},{1,5},{2,6},{3,7},{4,0},{5,1},{6,2},{7,3},{8,12},{9,13},{10,... | collective-permute-start | bytes 1572872 | tf_op jit(solution)/shard_map/ppermute | solution.py:270
  167.9 6.6 %collective-permute-start.26 = (f32[2,4,128,128]{3,2,1,0:T(8,128)S(1)}, f32[2,4,128,128]{3,2,1,0:T(8,128)S(1)}, u32[]{:S(2)}, u32[]{:S(2)}) collective-permute-start(f32[2,4,128,128]{3,2,1,0:T(8,128)S(1)} %get-tuple-element.86), channel_id=1, source_target_pairs={{0,4},{1,5},{2,6},{3,7},{4,0},{5,1},{6,2},{7,3},{8,12},{9,13},{10,... | collective-permute-start | bytes 1572872 | tf_op jit(solution)/shard_map/ppermute | solution.py:270
  176.0 2.6 %collective-permute-done.19.one_ref.refs_4_ = f32[4,2,128,128]{3,2,1,0:T(8,128)S(1)} collective-permute-done((f32[4,2,128,128]{3,2,1,0:T(8,128)S(1)}, f32[4,2,128,128]{3,2,1,0:T(8,128)S(1)}, u32[]{:S(2)}, u32[]{:S(2)}) %collective-permute-start.19) | collective-permute-done | bytes 524320 | tf_op jit(solution)/shard_map/ppermute | solution.py:270
  178.8 4.0 %collective-permute-done.18.refs_5_ = f32[2,2,128,128]{3,2,1,0:T(8,128)S(1)} collective-permute-done((f32[2,2,128,128]{3,2,1,0:T(8,128)S(1)}, f32[2,2,128,128]{3,2,1,0:T(8,128)S(1)}, u32[]{:S(2)}, u32[]{:S(2)}) %collective-permute-start.18) | collective-permute-done | bytes 262176 | tf_op jit(solution)/shard_map/ppermute | solution.py:270
  185.0 6.1 %collective-permute-start.23 = (f32[2,2,128,128]{3,2,1,0:T(8,128)S(1)}, f32[2,2,128,128]{3,2,1,0:T(8,128)S(1)}, u32[]{:S(2)}, u32[]{:S(2)}) collective-permute-start(f32[2,2,128,128]{3,2,1,0:T(8,128)S(1)} %get-tuple-element.85), channel_id=1, source_target_pairs={{0,4},{1,5},{2,6},{3,7},{4,0},{5,1},{6,2},{7,3},{8,12},{9,13},{10,... | collective-permute-start | bytes 786440 | tf_op jit(solution)/shard_map/ppermute | solution.py:270
  192.0 4.0 %collective-permute-start.28 = (f32[2,2,128,128]{3,2,1,0:T(8,128)S(1)}, f32[2,2,128,128]{3,2,1,0:T(8,128)S(1)}, u32[]{:S(2)}, u32[]{:S(2)}) collective-permute-start(f32[2,2,128,128]{3,2,1,0:T(8,128)S(1)} %get-tuple-element.89), channel_id=1, source_target_pairs={{0,4},{1,5},{2,6},{3,7},{4,0},{5,1},{6,2},{7,3},{8,12},{9,13},{10,... | collective-permute-start | bytes 786440 | tf_op jit(solution)/shard_map/ppermute | solution.py:270
  197.2 5.3 %collective-permute-done.28.three_ref = f32[2,2,128,128]{3,2,1,0:T(8,128)S(1)} collective-permute-done((f32[2,2,128,128]{3,2,1,0:T(8,128)S(1)}, f32[2,2,128,128]{3,2,1,0:T(8,128)S(1)}, u32[]{:S(2)}, u32[]{:S(2)}) %collective-permute-start.28) | collective-permute-done | bytes 262176 | tf_op jit(solution)/shard_map/ppermute | solution.py:270
  (93 shorter events, 37.6 us)
Async XLA Ops:
  0.0 50.8 %copy-start = (s32[8]{0:T(128)S(1)}, s32[8]{0:T(128)}, u32[]{:S(2)}) copy-start(s32[8]{0:T(128)} %param.6) | copy-start | bytes 100
  5.9 16.1 %all-to-all-start = ((f32[8,32,128]{2,1,0:T(8,128)}), f32[8,32,128]{2,1,0:T(8,128)S(1)}, u32[]{:S(2)}, u32[]{:S(2)}) async-start(f32[8,32,128]{2,1,0:T(8,128)} %local_sums.1), calls=%async_computation | async-start | bytes 262144 | tf_op jit(solution)/shard_map/all_to_all | solution.py:301
  14.2 4.9 %collective-permute-start = (s32[8]{0:T(128)S(1)}, s32[8]{0:T(128)S(1)}, u32[]{:S(2)}, u32[]{:S(2)}) collective-permute-start(s32[8]{0:T(128)S(1)} %slice_bitcast_fusion.10), channel_id=1, source_target_pairs={{0,104},{8,0},{16,120},{24,16},{32,8},{40,32},{48,24},{56,48},{64,... | collective-permute-start | bytes 104 | tf_op jit(solution)/shard_map/ppermute | solution.py:282
  15.2 3.9 %collective-permute-start.1 = (s32[8]{0:T(128)S(1)}, s32[8]{0:T(128)S(1)}, u32[]{:S(2)}, u32[]{:S(2)}) collective-permute-start(s32[8]{0:T(128)S(1)} %get-tuple-element.49), channel_id=1, source_target_pairs={{0,112},{8,120},{16,0},{24,8},{32,16},{40,24},{48,32},{56,40},{64,... | collective-permute-start | bytes 104 | tf_op jit(solution)/shard_map/ppermute | solution.py:282
  18.1 3.3 %collective-permute-start.2 = (s32[8]{0:T(128)S(1)}, s32[8]{0:T(128)S(1)}, u32[]{:S(2)}, u32[]{:S(2)}) collective-permute-start(s32[8]{0:T(128)S(1)} %get-tuple-element.50), channel_id=1, source_target_pairs={{0,120},{8,112},{16,8},{24,0},{32,24},{40,16},{48,40},{56,32},{64,... | collective-permute-start | bytes 104 | tf_op jit(solution)/shard_map/ppermute | solution.py:282
  32.9 14.4 %collective-permute-start.4 = (bf16[4,128,1024]{2,1,0:T(8,128)(2,1)}, bf16[4,128,1024]{2,1,0:T(8,128)(2,1)S(1)}, u32[]{:S(2)}, u32[]{:S(2)}) collective-permute-start(bf16[4,128,1024]{2,1,0:T(8,128)(2,1)} %get-tuple-element.56), channel_id=1, source_target_pairs={{0,8},{8,32},{16,24},{24,48},{32,40},{40,64},{48,56},{56,80},{64,7... | collective-permute-start | bytes 3145736 | tf_op jit(solution)/shard_map/ppermute | solution.py:282
  35.6 18.5 %collective-permute-start.3 = (bf16[22,128,128]{2,1,0:T(8,128)(2,1)}, bf16[22,128,128]{2,1,0:T(8,128)(2,1)S(1)}, u32[]{:S(2)}, u32[]{:S(2)}) collective-permute-start(bf16[22,128,128]{2,1,0:T(8,128)(2,1)} %get-tuple-element.53), channel_id=1, source_target_pairs={{0,1},{1,2},{2,3},{3,4},{4,5},{5,6},{6,7},{8,9},{9,10},{10,11},{11... | collective-permute-start | bytes 2162696 | tf_op jit(solution)/shard_map/ppermute | solution.py:315
  48.3 17.9 %collective-permute-start.5 = (bf16[4,128,1024]{2,1,0:T(8,128)(2,1)}, bf16[4,128,1024]{2,1,0:T(8,128)(2,1)}, u32[]{:S(2)}, u32[]{:S(2)}) collective-permute-start(bf16[4,128,1024]{2,1,0:T(8,128)(2,1)} %get-tuple-element.58), channel_id=1, source_target_pairs={{0,8},{8,32},{16,24},{24,48},{32,40},{40,64},{48,56},{56,80},{64,7... | collective-permute-start | bytes 3145736 | tf_op jit(solution)/shard_map/ppermute | solution.py:282
  54.1 60.1 %collective-permute-start.9 = (bf16[8,128,1024]{2,1,0:T(8,128)(2,1)}, bf16[8,128,1024]{2,1,0:T(8,128)(2,1)S(1)}, u32[]{:S(2)}, u32[]{:S(2)}) collective-permute-start(bf16[8,128,1024]{2,1,0:T(8,128)(2,1)} %get-tuple-element.67), channel_id=1, source_target_pairs={{0,16},{8,24},{16,32},{24,40},{32,48},{40,56},{48,64},{56,72},{64,... | collective-permute-start | bytes 6291464 | tf_op jit(solution)/shard_map/ppermute | solution.py:282
  64.0 25.7 %collective-permute-start.7 = (f32[4,4,128,128]{3,2,1,0:T(8,128)S(1)}, f32[4,4,128,128]{3,2,1,0:T(8,128)S(1)}, u32[]{:S(2)}, u32[]{:S(2)}) collective-permute-start(f32[4,4,128,128]{3,2,1,0:T(8,128)S(1)} %get-tuple-element.63), channel_id=1, source_target_pairs={{0,1},{1,0},{2,3},{3,2},{4,5},{5,4},{6,7},{7,6},{8,9},{9,8},{10,11... | collective-permute-start | bytes 3145736 | tf_op jit(solution)/shard_map/ppermute | solution.py:270
  72.4 25.5 %collective-permute-start.6 = (f32[4,4,128,128]{3,2,1,0:T(8,128)S(1)}, f32[4,4,128,128]{3,2,1,0:T(8,128)S(1)}, u32[]{:S(2)}, u32[]{:S(2)}) collective-permute-start(f32[4,4,128,128]{3,2,1,0:T(8,128)S(1)} %get-tuple-element.62), channel_id=1, source_target_pairs={{0,3},{1,2},{2,1},{3,0},{4,7},{5,6},{6,5},{7,4},{8,11},{9,10},{10,... | collective-permute-start | bytes 3145736 | tf_op jit(solution)/shard_map/ppermute | solution.py:270
  89.6 24.5 %copy-start.2 = (bf16[16,128,1024]{2,1,0:T(8,128)(2,1)S(1)}, bf16[16,128,1024]{2,1,0:T(8,128)(2,1)}, u32[]{:S(2)}) copy-start(bf16[16,128,1024]{2,1,0:T(8,128)(2,1)} %get-tuple-element.52.a_ref.refs_0_) | copy-start | bytes 12582916
  89.9 29.5 %collective-permute-start.10 = (f32[2,4,128,128]{3,2,1,0:T(8,128)S(1)}, f32[2,4,128,128]{3,2,1,0:T(8,128)S(1)}, u32[]{:S(2)}, u32[]{:S(2)}) collective-permute-start(f32[2,4,128,128]{3,2,1,0:T(8,128)S(1)} %forward.8.refs_0_), channel_id=1, source_target_pairs={{0,3},{1,2},{2,1},{3,0},{4,7},{5,6},{6,5},{7,4},{8,11},{9,10},{10,... | collective-permute-start | bytes 1572872 | tf_op jit(solution)/shard_map/ppermute | solution.py:270
  98.1 21.3 %collective-permute-start.11 = (f32[2,4,128,128]{3,2,1,0:T(8,128)S(1)}, f32[2,4,128,128]{3,2,1,0:T(8,128)S(1)}, u32[]{:S(2)}, u32[]{:S(2)}) collective-permute-start(f32[2,4,128,128]{3,2,1,0:T(8,128)S(1)} %forward.9.refs_0_), channel_id=1, source_target_pairs={{0,1},{1,0},{2,3},{3,2},{4,5},{5,4},{6,7},{7,6},{8,9},{9,8},{10,11... | collective-permute-start | bytes 1572872 | tf_op jit(solution)/shard_map/ppermute | solution.py:270
  98.2 32.7 %collective-permute-start.8 = (bf16[4,128,1024]{2,1,0:T(8,128)(2,1)S(1)}, bf16[4,128,1024]{2,1,0:T(8,128)(2,1)S(1)}, u32[]{:S(2)}, u32[]{:S(2)}) collective-permute-start(bf16[4,128,1024]{2,1,0:T(8,128)(2,1)S(1)} %copy-done.7), channel_id=1, source_target_pairs={{0,24},{8,16},{16,40},{24,32},{32,56},{40,48},{48,72},{56,64},{64,... | collective-permute-start | bytes 3145736 | tf_op jit(solution)/shard_map/ppermute | solution.py:282
  119.3 19.8 %collective-permute-start.15 = (f32[4,4,128,128]{3,2,1,0:T(8,128)S(1)}, f32[4,4,128,128]{3,2,1,0:T(8,128)S(1)}, u32[]{:S(2)}, u32[]{:S(2)}) collective-permute-start(f32[4,4,128,128]{3,2,1,0:T(8,128)S(1)} %get-tuple-element.76), channel_id=1, source_target_pairs={{0,1},{1,0},{2,3},{3,2},{4,5},{5,4},{6,7},{7,6},{8,9},{9,8},{10,11... | collective-permute-start | bytes 3145736 | tf_op jit(solution)/shard_map/ppermute | solution.py:270
  125.2 20.2 %collective-permute-start.14 = (f32[4,4,128,128]{3,2,1,0:T(8,128)S(1)}, f32[4,4,128,128]{3,2,1,0:T(8,128)S(1)}, u32[]{:S(2)}, u32[]{:S(2)}) collective-permute-start(f32[4,4,128,128]{3,2,1,0:T(8,128)S(1)} %get-tuple-element.75), channel_id=1, source_target_pairs={{0,3},{1,2},{2,1},{3,0},{4,7},{5,6},{6,5},{7,4},{8,11},{9,10},{10,... | collective-permute-start | bytes 3145736 | tf_op jit(solution)/shard_map/ppermute | solution.py:270
  128.3 27.9 %collective-permute-start.13 = (bf16[4,128,1024]{2,1,0:T(8,128)(2,1)S(1)}, bf16[4,128,1024]{2,1,0:T(8,128)(2,1)S(1)}, u32[]{:S(2)}, u32[]{:S(2)}) collective-permute-start(bf16[4,128,1024]{2,1,0:T(8,128)(2,1)S(1)} %copy-done.6), channel_id=1, source_target_pairs={{0,24},{8,16},{16,40},{24,32},{32,56},{40,48},{48,72},{56,64},{64,... | collective-permute-start | bytes 3145736 | tf_op jit(solution)/shard_map/ppermute | solution.py:282
  133.8 29.1 %collective-permute-start.12 = (f32[4,2,128,128]{3,2,1,0:T(8,128)S(1)}, f32[4,2,128,128]{3,2,1,0:T(8,128)S(1)}, u32[]{:S(2)}, u32[]{:S(2)}) collective-permute-start(f32[4,2,128,128]{3,2,1,0:T(8,128)S(1)} %get-tuple-element.73), channel_id=1, source_target_pairs={{0,1},{1,0},{2,3},{3,2},{4,5},{5,4},{6,7},{7,6},{8,9},{9,8},{10,11... | collective-permute-start | bytes 1572872 | tf_op jit(solution)/shard_map/ppermute | solution.py:270
  138.6 25.3 %collective-permute-start.17 = (f32[4,2,128,128]{3,2,1,0:T(8,128)S(1)}, f32[4,2,128,128]{3,2,1,0:T(8,128)S(1)}, u32[]{:S(2)}, u32[]{:S(2)}) collective-permute-start(f32[4,2,128,128]{3,2,1,0:T(8,128)S(1)} %get-tuple-element.80), channel_id=1, source_target_pairs={{0,3},{1,2},{2,1},{3,0},{4,7},{5,6},{6,5},{7,4},{8,11},{9,10},{10,... | collective-permute-start | bytes 1572872 | tf_op jit(solution)/shard_map/ppermute | solution.py:270
  139.4 27.9 %collective-permute-start.21 = (f32[2,4,128,128]{3,2,1,0:T(8,128)S(1)}, f32[2,4,128,128]{3,2,1,0:T(8,128)S(1)}, u32[]{:S(2)}, u32[]{:S(2)}) collective-permute-start(f32[2,4,128,128]{3,2,1,0:T(8,128)S(1)} %forward.10.refs_0_), channel_id=1, source_target_pairs={{0,3},{1,2},{2,1},{3,0},{4,7},{5,6},{6,5},{7,4},{8,11},{9,10},{10,... | collective-permute-start | bytes 1572872 | tf_op jit(solution)/shard_map/ppermute | solution.py:270
  145.7 21.7 %collective-permute-start.22 = (f32[2,4,128,128]{3,2,1,0:T(8,128)S(1)}, f32[2,4,128,128]{3,2,1,0:T(8,128)S(1)}, u32[]{:S(2)}, u32[]{:S(2)}) collective-permute-start(f32[2,4,128,128]{3,2,1,0:T(8,128)S(1)} %forward.11.refs_0_), channel_id=1, source_target_pairs={{0,1},{1,0},{2,3},{3,2},{4,5},{5,4},{6,7},{7,6},{8,9},{9,8},{10,11... | collective-permute-start | bytes 1572872 | tf_op jit(solution)/shard_map/ppermute | solution.py:270
  159.1 16.7 %collective-permute-start.20 = (f32[4,2,128,128]{3,2,1,0:T(8,128)S(1)}, f32[4,2,128,128]{3,2,1,0:T(8,128)S(1)}, u32[]{:S(2)}, u32[]{:S(2)}) collective-permute-start(f32[4,2,128,128]{3,2,1,0:T(8,128)S(1)} %get-tuple-element.82), channel_id=1, source_target_pairs={{0,1},{1,0},{2,3},{3,2},{4,5},{5,4},{6,7},{7,6},{8,9},{9,8},{10,11... | collective-permute-start | bytes 1572872 | tf_op jit(solution)/shard_map/ppermute | solution.py:270
  162.9 15.6 %collective-permute-start.19 = (f32[4,2,128,128]{3,2,1,0:T(8,128)S(1)}, f32[4,2,128,128]{3,2,1,0:T(8,128)S(1)}, u32[]{:S(2)}, u32[]{:S(2)}) collective-permute-start(f32[4,2,128,128]{3,2,1,0:T(8,128)S(1)} %get-tuple-element.81), channel_id=1, source_target_pairs={{0,3},{1,2},{2,1},{3,0},{4,7},{5,6},{6,5},{7,4},{8,11},{9,10},{10,... | collective-permute-start | bytes 1572872 | tf_op jit(solution)/shard_map/ppermute | solution.py:270
  163.9 27.2 %collective-permute-start.27 = (f32[2,4,128,128]{3,2,1,0:T(8,128)S(1)}, f32[2,4,128,128]{3,2,1,0:T(8,128)S(1)}, u32[]{:S(2)}, u32[]{:S(2)}) collective-permute-start(f32[2,4,128,128]{3,2,1,0:T(8,128)S(1)} %get-tuple-element.87), channel_id=1, source_target_pairs={{0,4},{1,5},{2,6},{3,7},{4,0},{5,1},{6,2},{7,3},{8,12},{9,13},{10,... | collective-permute-start | bytes 1572872 | tf_op jit(solution)/shard_map/ppermute | solution.py:270
  167.9 23.5 %collective-permute-start.26 = (f32[2,4,128,128]{3,2,1,0:T(8,128)S(1)}, f32[2,4,128,128]{3,2,1,0:T(8,128)S(1)}, u32[]{:S(2)}, u32[]{:S(2)}) collective-permute-start(f32[2,4,128,128]{3,2,1,0:T(8,128)S(1)} %get-tuple-element.86), channel_id=1, source_target_pairs={{0,4},{1,5},{2,6},{3,7},{4,0},{5,1},{6,2},{7,3},{8,12},{9,13},{10,... | collective-permute-start | bytes 1572872 | tf_op jit(solution)/shard_map/ppermute | solution.py:270
  174.5 8.3 %collective-permute-start.18 = (f32[2,2,128,128]{3,2,1,0:T(8,128)S(1)}, f32[2,2,128,128]{3,2,1,0:T(8,128)S(1)}, u32[]{:S(2)}, u32[]{:S(2)}) collective-permute-start(f32[2,2,128,128]{3,2,1,0:T(8,128)S(1)} %forward.13.refs_6_), channel_id=1, source_target_pairs={{0,1},{1,0},{2,3},{3,2},{4,5},{5,4},{6,7},{7,6},{8,9},{9,8},{10,11... | collective-permute-start | bytes 786440 | tf_op jit(solution)/shard_map/ppermute | solution.py:270
  175.8 8.9 %collective-permute-start.16 = (f32[2,2,128,128]{3,2,1,0:T(8,128)S(1)}, f32[2,2,128,128]{3,2,1,0:T(8,128)S(1)}, u32[]{:S(2)}, u32[]{:S(2)}) collective-permute-start(f32[2,2,128,128]{3,2,1,0:T(8,128)S(1)} %forward.12.refs_0_), channel_id=1, source_target_pairs={{0,3},{1,2},{2,1},{3,0},{4,7},{5,6},{6,5},{7,4},{8,11},{9,10},{10,... | collective-permute-start | bytes 786440 | tf_op jit(solution)/shard_map/ppermute | solution.py:270
  178.7 13.0 %collective-permute-start.25 = (f32[2,2,128,128]{3,2,1,0:T(8,128)S(1)}, f32[2,2,128,128]{3,2,1,0:T(8,128)S(1)}, u32[]{:S(2)}, u32[]{:S(2)}) collective-permute-start(f32[2,2,128,128]{3,2,1,0:T(8,128)S(1)} %forward.15.refs_6_), channel_id=1, source_target_pairs={{0,1},{1,0},{2,3},{3,2},{4,5},{5,4},{6,7},{7,6},{8,9},{9,8},{10,11... | collective-permute-start | bytes 786440 | tf_op jit(solution)/shard_map/ppermute | solution.py:270
  182.8 8.9 %collective-permute-start.24 = (f32[2,2,128,128]{3,2,1,0:T(8,128)S(1)}, f32[2,2,128,128]{3,2,1,0:T(8,128)S(1)}, u32[]{:S(2)}, u32[]{:S(2)}) collective-permute-start(f32[2,2,128,128]{3,2,1,0:T(8,128)S(1)} %forward.14.refs_0_), channel_id=1, source_target_pairs={{0,3},{1,2},{2,1},{3,0},{4,7},{5,6},{6,5},{7,4},{8,11},{9,10},{10,... | collective-permute-start | bytes 786440 | tf_op jit(solution)/shard_map/ppermute | solution.py:270
  185.0 12.0 %collective-permute-start.23 = (f32[2,2,128,128]{3,2,1,0:T(8,128)S(1)}, f32[2,2,128,128]{3,2,1,0:T(8,128)S(1)}, u32[]{:S(2)}, u32[]{:S(2)}) collective-permute-start(f32[2,2,128,128]{3,2,1,0:T(8,128)S(1)} %get-tuple-element.85), channel_id=1, source_target_pairs={{0,4},{1,5},{2,6},{3,7},{4,0},{5,1},{6,2},{7,3},{8,12},{9,13},{10,... | collective-permute-start | bytes 786440 | tf_op jit(solution)/shard_map/ppermute | solution.py:270
  192.0 10.5 %collective-permute-start.28 = (f32[2,2,128,128]{3,2,1,0:T(8,128)S(1)}, f32[2,2,128,128]{3,2,1,0:T(8,128)S(1)}, u32[]{:S(2)}, u32[]{:S(2)}) collective-permute-start(f32[2,2,128,128]{3,2,1,0:T(8,128)S(1)} %get-tuple-element.89), channel_id=1, source_target_pairs={{0,4},{1,5},{2,6},{3,7},{4,0},{5,1},{6,2},{7,3},{8,12},{9,13},{10,... | collective-permute-start | bytes 786440 | tf_op jit(solution)/shard_map/ppermute | solution.py:270
  (6 other events, 21.7 us)

commit v6 on v5

--- a/solution.py
+++ b/solution.py
@@ -159,6 +159,43 @@
     )(index, blocks, norm)
 
 
+def rows_kernel(counts, start, index_ref, scaled_ref, *refs):
+    send_refs, (held, came, went) = refs[:len(counts)], refs[len(counts):]
+    places = [send_ref.at[i] for send_ref, count in zip(send_refs, counts) for i in range(count)]
+
+    def arriving(i):
+        return pltpu.make_async_copy(scaled_ref.at[index_ref[start + i]], held.at[i], came.at[i])
+
+    def leaving(i):
+        return pltpu.make_async_copy(held.at[i], places[i], went.at[i])
+
+    for i in range(len(places)):
+        arriving(i).start()
+    for i in range(len(places)):
+        arriving(i).wait()
+        leaving(i).start()
+    for i in range(len(places)):
+        leaving(i).wait()
+
+
+def picked_rows(index, counts, start, scaled):
+    shapes = [jax.ShapeDtypeStruct((count,) + scaled.shape[1:], scaled.dtype) for count in counts]
+    return pl.pallas_call(
+        functools.partial(rows_kernel, counts, start),
+        in_specs=[pl.BlockSpec(memory_space=pltpu.SMEM), pl.BlockSpec(memory_space=pl.ANY)],
+        out_specs=[pl.BlockSpec(memory_space=pl.ANY)] * len(shapes),
+        out_shape=shapes,
+        scratch_shapes=[
+            pltpu.VMEM((sum(counts),) + scaled.shape[1:], scaled.dtype),
+            pltpu.SemaphoreType.DMA((sum(counts),)),
+            pltpu.SemaphoreType.DMA((sum(counts),)),
+        ],
+        compiler_params=pltpu.CompilerParams(vmem_limit_bytes=MANY),
+        cost_estimate=pl.CostEstimate(flops=1, bytes_accessed=1, transcendentals=0),
+        name="picked_rows",
+    )(index, scaled)
+
+
 def piece_kernel(index_ref, lag_ref, a_ref, halo_ref, spare_ref, b_ref, *refs):
     keep_ref, send_ref, long_ref, shift_ref = refs[-4:]
     hours = a_ref.shape[2]
@@ -311,9 +348,10 @@
     lag_slots = [jnp.take(lag_list, (order[:, None] + parts[None, :]).reshape(-1)) for order in orders]
     divisor = (all_hours - lag_slots[0][0]).astype(jnp.float32)
 
-    scaled, tail, *picked = scaled_parts(wanted, (4, 4, 8, 4, 4), blocks, norm)
+    scaled, tail, *picked = scaled_parts(wanted, (4, 4), blocks, norm)
     halo = lax.ppermute(tail, "tm", [(i, i + 1) for i in range(n_tm - 1)])
     beside = along_grid(picked[0], routes[0])
+    picked += picked_rows(wanted, (8, 4, 4), PAIRS, scaled)
     beside, waiting = lax.optimization_barrier((beside, picked[1]))
     beside = [beside, along_grid(waiting, routes[0])]
     halo, waiting = lax.optimization_barrier((halo, picked[2]))

time: 204 us -> 202 us (level)
  waiting for transfers between devices: 74.8 us -> 70.7 us
  Pallas kernels: 52.6 us -> 56 us
    pallas_call x0 -> x1, Pallas kernels: none -> 4.91 us  [picked_rows(): pl.pallas_call(functools.partial(rows_kernel, counts, start), in_specs=[p...]
    ppermute x8, starting transfers between devices: 19.8 us -> 17 us  [along_grid(): lax.ppermute(value, 'grid', [(i, route(i) % n_grid) for i in range(n_grid)])]
    ppermute x1, waiting for transfers between devices: 2.64 us -> 0.01 us  [per_device(): halo = lax.ppermute(tail, 'tm', [(i, i + 1) for i in range(n_tm - 1)])]
    ppermute x20, starting transfers between devices: 35.9 us -> 38 us  [along_tm(): return lax.ppermute(value, 'tm', [(i, target(i)) for i in range(n_tm)])]
  transfers between devices with their start and end apart: 30 -> 30, of which waited for: 15 -> 14; matrix products, arithmetic and copies ran while one was open for 1% -> 1% of each run, Pallas kernels for 18% -> 21%
where the time goes in v6:
time: 202 us
  waiting for transfers between devices  70.7 us (35%)
  starting transfers between devices  65.8 us (33%)
  Pallas kernels  56 us (28%)
  local copies, waits for them, and re-layouts  5.77 us (3%)
  other arithmetic  2.93 us (1%)
    ppermute x20, waiting for transfers between devices, along_tm(): return lax.ppermute(value, 'tm', [(i, target(i)) for i in range(n_tm)])  39.8 us
    ppermute x20, starting transfers between devices, along_tm(): return lax.ppermute(value, 'tm', [(i, target(i)) for i in range(n_tm)])  38 us
    pallas_call x8, Pallas kernels, pieces(): pl.pallas_call(piece_kernel, grid_spec=pltpu.PrefetchScalarGridSpec(num_s...  33 us
    ppermute x8, waiting for transfers between devices, along_grid(): lax.ppermute(value, 'grid', [(i, route(i) % n_grid) for i in range(n_grid)])  30.9 us
    ppermute x8, starting transfers between devices, along_grid(): lax.ppermute(value, 'grid', [(i, route(i) % n_grid) for i in range(n_grid)])  17 us
    all_to_all x1, starting transfers between devices, per_device(): norm = norms(lax.all_to_all(sums, 'tm', 0, 0), all_hours)  8.33 us
    pallas_call x1, Pallas kernels, scaled_parts(): pl.pallas_call(functools.partial(scale_kernel, counts), in_specs=[pl.Bloc...  7.22 us
    pallas_call x1, Pallas kernels, local_sums(): pl.pallas_call(sums_kernel, grid=(steps,), in_specs=[pl.BlockSpec((4 * SU...  5.15 us
  transfers between devices with their start and end apart: 30, of which 14 were waited for; matrix products, arithmetic and copies ran while one was open for 1% of the time, Pallas kernels for 21%

profile of v6, /device:TPU:1, one launch (start us, length us, event | category | flops | bytes accessed | tf_op | source)
XLA Modules:
  0.0 201.6 jit_solution(3887563432001727677)
XLA Ops:
  0.7 5.1 %local_sums.1 = f32[8,32,128]{2,1,0:T(8,128)} custom-call(f32[2048,1024]{1,0:T(8,128)} %x_ref.1), custom_call_target="tpu_custom_call" | custom-call | flops 6291456 | bytes 8388608 | tf_op jit(solution)/shard_map/local_sums/pallas_call | solution.py:40
  5.9 8.3 %all-to-all-start = ((f32[8,32,128]{2,1,0:T(8,128)}), f32[8,32,128]{2,1,0:T(8,128)S(1)}, u32[]{:S(2)}, u32[]{:S(2)}) async-start(f32[8,32,128]{2,1,0:T(8,128)} %local_sums.1), calls=%async_computation | async-start | bytes 262144 | tf_op jit(solution)/shard_map/all_to_all | solution.py:338
  15.2 2.9 %collective-permute-start.1 = (s32[8]{0:T(128)S(1)}, s32[8]{0:T(128)S(1)}, u32[]{:S(2)}, u32[]{:S(2)}) collective-permute-start(s32[8]{0:T(128)S(1)} %get-tuple-element.49), channel_id=1, source_target_pairs={{0,112},{8,120},{16,0},{24,8},{32,16},{40,24},{48,32},{56,40},{64,... | collective-permute-start | bytes 104 | tf_op jit(solution)/shard_map/ppermute | solution.py:319
  19.1 2.3 %collective-permute-done.2 = s32[8]{0:T(128)S(1)} collective-permute-done((s32[8]{0:T(128)S(1)}, s32[8]{0:T(128)S(1)}, u32[]{:S(2)}, u32[]{:S(2)}) %collective-permute-start.2) | collective-permute-done | bytes 64 | tf_op jit(solution)/shard_map/ppermute | solution.py:319
  24.2 7.2 %scaled_parts.1 = (bf16[16,128,1024]{2,1,0:T(8,128)(2,1)}, bf16[22,128,128]{2,1,0:T(8,128)(2,1)}, bf16[4,128,1024]{2,1,0:T(8,128)(2,1)}, bf16[4,128,1024]{2,1,0:T(8,128)(2,1)}) custom-call(s32[24]{0:T(128)} %pad_add_fusion.1.index_ref, f32[16,128,1024]{2,1,0:T(8,128)} %bitcast.51, f32[2,16,128]{2,1,0:T(8,128)} %norms.1.norm_ref), custom_call_target="tpu_custom_call" | custom-call | flops 1 | bytes 1 | tf_op jit(solution)/shard_map/scaled_parts/pallas_call | solution.py:137
  31.4 2.4 %collective-permute-start.4 = (bf16[4,128,1024]{2,1,0:T(8,128)(2,1)}, bf16[4,128,1024]{2,1,0:T(8,128)(2,1)S(1)}, u32[]{:S(2)}, u32[]{:S(2)}) collective-permute-start(bf16[4,128,1024]{2,1,0:T(8,128)(2,1)} %get-tuple-element.56), channel_id=1, source_target_pairs={{0,8},{8,32},{16,24},{24,48},{32,40},{40,64},{48,56},{56,80},{64,7... | collective-permute-start | bytes 3145736 | tf_op jit(solution)/shard_map/ppermute | solution.py:319
  34.1 2.5 %collective-permute-start.3 = (bf16[22,128,128]{2,1,0:T(8,128)(2,1)}, bf16[22,128,128]{2,1,0:T(8,128)(2,1)S(1)}, u32[]{:S(2)}, u32[]{:S(2)}) collective-permute-start(bf16[22,128,128]{2,1,0:T(8,128)(2,1)} %get-tuple-element.53), channel_id=1, source_target_pairs={{0,1},{1,2},{2,3},{3,4},{4,5},{5,6},{6,7},{8,9},{9,10},{10,11},{11... | collective-permute-start | bytes 2162696 | tf_op jit(solution)/shard_map/ppermute | solution.py:352
  36.6 9.2 %collective-permute-done.4.b_ref = bf16[4,128,1024]{2,1,0:T(8,128)(2,1)S(1)} collective-permute-done((bf16[4,128,1024]{2,1,0:T(8,128)(2,1)}, bf16[4,128,1024]{2,1,0:T(8,128)(2,1)S(1)}, u32[]{:S(2)}, u32[]{:S(2)}) %collective-permute-start.4) | collective-permute-done | bytes 1048608 | tf_op jit(solution)/shard_map/ppermute | solution.py:319
  45.8 2.4 %collective-permute-start.5 = (bf16[4,128,1024]{2,1,0:T(8,128)(2,1)}, bf16[4,128,1024]{2,1,0:T(8,128)(2,1)}, u32[]{:S(2)}, u32[]{:S(2)}) collective-permute-start(bf16[4,128,1024]{2,1,0:T(8,128)(2,1)} %get-tuple-element.58), channel_id=1, source_target_pairs={{0,8},{8,32},{16,24},{24,48},{32,40},{40,64},{48,56},{56,80},{64,7... | collective-permute-start | bytes 3145736 | tf_op jit(solution)/shard_map/ppermute | solution.py:319
  49.0 4.9 %picked_rows.1 = (bf16[8,128,1024]{2,1,0:T(8,128)(2,1)}, bf16[4,128,1024]{2,1,0:T(8,128)(2,1)}, bf16[4,128,1024]{2,1,0:T(8,128)(2,1)}) custom-call(s32[24]{0:T(128)} %pad_add_fusion.1.index_ref, bf16[16,128,1024]{2,1,0:T(8,128)(2,1)} %get-tuple-element.52.scaled_ref.a_ref.refs_0_), custom_call_target="tpu_custom_call" | custom-call | flops 1 | bytes 1 | tf_op jit(solution)/shard_map/picked_rows/pallas_call | solution.py:183
  58.8 5.1 %pieces.8 = (f32[4,4,128,128]{3,2,1,0:T(8,128)S(1)}, f32[4,4,128,128]{3,2,1,0:T(8,128)S(1)}) custom-call(s32[4]{0:T(128)S(1)} %get-tuple-element.102.index_ref, s32[8]{0:T(128)S(1)} %and_select_fusion.1.lag_ref, bf16[16,128,1024]{2,1,0:T(8,128)(2,1)S(1)} %copy-done.1, bf16[22,128,128]{2,1,0:T(8,128)(2,1)S(1)} %collective-permute-done.3.halo_ref.spare_ref, ...), custom_call_target="tpu_custom_call" | custom-call | flops 1 | bytes 1 | tf_op jit(solution)/shard_map/pieces/pallas_call | solution.py:237
  64.7 6.1 %pieces.9 = (f32[4,4,128,128]{3,2,1,0:T(8,128)S(1)}, f32[4,4,128,128]{3,2,1,0:T(8,128)S(1)}) custom-call(s32[4]{0:T(128)S(1)} %get-tuple-element.101.index_ref, s32[8]{0:T(128)S(1)} %and_select_fusion.lag_ref, bf16[16,128,1024]{2,1,0:T(8,128)(2,1)S(1)} %copy-done.1, bf16[22,128,128]{2,1,0:T(8,128)(2,1)S(1)} %collective-permute-done.3.halo_ref.spare_ref, ...), custom_call_target="tpu_custom_call" | custom-call | flops 1 | bytes 1 | tf_op jit(solution)/shard_map/pieces/pallas_call | solution.py:237
  72.0 16.4 %collective-permute-done.7.one_ref.refs_1_ = f32[4,4,128,128]{3,2,1,0:T(8,128)S(1)} collective-permute-done((f32[4,4,128,128]{3,2,1,0:T(8,128)S(1)}, f32[4,4,128,128]{3,2,1,0:T(8,128)S(1)}, u32[]{:S(2)}, u32[]{:S(2)}) %collective-permute-start.7) | collective-permute-done | bytes 1048608 | tf_op jit(solution)/shard_map/ppermute | solution.py:307
  90.2 5.8 %collective-permute-done.6.one_ref.refs_4_ = f32[4,4,128,128]{3,2,1,0:T(8,128)S(1)} collective-permute-done((f32[4,4,128,128]{3,2,1,0:T(8,128)S(1)}, f32[4,4,128,128]{3,2,1,0:T(8,128)S(1)}, u32[]{:S(2)}, u32[]{:S(2)}) %collective-permute-start.6) | collective-permute-done | bytes 1048608 | tf_op jit(solution)/shard_map/ppermute | solution.py:307
  96.4 6.6 %collective-permute-start.8 = (bf16[4,128,1024]{2,1,0:T(8,128)(2,1)S(1)}, bf16[4,128,1024]{2,1,0:T(8,128)(2,1)S(1)}, u32[]{:S(2)}, u32[]{:S(2)}) collective-permute-start(bf16[4,128,1024]{2,1,0:T(8,128)(2,1)S(1)} %copy-done.7), channel_id=1, source_target_pairs={{0,24},{8,16},{16,40},{24,32},{32,56},{40,48},{48,72},{56,64},{64,... | collective-permute-start | bytes 3145736 | tf_op jit(solution)/shard_map/ppermute | solution.py:319
  103.0 10.0 %collective-permute-done.9.b_ref = bf16[8,128,1024]{2,1,0:T(8,128)(2,1)S(1)} collective-permute-done((bf16[8,128,1024]{2,1,0:T(8,128)(2,1)}, bf16[8,128,1024]{2,1,0:T(8,128)(2,1)S(1)}, u32[]{:S(2)}, u32[]{:S(2)}) %collective-permute-start.9) | collective-permute-done | bytes 2097184 | tf_op jit(solution)/shard_map/ppermute | solution.py:319
  113.0 5.2 %pieces.10 = (f32[4,4,128,128]{3,2,1,0:T(8,128)S(1)}, f32[4,4,128,128]{3,2,1,0:T(8,128)S(1)}) custom-call(s32[4]{0:T(128)S(1)} %get-tuple-element.100.index_ref, s32[8]{0:T(128)S(1)} %and_select_fusion.1.lag_ref, bf16[16,128,1024]{2,1,0:T(8,128)(2,1)S(1)} %copy-done.2, bf16[22,128,128]{2,1,0:T(8,128)(2,1)S(1)} %collective-permute-done.3.halo_ref.spare_ref, ...), custom_call_target="tpu_custom_call" | custom-call | flops 1 | bytes 1 | tf_op jit(solution)/shard_map/pieces/pallas_call | solution.py:237
  119.0 5.2 %pieces.11 = (f32[4,4,128,128]{3,2,1,0:T(8,128)S(1)}, f32[4,4,128,128]{3,2,1,0:T(8,128)S(1)}) custom-call(s32[4]{0:T(128)S(1)} %get-tuple-element.99.index_ref, s32[8]{0:T(128)S(1)} %and_select_fusion.lag_ref, bf16[16,128,1024]{2,1,0:T(8,128)(2,1)S(1)} %copy-done.2, bf16[22,128,128]{2,1,0:T(8,128)(2,1)S(1)} %collective-permute-done.3.halo_ref.spare_ref, ...), custom_call_target="tpu_custom_call" | custom-call | flops 1 | bytes 1 | tf_op jit(solution)/shard_map/pieces/pallas_call | solution.py:237
  124.1 2.4 %collective-permute-start.14 = (f32[4,4,128,128]{3,2,1,0:T(8,128)S(1)}, f32[4,4,128,128]{3,2,1,0:T(8,128)S(1)}, u32[]{:S(2)}, u32[]{:S(2)}) collective-permute-start(f32[4,4,128,128]{3,2,1,0:T(8,128)S(1)} %get-tuple-element.75), channel_id=1, source_target_pairs={{0,3},{1,2},{2,1},{3,0},{4,7},{5,6},{6,5},{7,4},{8,11},{9,10},{10,... | collective-permute-start | bytes 3145736 | tf_op jit(solution)/shard_map/ppermute | solution.py:307
  127.1 2.9 %pieces.12 = (f32[4,2,128,128]{3,2,1,0:T(8,128)S(1)}, f32[4,2,128,128]{3,2,1,0:T(8,128)S(1)}) custom-call(s32[2]{0:T(128)S(1)} %get-tuple-element.98.index_ref, s32[8]{0:T(128)S(1)} %and_select_fusion.1.lag_ref, bf16[16,128,1024]{2,1,0:T(8,128)(2,1)S(1)} %copy-done.2, bf16[22,128,128]{2,1,0:T(8,128)(2,1)S(1)} %collective-permute-done.3.halo_ref.spare_ref, ...), custom_call_target="tpu_custom_call" | custom-call | flops 1 | bytes 1 | tf_op jit(solution)/shard_map/pieces/pallas_call | solution.py:237
  131.6 2.9 %pieces.13 = (f32[4,2,128,128]{3,2,1,0:T(8,128)S(1)}, f32[4,2,128,128]{3,2,1,0:T(8,128)S(1)}) custom-call(s32[2]{0:T(128)S(1)} %get-tuple-element.95.index_ref, s32[8]{0:T(128)S(1)} %and_select_fusion.lag_ref, bf16[16,128,1024]{2,1,0:T(8,128)(2,1)S(1)} %copy-done.2, bf16[22,128,128]{2,1,0:T(8,128)(2,1)S(1)} %collective-permute-done.3.halo_ref.spare_ref, ...), custom_call_target="tpu_custom_call" | custom-call | flops 1 | bytes 1 | tf_op jit(solution)/shard_map/pieces/pallas_call | solution.py:237
  136.3 2.8 %collective-permute-start.21 = (f32[2,4,128,128]{3,2,1,0:T(8,128)S(1)}, f32[2,4,128,128]{3,2,1,0:T(8,128)S(1)}, u32[]{:S(2)}, u32[]{:S(2)}) collective-permute-start(f32[2,4,128,128]{3,2,1,0:T(8,128)S(1)} %forward.10.refs_0_), channel_id=1, source_target_pairs={{0,3},{1,2},{2,1},{3,0},{4,7},{5,6},{6,5},{7,4},{8,11},{9,10},{10,... | collective-permute-start | bytes 1572872 | tf_op jit(solution)/shard_map/ppermute | solution.py:307
  139.1 4.8 %collective-permute-done.14.one_ref.refs_4_ = f32[4,4,128,128]{3,2,1,0:T(8,128)S(1)} collective-permute-done((f32[4,4,128,128]{3,2,1,0:T(8,128)S(1)}, f32[4,4,128,128]{3,2,1,0:T(8,128)S(1)}, u32[]{:S(2)}, u32[]{:S(2)}) %collective-permute-start.14) | collective-permute-done | bytes 1048608 | tf_op jit(solution)/shard_map/ppermute | solution.py:307
  144.7 8.9 %collective-permute-done.13.b_ref = bf16[4,128,1024]{2,1,0:T(8,128)(2,1)S(1)} collective-permute-done((bf16[4,128,1024]{2,1,0:T(8,128)(2,1)S(1)}, bf16[4,128,1024]{2,1,0:T(8,128)(2,1)S(1)}, u32[]{:S(2)}, u32[]{:S(2)}) %collective-permute-start.13) | collective-permute-done | bytes 1048608 | tf_op jit(solution)/shard_map/ppermute | solution.py:319
  153.6 2.9 %pieces.14 = (f32[4,2,128,128]{3,2,1,0:T(8,128)S(1)}, f32[4,2,128,128]{3,2,1,0:T(8,128)S(1)}) custom-call(s32[2]{0:T(128)S(1)} %get-tuple-element.96.index_ref, s32[8]{0:T(128)S(1)} %and_select_fusion.1.lag_ref, bf16[16,128,1024]{2,1,0:T(8,128)(2,1)S(1)} %copy-done.2, bf16[22,128,128]{2,1,0:T(8,128)(2,1)S(1)} %collective-permute-done.3.halo_ref.spare_ref, ...), custom_call_target="tpu_custom_call" | custom-call | flops 1 | bytes 1 | tf_op jit(solution)/shard_map/pieces/pallas_call | solution.py:237
  156.9 2.9 %pieces.15 = (f32[4,2,128,128]{3,2,1,0:T(8,128)S(1)}, f32[4,2,128,128]{3,2,1,0:T(8,128)S(1)}) custom-call(s32[2]{0:T(128)S(1)} %get-tuple-element.97.index_ref, s32[8]{0:T(128)S(1)} %and_select_fusion.lag_ref, bf16[16,128,1024]{2,1,0:T(8,128)(2,1)S(1)} %copy-done.2, bf16[22,128,128]{2,1,0:T(8,128)(2,1)S(1)} %collective-permute-done.3.halo_ref.spare_ref, ...), custom_call_target="tpu_custom_call" | custom-call | flops 1 | bytes 1 | tf_op jit(solution)/shard_map/pieces/pallas_call | solution.py:237
  161.6 2.3 %collective-permute-start.27 = (f32[2,4,128,128]{3,2,1,0:T(8,128)S(1)}, f32[2,4,128,128]{3,2,1,0:T(8,128)S(1)}, u32[]{:S(2)}, u32[]{:S(2)}) collective-permute-start(f32[2,4,128,128]{3,2,1,0:T(8,128)S(1)} %get-tuple-element.87), channel_id=1, source_target_pairs={{0,4},{1,5},{2,6},{3,7},{4,0},{5,1},{6,2},{7,3},{8,12},{9,13},{10,... | collective-permute-start | bytes 1572872 | tf_op jit(solution)/shard_map/ppermute | solution.py:307
  166.7 8.2 %collective-permute-start.26 = (f32[2,4,128,128]{3,2,1,0:T(8,128)S(1)}, f32[2,4,128,128]{3,2,1,0:T(8,128)S(1)}, u32[]{:S(2)}, u32[]{:S(2)}) collective-permute-start(f32[2,4,128,128]{3,2,1,0:T(8,128)S(1)} %get-tuple-element.86), channel_id=1, source_target_pairs={{0,4},{1,5},{2,6},{3,7},{4,0},{5,1},{6,2},{7,3},{8,12},{9,13},{10,... | collective-permute-start | bytes 1572872 | tf_op jit(solution)/shard_map/ppermute | solution.py:307
  175.1 2.2 %collective-permute-done.19.one_ref.refs_4_ = f32[4,2,128,128]{3,2,1,0:T(8,128)S(1)} collective-permute-done((f32[4,2,128,128]{3,2,1,0:T(8,128)S(1)}, f32[4,2,128,128]{3,2,1,0:T(8,128)S(1)}, u32[]{:S(2)}, u32[]{:S(2)}) %collective-permute-start.19) | collective-permute-done | bytes 524320 | tf_op jit(solution)/shard_map/ppermute | solution.py:307
  183.5 7.2 %collective-permute-start.23 = (f32[2,2,128,128]{3,2,1,0:T(8,128)S(1)}, f32[2,2,128,128]{3,2,1,0:T(8,128)S(1)}, u32[]{:S(2)}, u32[]{:S(2)}) collective-permute-start(f32[2,2,128,128]{3,2,1,0:T(8,128)S(1)} %get-tuple-element.85), channel_id=1, source_target_pairs={{0,4},{1,5},{2,6},{3,7},{4,0},{5,1},{6,2},{7,3},{8,12},{9,13},{10,... | collective-permute-start | bytes 786440 | tf_op jit(solution)/shard_map/ppermute | solution.py:307
  191.6 2.8 %collective-permute-start.28 = (f32[2,2,128,128]{3,2,1,0:T(8,128)S(1)}, f32[2,2,128,128]{3,2,1,0:T(8,128)S(1)}, u32[]{:S(2)}, u32[]{:S(2)}) collective-permute-start(f32[2,2,128,128]{3,2,1,0:T(8,128)S(1)} %get-tuple-element.89), channel_id=1, source_target_pairs={{0,4},{1,5},{2,6},{3,7},{4,0},{5,1},{6,2},{7,3},{8,12},{9,13},{10,... | collective-permute-start | bytes 786440 | tf_op jit(solution)/shard_map/ppermute | solution.py:307
  195.0 5.1 %collective-permute-done.28.three_ref = f32[2,2,128,128]{3,2,1,0:T(8,128)S(1)} collective-permute-done((f32[2,2,128,128]{3,2,1,0:T(8,128)S(1)}, f32[2,2,128,128]{3,2,1,0:T(8,128)S(1)}, u32[]{:S(2)}, u32[]{:S(2)}) %collective-permute-start.28) | collective-permute-done | bytes 262176 | tf_op jit(solution)/shard_map/ppermute | solution.py:307
  (94 shorter events, 35.3 us)
Async XLA Ops:
  0.0 48.3 %copy-start = (s32[8]{0:T(128)S(1)}, s32[8]{0:T(128)}, u32[]{:S(2)}) copy-start(s32[8]{0:T(128)} %param.6) | copy-start | bytes 100
  5.9 16.1 %all-to-all-start = ((f32[8,32,128]{2,1,0:T(8,128)}), f32[8,32,128]{2,1,0:T(8,128)S(1)}, u32[]{:S(2)}, u32[]{:S(2)}) async-start(f32[8,32,128]{2,1,0:T(8,128)} %local_sums.1), calls=%async_computation | async-start | bytes 262144 | tf_op jit(solution)/shard_map/all_to_all | solution.py:338
  14.2 4.9 %collective-permute-start = (s32[8]{0:T(128)S(1)}, s32[8]{0:T(128)S(1)}, u32[]{:S(2)}, u32[]{:S(2)}) collective-permute-start(s32[8]{0:T(128)S(1)} %slice_bitcast_fusion.10), channel_id=1, source_target_pairs={{0,104},{8,0},{16,120},{24,16},{32,8},{40,32},{48,24},{56,48},{64,... | collective-permute-start | bytes 104 | tf_op jit(solution)/shard_map/ppermute | solution.py:319
  15.2 3.9 %collective-permute-start.1 = (s32[8]{0:T(128)S(1)}, s32[8]{0:T(128)S(1)}, u32[]{:S(2)}, u32[]{:S(2)}) collective-permute-start(s32[8]{0:T(128)S(1)} %get-tuple-element.49), channel_id=1, source_target_pairs={{0,112},{8,120},{16,0},{24,8},{32,16},{40,24},{48,32},{56,40},{64,... | collective-permute-start | bytes 104 | tf_op jit(solution)/shard_map/ppermute | solution.py:319
  18.1 3.3 %collective-permute-start.2 = (s32[8]{0:T(128)S(1)}, s32[8]{0:T(128)S(1)}, u32[]{:S(2)}, u32[]{:S(2)}) collective-permute-start(s32[8]{0:T(128)S(1)} %get-tuple-element.50), channel_id=1, source_target_pairs={{0,120},{8,112},{16,8},{24,0},{32,24},{40,16},{48,40},{56,32},{64,... | collective-permute-start | bytes 104 | tf_op jit(solution)/shard_map/ppermute | solution.py:319
  31.4 14.5 %collective-permute-start.4 = (bf16[4,128,1024]{2,1,0:T(8,128)(2,1)}, bf16[4,128,1024]{2,1,0:T(8,128)(2,1)S(1)}, u32[]{:S(2)}, u32[]{:S(2)}) collective-permute-start(bf16[4,128,1024]{2,1,0:T(8,128)(2,1)} %get-tuple-element.56), channel_id=1, source_target_pairs={{0,8},{8,32},{16,24},{24,48},{32,40},{40,64},{48,56},{56,80},{64,7... | collective-permute-start | bytes 3145736 | tf_op jit(solution)/shard_map/ppermute | solution.py:319
  34.1 19.8 %collective-permute-start.3 = (bf16[22,128,128]{2,1,0:T(8,128)(2,1)}, bf16[22,128,128]{2,1,0:T(8,128)(2,1)S(1)}, u32[]{:S(2)}, u32[]{:S(2)}) collective-permute-start(bf16[22,128,128]{2,1,0:T(8,128)(2,1)} %get-tuple-element.53), channel_id=1, source_target_pairs={{0,1},{1,2},{2,3},{3,4},{4,5},{5,6},{6,7},{8,9},{9,10},{10,11},{11... | collective-permute-start | bytes 2162696 | tf_op jit(solution)/shard_map/ppermute | solution.py:352
  45.8 18.9 %collective-permute-start.5 = (bf16[4,128,1024]{2,1,0:T(8,128)(2,1)}, bf16[4,128,1024]{2,1,0:T(8,128)(2,1)}, u32[]{:S(2)}, u32[]{:S(2)}) collective-permute-start(bf16[4,128,1024]{2,1,0:T(8,128)(2,1)} %get-tuple-element.58), channel_id=1, source_target_pairs={{0,8},{8,32},{16,24},{24,48},{32,40},{40,64},{48,56},{56,80},{64,7... | collective-permute-start | bytes 3145736 | tf_op jit(solution)/shard_map/ppermute | solution.py:319
  53.9 59.1 %collective-permute-start.9 = (bf16[8,128,1024]{2,1,0:T(8,128)(2,1)}, bf16[8,128,1024]{2,1,0:T(8,128)(2,1)S(1)}, u32[]{:S(2)}, u32[]{:S(2)}) collective-permute-start(bf16[8,128,1024]{2,1,0:T(8,128)(2,1)} %get-tuple-element.67), channel_id=1, source_target_pairs={{0,16},{8,24},{16,32},{24,40},{32,48},{40,56},{48,64},{56,72},{64,... | collective-permute-start | bytes 6291464 | tf_op jit(solution)/shard_map/ppermute | solution.py:319
  64.0 24.4 %collective-permute-start.7 = (f32[4,4,128,128]{3,2,1,0:T(8,128)S(1)}, f32[4,4,128,128]{3,2,1,0:T(8,128)S(1)}, u32[]{:S(2)}, u32[]{:S(2)}) collective-permute-start(f32[4,4,128,128]{3,2,1,0:T(8,128)S(1)} %get-tuple-element.63), channel_id=1, source_target_pairs={{0,1},{1,0},{2,3},{3,2},{4,5},{5,4},{6,7},{7,6},{8,9},{9,8},{10,11... | collective-permute-start | bytes 3145736 | tf_op jit(solution)/shard_map/ppermute | solution.py:307
  70.8 25.2 %collective-permute-start.6 = (f32[4,4,128,128]{3,2,1,0:T(8,128)S(1)}, f32[4,4,128,128]{3,2,1,0:T(8,128)S(1)}, u32[]{:S(2)}, u32[]{:S(2)}) collective-permute-start(f32[4,4,128,128]{3,2,1,0:T(8,128)S(1)} %get-tuple-element.62), channel_id=1, source_target_pairs={{0,3},{1,2},{2,1},{3,0},{4,7},{5,6},{6,5},{7,4},{8,11},{9,10},{10,... | collective-permute-start | bytes 3145736 | tf_op jit(solution)/shard_map/ppermute | solution.py:307
  88.4 24.7 %copy-start.2 = (bf16[16,128,1024]{2,1,0:T(8,128)(2,1)S(1)}, bf16[16,128,1024]{2,1,0:T(8,128)(2,1)}, u32[]{:S(2)}) copy-start(bf16[16,128,1024]{2,1,0:T(8,128)(2,1)} %get-tuple-element.52.scaled_ref.a_ref.refs_0_) | copy-start | bytes 12582916
  88.6 29.7 %collective-permute-start.10 = (f32[2,4,128,128]{3,2,1,0:T(8,128)S(1)}, f32[2,4,128,128]{3,2,1,0:T(8,128)S(1)}, u32[]{:S(2)}, u32[]{:S(2)}) collective-permute-start(f32[2,4,128,128]{3,2,1,0:T(8,128)S(1)} %forward.8.refs_0_), channel_id=1, source_target_pairs={{0,3},{1,2},{2,1},{3,0},{4,7},{5,6},{6,5},{7,4},{8,11},{9,10},{10,... | collective-permute-start | bytes 1572872 | tf_op jit(solution)/shard_map/ppermute | solution.py:307
  96.3 22.1 %collective-permute-start.11 = (f32[2,4,128,128]{3,2,1,0:T(8,128)S(1)}, f32[2,4,128,128]{3,2,1,0:T(8,128)S(1)}, u32[]{:S(2)}, u32[]{:S(2)}) collective-permute-start(f32[2,4,128,128]{3,2,1,0:T(8,128)S(1)} %forward.9.refs_0_), channel_id=1, source_target_pairs={{0,1},{1,0},{2,3},{3,2},{4,5},{5,4},{6,7},{7,6},{8,9},{9,8},{10,11... | collective-permute-start | bytes 1572872 | tf_op jit(solution)/shard_map/ppermute | solution.py:307
  96.4 30.7 %collective-permute-start.8 = (bf16[4,128,1024]{2,1,0:T(8,128)(2,1)S(1)}, bf16[4,128,1024]{2,1,0:T(8,128)(2,1)S(1)}, u32[]{:S(2)}, u32[]{:S(2)}) collective-permute-start(bf16[4,128,1024]{2,1,0:T(8,128)(2,1)S(1)} %copy-done.7), channel_id=1, source_target_pairs={{0,24},{8,16},{16,40},{24,32},{32,56},{40,48},{48,72},{56,64},{64,... | collective-permute-start | bytes 3145736 | tf_op jit(solution)/shard_map/ppermute | solution.py:319
  118.2 17.9 %collective-permute-start.15 = (f32[4,4,128,128]{3,2,1,0:T(8,128)S(1)}, f32[4,4,128,128]{3,2,1,0:T(8,128)S(1)}, u32[]{:S(2)}, u32[]{:S(2)}) collective-permute-start(f32[4,4,128,128]{3,2,1,0:T(8,128)S(1)} %get-tuple-element.76), channel_id=1, source_target_pairs={{0,1},{1,0},{2,3},{3,2},{4,5},{5,4},{6,7},{7,6},{8,9},{9,8},{10,11... | collective-permute-start | bytes 3145736 | tf_op jit(solution)/shard_map/ppermute | solution.py:307
  124.1 19.8 %collective-permute-start.14 = (f32[4,4,128,128]{3,2,1,0:T(8,128)S(1)}, f32[4,4,128,128]{3,2,1,0:T(8,128)S(1)}, u32[]{:S(2)}, u32[]{:S(2)}) collective-permute-start(f32[4,4,128,128]{3,2,1,0:T(8,128)S(1)} %get-tuple-element.75), channel_id=1, source_target_pairs={{0,3},{1,2},{2,1},{3,0},{4,7},{5,6},{6,5},{7,4},{8,11},{9,10},{10,... | collective-permute-start | bytes 3145736 | tf_op jit(solution)/shard_map/ppermute | solution.py:307
  126.5 27.1 %collective-permute-start.13 = (bf16[4,128,1024]{2,1,0:T(8,128)(2,1)S(1)}, bf16[4,128,1024]{2,1,0:T(8,128)(2,1)S(1)}, u32[]{:S(2)}, u32[]{:S(2)}) collective-permute-start(bf16[4,128,1024]{2,1,0:T(8,128)(2,1)S(1)} %copy-done.6), channel_id=1, source_target_pairs={{0,24},{8,16},{16,40},{24,32},{32,56},{40,48},{48,72},{56,64},{64,... | collective-permute-start | bytes 3145736 | tf_op jit(solution)/shard_map/ppermute | solution.py:319
  130.0 29.8 %collective-permute-start.12 = (f32[4,2,128,128]{3,2,1,0:T(8,128)S(1)}, f32[4,2,128,128]{3,2,1,0:T(8,128)S(1)}, u32[]{:S(2)}, u32[]{:S(2)}) collective-permute-start(f32[4,2,128,128]{3,2,1,0:T(8,128)S(1)} %get-tuple-element.73), channel_id=1, source_target_pairs={{0,1},{1,0},{2,3},{3,2},{4,5},{5,4},{6,7},{7,6},{8,9},{9,8},{10,11... | collective-permute-start | bytes 1572872 | tf_op jit(solution)/shard_map/ppermute | solution.py:307
  134.5 27.1 %collective-permute-start.17 = (f32[4,2,128,128]{3,2,1,0:T(8,128)S(1)}, f32[4,2,128,128]{3,2,1,0:T(8,128)S(1)}, u32[]{:S(2)}, u32[]{:S(2)}) collective-permute-start(f32[4,2,128,128]{3,2,1,0:T(8,128)S(1)} %get-tuple-element.80), channel_id=1, source_target_pairs={{0,3},{1,2},{2,1},{3,0},{4,7},{5,6},{6,5},{7,4},{8,11},{9,10},{10,... | collective-permute-start | bytes 1572872 | tf_op jit(solution)/shard_map/ppermute | solution.py:307
  136.3 29.8 %collective-permute-start.21 = (f32[2,4,128,128]{3,2,1,0:T(8,128)S(1)}, f32[2,4,128,128]{3,2,1,0:T(8,128)S(1)}, u32[]{:S(2)}, u32[]{:S(2)}) collective-permute-start(f32[2,4,128,128]{3,2,1,0:T(8,128)S(1)} %forward.10.refs_0_), channel_id=1, source_target_pairs={{0,3},{1,2},{2,1},{3,0},{4,7},{5,6},{6,5},{7,4},{8,11},{9,10},{10,... | collective-permute-start | bytes 1572872 | tf_op jit(solution)/shard_map/ppermute | solution.py:307
  144.1 22.0 %collective-permute-start.22 = (f32[2,4,128,128]{3,2,1,0:T(8,128)S(1)}, f32[2,4,128,128]{3,2,1,0:T(8,128)S(1)}, u32[]{:S(2)}, u32[]{:S(2)}) collective-permute-start(f32[2,4,128,128]{3,2,1,0:T(8,128)S(1)} %forward.11.refs_0_), channel_id=1, source_target_pairs={{0,1},{1,0},{2,3},{3,2},{4,5},{5,4},{6,7},{7,6},{8,9},{9,8},{10,11... | collective-permute-start | bytes 1572872 | tf_op jit(solution)/shard_map/ppermute | solution.py:307
  156.5 18.4 %collective-permute-start.20 = (f32[4,2,128,128]{3,2,1,0:T(8,128)S(1)}, f32[4,2,128,128]{3,2,1,0:T(8,128)S(1)}, u32[]{:S(2)}, u32[]{:S(2)}) collective-permute-start(f32[4,2,128,128]{3,2,1,0:T(8,128)S(1)} %get-tuple-element.82), channel_id=1, source_target_pairs={{0,1},{1,0},{2,3},{3,2},{4,5},{5,4},{6,7},{7,6},{8,9},{9,8},{10,11... | collective-permute-start | bytes 1572872 | tf_op jit(solution)/shard_map/ppermute | solution.py:307
  159.8 17.5 %collective-permute-start.19 = (f32[4,2,128,128]{3,2,1,0:T(8,128)S(1)}, f32[4,2,128,128]{3,2,1,0:T(8,128)S(1)}, u32[]{:S(2)}, u32[]{:S(2)}) collective-permute-start(f32[4,2,128,128]{3,2,1,0:T(8,128)S(1)} %get-tuple-element.81), channel_id=1, source_target_pairs={{0,3},{1,2},{2,1},{3,0},{4,7},{5,6},{6,5},{7,4},{8,11},{9,10},{10,... | collective-permute-start | bytes 1572872 | tf_op jit(solution)/shard_map/ppermute | solution.py:307
  161.6 29.1 %collective-permute-start.27 = (f32[2,4,128,128]{3,2,1,0:T(8,128)S(1)}, f32[2,4,128,128]{3,2,1,0:T(8,128)S(1)}, u32[]{:S(2)}, u32[]{:S(2)}) collective-permute-start(f32[2,4,128,128]{3,2,1,0:T(8,128)S(1)} %get-tuple-element.87), channel_id=1, source_target_pairs={{0,4},{1,5},{2,6},{3,7},{4,0},{5,1},{6,2},{7,3},{8,12},{9,13},{10,... | collective-permute-start | bytes 1572872 | tf_op jit(solution)/shard_map/ppermute | solution.py:307
  166.7 24.3 %collective-permute-start.26 = (f32[2,4,128,128]{3,2,1,0:T(8,128)S(1)}, f32[2,4,128,128]{3,2,1,0:T(8,128)S(1)}, u32[]{:S(2)}, u32[]{:S(2)}) collective-permute-start(f32[2,4,128,128]{3,2,1,0:T(8,128)S(1)} %get-tuple-element.86), channel_id=1, source_target_pairs={{0,4},{1,5},{2,6},{3,7},{4,0},{5,1},{6,2},{7,3},{8,12},{9,13},{10,... | collective-permute-start | bytes 1572872 | tf_op jit(solution)/shard_map/ppermute | solution.py:307
  174.9 5.5 %collective-permute-start.18 = (f32[2,2,128,128]{3,2,1,0:T(8,128)S(1)}, f32[2,2,128,128]{3,2,1,0:T(8,128)S(1)}, u32[]{:S(2)}, u32[]{:S(2)}) collective-permute-start(f32[2,2,128,128]{3,2,1,0:T(8,128)S(1)} %forward.13.refs_6_), channel_id=1, source_target_pairs={{0,1},{1,0},{2,3},{3,2},{4,5},{5,4},{6,7},{7,6},{8,9},{9,8},{10,11... | collective-permute-start | bytes 786440 | tf_op jit(solution)/shard_map/ppermute | solution.py:307
  174.9 8.3 %collective-permute-start.16 = (f32[2,2,128,128]{3,2,1,0:T(8,128)S(1)}, f32[2,2,128,128]{3,2,1,0:T(8,128)S(1)}, u32[]{:S(2)}, u32[]{:S(2)}) collective-permute-start(f32[2,2,128,128]{3,2,1,0:T(8,128)S(1)} %forward.12.refs_0_), channel_id=1, source_target_pairs={{0,3},{1,2},{2,1},{3,0},{4,7},{5,6},{6,5},{7,4},{8,11},{9,10},{10,... | collective-permute-start | bytes 786440 | tf_op jit(solution)/shard_map/ppermute | solution.py:307
  177.5 13.8 %collective-permute-start.25 = (f32[2,2,128,128]{3,2,1,0:T(8,128)S(1)}, f32[2,2,128,128]{3,2,1,0:T(8,128)S(1)}, u32[]{:S(2)}, u32[]{:S(2)}) collective-permute-start(f32[2,2,128,128]{3,2,1,0:T(8,128)S(1)} %forward.15.refs_6_), channel_id=1, source_target_pairs={{0,1},{1,0},{2,3},{3,2},{4,5},{5,4},{6,7},{7,6},{8,9},{9,8},{10,11... | collective-permute-start | bytes 786440 | tf_op jit(solution)/shard_map/ppermute | solution.py:307
  180.4 10.9 %collective-permute-start.24 = (f32[2,2,128,128]{3,2,1,0:T(8,128)S(1)}, f32[2,2,128,128]{3,2,1,0:T(8,128)S(1)}, u32[]{:S(2)}, u32[]{:S(2)}) collective-permute-start(f32[2,2,128,128]{3,2,1,0:T(8,128)S(1)} %forward.14.refs_0_), channel_id=1, source_target_pairs={{0,3},{1,2},{2,1},{3,0},{4,7},{5,6},{6,5},{7,4},{8,11},{9,10},{10,... | collective-permute-start | bytes 786440 | tf_op jit(solution)/shard_map/ppermute | solution.py:307
  183.5 11.3 %collective-permute-start.23 = (f32[2,2,128,128]{3,2,1,0:T(8,128)S(1)}, f32[2,2,128,128]{3,2,1,0:T(8,128)S(1)}, u32[]{:S(2)}, u32[]{:S(2)}) collective-permute-start(f32[2,2,128,128]{3,2,1,0:T(8,128)S(1)} %get-tuple-element.85), channel_id=1, source_target_pairs={{0,4},{1,5},{2,6},{3,7},{4,0},{5,1},{6,2},{7,3},{8,12},{9,13},{10,... | collective-permute-start | bytes 786440 | tf_op jit(solution)/shard_map/ppermute | solution.py:307
  191.6 8.5 %collective-permute-start.28 = (f32[2,2,128,128]{3,2,1,0:T(8,128)S(1)}, f32[2,2,128,128]{3,2,1,0:T(8,128)S(1)}, u32[]{:S(2)}, u32[]{:S(2)}) collective-permute-start(f32[2,2,128,128]{3,2,1,0:T(8,128)S(1)} %get-tuple-element.89), channel_id=1, source_target_pairs={{0,4},{1,5},{2,6},{3,7},{4,0},{5,1},{6,2},{7,3},{8,12},{9,13},{10,... | collective-permute-start | bytes 786440 | tf_op jit(solution)/shard_map/ppermute | solution.py:307
  (6 other events, 27.5 us)
